TPU v7x, 32 devices: a whole 2x2x4 slice. The times are simulated.
32 devices in a mesh: dp: 8 (over y, x, core), mp: 4 (over z).
Axes of the slice: x: 2, y: 2, z: 4, core: 2. Of those that a mesh axis runs over, the one named last changes fastest.
Arguments:
- block_input: bfloat16 [8192, 2048], P(('dp', 'mp')), may hold values from -6 to 6
- cotangent: bfloat16 [8192, 2048], P(('dp', 'mp')), may hold values from -6 to 6
- lengths: int32 [8], replicated, may hold values from 256 to 1024, as said below
- vectors: float32 [4, 2048], replicated, may hold values from 0.5 to 1.5, as said below
- vectors_first: float32 [4, 2048], replicated, may hold values from -60 to 60
- vectors_second: float32 [4, 2048], replicated, may hold values from 1 to 1000
- mixer_in: float32 [3, 2048, 2048], P(None, 'dp', 'mp'), may hold values from -0.125 to 0.125
- mixer_in_first: float32 [3, 2048, 2048], P(None, 'dp', 'mp'), may hold values from -60 to 60
- mixer_in_second: float32 [3, 2048, 2048], P(None, 'dp', 'mp'), may hold values from 1 to 1000
- mixer_out: float32 [2048, 2048], P('mp', 'dp'), may hold values from -0.125 to 0.125
- mixer_out_first: float32 [2048, 2048], P('mp', 'dp'), may hold values from -60 to 60
- mixer_out_second: float32 [2048, 2048], P('mp', 'dp'), may hold values from 1 to 1000
- ffn_in: float32 [2, 2048, 5632], P(None, 'dp', 'mp'), may hold values from -0.125 to 0.125
- ffn_in_first: float32 [2, 2048, 5632], P(None, 'dp', 'mp'), may hold values from -60 to 60
- ffn_in_second: float32 [2, 2048, 5632], P(None, 'dp', 'mp'), may hold values from 1 to 1000
- ffn_out: float32 [5632, 2048], P('mp', 'dp'), may hold values from -0.078125 to 0.078125
- ffn_out_first: float32 [5632, 2048], P('mp', 'dp'), may hold values from -60 to 60
- ffn_out_second: float32 [5632, 2048], P('mp', 'dp'), may hold values from 1 to 1000
Outputs:
- block_output: bfloat16 [8192, 2048], P(('dp', 'mp'))
- input_grad: float32 [8192, 2048], P(('dp', 'mp'))
- stats: float32 [3], replicated
- vectors_grad: float32 [4, 2048], replicated
- vectors_first_new: float32 [4, 2048], replicated
- vectors_second_new: float32 [4, 2048], replicated
- mixer_in_grad: float32 [3, 2048, 2048], P(None, 'dp', 'mp')
- mixer_in_new: float32 [3, 2048, 2048], P(None, 'dp', 'mp')
- mixer_in_first_new: float32 [3, 2048, 2048], P(None, 'dp', 'mp')
- mixer_in_second_new: float32 [3, 2048, 2048], P(None, 'dp', 'mp')
- mixer_in_bf16: bfloat16 [3, 2048, 2048], P(None, None, 'mp')
- mixer_out_grad: float32 [2048, 2048], P('mp', 'dp')
- mixer_out_new: float32 [2048, 2048], P('mp', 'dp')
- mixer_out_first_new: float32 [2048, 2048], P('mp', 'dp')
- mixer_out_second_new: float32 [2048, 2048], P('mp', 'dp')
- mixer_out_bf16: bfloat16 [2048, 2048], P('mp')
- ffn_in_grad: float32 [2, 2048, 5632], P(None, 'dp', 'mp')
- ffn_in_new: float32 [2, 2048, 5632], P(None, 'dp', 'mp')
- ffn_in_first_new: float32 [2, 2048, 5632], P(None, 'dp', 'mp')
- ffn_in_second_new: float32 [2, 2048, 5632], P(None, 'dp', 'mp')
- ffn_in_bf16: bfloat16 [2, 2048, 5632], P(None, None, 'mp')
- ffn_out_grad: float32 [5632, 2048], P('mp', 'dp')
- ffn_out_new: float32 [5632, 2048], P('mp', 'dp')
- ffn_out_first_new: float32 [5632, 2048], P('mp', 'dp')
- ffn_out_second_new: float32 [5632, 2048], P('mp', 'dp')
- ffn_out_bf16: bfloat16 [5632, 2048], P('mp')
Inputs may be any that keep to these rules, and one draw needn't show every extreme that they name: `lengths`: each sequence's valid slots come first; sequence 0 is full (1024 valid slots). `vectors`: rows 0, 1 and 3 are gains; row 2 lies in 0.85 to 0.97.
All inputs are finite; a program needn't handle non-finite values.
Results may differ from a plain program's by a relative error of at most 0.02.
Values may be sent and summed in bfloat16 or wider, within the bound.
No kernel may reach another device: no remote copies, remote signals or barrier semaphores. Data moves between devices by JAX's collectives and lax.ppermute only.
A program may use at most 320 MiB of HBM per device.

v0:
```python
import jax
import jax.numpy as jnp
from jax import lax
from jax.sharding import PartitionSpec as P

D = 2048
HEAD = 128
SPAN = 64
STEP = 10


EPS = 1e-06
BETA_ONE = 0.9
BETA_TWO = 0.95
DECAY = 0.1
ADAM_EPS = 1e-08
LEARN_RATE = 0.005


def rms_norm(value, gain):
    return value * lax.rsqrt(jnp.mean(value * value, axis=-1, keepdims=True) + EPS) * gain


def recurrence(query, log_forget, key, value):
    length, heads, width = query.shape
    blocks = length // SPAN
    shape = (blocks, SPAN, heads, width)
    parts = (
        query.reshape(shape),
        log_forget.reshape(shape),
        key.reshape(shape),
        value.reshape(shape),
    )
    lower_tri = jnp.arange(SPAN)[:, None] >= jnp.arange(SPAN)[None, :]
    highest_precision = lax.Precision.HIGHEST

    def block(running_state, piece):
        query_block, decay_block, key_block, value_block_rows = piece
        running = jnp.cumsum(decay_block, axis=0)
        final_state = running[-1]
        decayed_query_rows = query_block * jnp.exp(running)
        key_decayed = key_block * jnp.exp(-running)
        inter_block_output = jnp.einsum(
            "xil,ilf->xif", decayed_query_rows, running_state, precision=highest_precision
        )
        scores = jnp.einsum(
            "chk,shk->hcs", decayed_query_rows, key_decayed, precision=highest_precision
        )
        scores = jnp.where(lower_tri[None], scores, 0.0)
        intra = jnp.einsum("hcs,shv->chv", scores, value_block_rows, precision=highest_precision)
        carried_state = key_block * jnp.exp(final_state[None] - running)
        running_state = jnp.exp(final_state)[:, :, None] * running_state + jnp.einsum(
            "gux,gup->uxp", carried_state, value_block_rows, precision=highest_precision
        )
        return (running_state, inter_block_output + intra)

    initial = jnp.zeros((heads, width, width), query.dtype)
    _, outputs = lax.scan(jax.checkpoint(block), initial, parts)
    return outputs.reshape(length, heads, width)


def mixer_core(query_raw, forget_raw, value_raw, lower, group_gain, valid):
    length, channels = query_raw.shape
    heads = channels // HEAD
    sigma = jax.nn.sigmoid(forget_raw)
    forget = lower + (1.0 - lower) * sigma
    keep = valid[:, None]
    log_forget = keep * jnp.log(forget)
    key = keep * (1.0 - forget)
    query = jax.nn.silu(query_raw)
    split = (length, heads, HEAD)
    mixed = recurrence(
        query.reshape(split),
        log_forget.reshape(split),
        key.reshape(split),
        value_raw.reshape(split),
    )
    normed = mixed * lax.rsqrt(jnp.mean(mixed * mixed, axis=-1, keepdims=True) + EPS)
    return normed.reshape(length, channels) * group_gain


def swiglu(gate, upward):
    return jax.nn.silu(gate) * upward


def moments(first, second, grad):
    first = BETA_ONE * first + (1.0 - BETA_ONE) * grad
    second = BETA_TWO * second + (1.0 - BETA_TWO) * grad * grad
    return (first, second)


def adamw(param, first, second, grad, decay):
    first, second = moments(first, second, grad)
    fix_one = 1.0 - BETA_ONE**STEP
    fix_two = 1.0 - BETA_TWO**STEP
    update = first / fix_one / (jnp.sqrt(second / fix_two) + ADAM_EPS) + decay * param
    return (param - LEARN_RATE * update, first, second)


def body(
    block_input,
    cotangent,
    lengths,
    vectors,
    vectors_first,
    vectors_second,
    mixer_in,
    mixer_in_first,
    mixer_in_second,
    mixer_out,
    mixer_out_first,
    mixer_out_second,
    ffn_in,
    ffn_in_first,
    ffn_in_second,
    ffn_out,
    ffn_out_first,
    ffn_out_second,
):
    own_rows = block_input.shape[0]
    group = lax.axis_index("dp")
    member = lax.axis_index("mp")
    seq_rows = own_rows * lax.axis_size("mp")
    seq_len = lax.dynamic_index_in_dim(lengths, group, 0, keepdims=False)
    valid_all = (jnp.arange(seq_rows, dtype=jnp.int32) < seq_len).astype(jnp.float32)
    own_pos = member * own_rows + jnp.arange(own_rows, dtype=jnp.int32)
    valid_own = (own_pos < seq_len).astype(jnp.float32)
    channels = mixer_in.shape[2]
    channel_start = member * channels
    group_gain = lax.dynamic_slice_in_dim(vectors[1], channel_start, channels)
    lower = lax.dynamic_slice_in_dim(vectors[2], channel_start, channels)
    gathered_in, gathered_out, gathered_gate_up, gathered_down = (
        lax.all_gather(mixer_in.astype(jnp.bfloat16), "dp", axis=1, tiled=True),
        lax.all_gather(mixer_out.astype(jnp.bfloat16), "dp", axis=1, tiled=True),
        lax.all_gather(ffn_in.astype(jnp.bfloat16), "dp", axis=1, tiled=True),
        lax.all_gather(ffn_out.astype(jnp.bfloat16), "dp", axis=1, tiled=True),
    )
    inputs = block_input.astype(jnp.float32)
    normed_one, norm_one_back = jax.vjp(rms_norm, inputs, vectors[0])
    normed_seq = lax.all_gather(normed_one.astype(jnp.bfloat16), "mp", axis=0, tiled=True)
    projected = jnp.einsum(
        "td,jdc->jtc", normed_seq, gathered_in, preferred_element_type=jnp.float32
    )

    def local_core(query_raw, forget_raw, value_raw, bound, gain):
        return mixer_core(query_raw, forget_raw, value_raw, bound, gain, valid_all)

    core, core_back = jax.vjp(
        local_core, projected[0], projected[1], projected[2], lower, group_gain
    )
    core_low = core.astype(jnp.bfloat16)
    mix_part = jnp.dot(core_low, gathered_out, preferred_element_type=jnp.float32)
    mix = lax.psum_scatter(mix_part, "mp", scatter_dimension=0, tiled=True)
    resid = inputs + mix
    normed_two, norm_two_back = jax.vjp(rms_norm, resid, vectors[3])
    normed_two_seq = lax.all_gather(normed_two.astype(jnp.bfloat16), "mp", axis=0, tiled=True)
    gate_up = jnp.einsum(
        "td,jdf->jtf", normed_two_seq, gathered_gate_up, preferred_element_type=jnp.float32
    )
    activated, act_back = jax.vjp(swiglu, gate_up[0], gate_up[1])
    hidden = activated.astype(jnp.bfloat16)
    ffn_part = jnp.dot(hidden, gathered_down, preferred_element_type=jnp.float32)
    ffn = lax.psum_scatter(
        ffn_part.astype(jnp.bfloat16), "mp", scatter_dimension=0, tiled=True
    ).astype(jnp.float32)
    total = resid + ffn
    back_in, back_out, back_gate_up, back_down = (
        lax.all_gather(mixer_in.astype(jnp.bfloat16), "dp", axis=1, tiled=True),
        lax.all_gather(mixer_out.astype(jnp.bfloat16), "dp", axis=1, tiled=True),
        lax.all_gather(ffn_in.astype(jnp.bfloat16), "dp", axis=1, tiled=True),
        lax.all_gather(ffn_out.astype(jnp.bfloat16), "dp", axis=1, tiled=True),
    )
    grad_total = cotangent.astype(jnp.float32) * valid_own[:, None]
    grad_seq = lax.all_gather(grad_total.astype(jnp.bfloat16), "mp", axis=0, tiled=True)
    grad_down = jnp.einsum("tf,td->fd", hidden, grad_seq, preferred_element_type=jnp.float32)
    grad_hidden = jnp.einsum("td,fd->tf", grad_seq, back_down, preferred_element_type=jnp.float32)
    grad_gate, grad_upward = act_back(grad_hidden)
    grad_gu_low = jnp.stack([grad_gate, grad_upward]).astype(jnp.bfloat16)
    grad_gate_up = jnp.einsum(
        "td,jtf->jdf", normed_two_seq, grad_gu_low, preferred_element_type=jnp.float32
    )
    grad_two_part = jnp.einsum(
        "jtf,jdf->td", grad_gu_low, back_gate_up, preferred_element_type=jnp.float32
    )
    grad_two = lax.psum_scatter(
        grad_two_part.astype(jnp.bfloat16), "mp", scatter_dimension=0, tiled=True
    ).astype(jnp.float32)
    grad_resid_norm, grad_gain_two = norm_two_back(grad_two)
    grad_resid = grad_total + grad_resid_norm
    grad_mix_seq = lax.all_gather(grad_resid.astype(jnp.bfloat16), "mp", axis=0, tiled=True)
    grad_weight_out = jnp.einsum(
        "tc,td->cd", core_low, grad_mix_seq, preferred_element_type=jnp.float32
    )
    grad_core = jnp.einsum("td,cd->tc", grad_mix_seq, back_out, preferred_element_type=jnp.float32)
    grad_query, grad_forget, grad_value, grad_lower, grad_group = core_back(grad_core)
    grad_proj_low = jnp.stack([grad_query, grad_forget, grad_value]).astype(jnp.bfloat16)
    grad_weight_in = jnp.einsum(
        "td,jtc->jdc", normed_seq, grad_proj_low, preferred_element_type=jnp.float32
    )
    grad_one_part = jnp.einsum(
        "jtc,jdc->td", grad_proj_low, back_in, preferred_element_type=jnp.float32
    )
    grad_one = lax.psum_scatter(
        grad_one_part.astype(jnp.bfloat16), "mp", scatter_dimension=0, tiled=True
    ).astype(jnp.float32)
    grad_input_norm, grad_gain_one = norm_one_back(grad_one)
    input_grad = grad_resid + grad_input_norm
    shard_in, shard_out, shard_gate_up, shard_down = (
        lax.psum_scatter(
            grad_weight_in.astype(jnp.bfloat16), "dp", scatter_dimension=1, tiled=True
        ).astype(jnp.float32),
        lax.psum_scatter(
            grad_weight_out.astype(jnp.bfloat16), "dp", scatter_dimension=1, tiled=True
        ).astype(jnp.float32),
        lax.psum_scatter(
            grad_gate_up.astype(jnp.bfloat16), "dp", scatter_dimension=1, tiled=True
        ).astype(jnp.float32),
        lax.psum_scatter(
            grad_down.astype(jnp.bfloat16), "dp", scatter_dimension=1, tiled=True
        ).astype(jnp.float32),
    )
    blank = jnp.zeros((vectors.shape[1],), jnp.float32)
    vector_part = jnp.stack(
        [
            grad_gain_one,
            lax.dynamic_update_slice_in_dim(blank, grad_group, channel_start, 0),
            lax.dynamic_update_slice_in_dim(blank, grad_lower, channel_start, 0),
            grad_gain_two,
        ]
    )
    keep_rows = valid_own[:, None]
    squares = jnp.stack(
        [
            jnp.sum(keep_rows * total * total),
            jnp.sum(keep_rows * mix * mix),
            jnp.sum(keep_rows * ffn * ffn),
        ]
    )
    vectors_grad, square_sums = lax.psum((vector_part, squares), ("dp", "mp"))
    denom = jnp.sum(lengths).astype(jnp.float32) * D
    stats = jnp.sqrt(square_sums / denom)
    vec_first, vec_second = moments(vectors_first, vectors_second, vectors_grad)
    in_new, in_first, in_second = adamw(mixer_in, mixer_in_first, mixer_in_second, shard_in, DECAY)
    out_new, out_first, out_second = adamw(
        mixer_out, mixer_out_first, mixer_out_second, shard_out, DECAY
    )
    gu_new, gu_first, gu_second = adamw(ffn_in, ffn_in_first, ffn_in_second, shard_gate_up, DECAY)
    down_new, down_first, down_second = adamw(
        ffn_out, ffn_out_first, ffn_out_second, shard_down, DECAY
    )
    in_low, out_low, gu_low, down_low = (
        lax.all_gather(in_new.astype(jnp.bfloat16), "dp", axis=1, tiled=True),
        lax.all_gather(out_new.astype(jnp.bfloat16), "dp", axis=1, tiled=True),
        lax.all_gather(gu_new.astype(jnp.bfloat16), "dp", axis=1, tiled=True),
        lax.all_gather(down_new.astype(jnp.bfloat16), "dp", axis=1, tiled=True),
    )
    return (
        total.astype(jnp.bfloat16),
        input_grad,
        stats,
        vectors_grad,
        vec_first,
        vec_second,
        shard_in,
        in_new,
        in_first,
        in_second,
        in_low,
        shard_out,
        out_new,
        out_first,
        out_second,
        out_low,
        shard_gate_up,
        gu_new,
        gu_first,
        gu_second,
        gu_low,
        shard_down,
        down_new,
        down_first,
        down_second,
        down_low,
    )


def solution(mesh):
    in_specs = (
        P(("dp", "mp"), None),
        P(("dp", "mp"), None),
        P(),
        P(),
        P(),
        P(),
        P(None, "dp", "mp"),
        P(None, "dp", "mp"),
        P(None, "dp", "mp"),
        P("mp", "dp"),
        P("mp", "dp"),
        P("mp", "dp"),
        P(None, "dp", "mp"),
        P(None, "dp", "mp"),
        P(None, "dp", "mp"),
        P("mp", "dp"),
        P("mp", "dp"),
        P("mp", "dp"),
    )
    out_specs = (
        P(("dp", "mp"), None),
        P(("dp", "mp"), None),
        P(),
        P(),
        P(),
        P(),
        P(None, "dp", "mp"),
        P(None, "dp", "mp"),
        P(None, "dp", "mp"),
        P(None, "dp", "mp"),
        P(None, None, "mp"),
        P("mp", "dp"),
        P("mp", "dp"),
        P("mp", "dp"),
        P("mp", "dp"),
        P("mp", None),
        P(None, "dp", "mp"),
        P(None, "dp", "mp"),
        P(None, "dp", "mp"),
        P(None, "dp", "mp"),
        P(None, None, "mp"),
        P("mp", "dp"),
        P("mp", "dp"),
        P("mp", "dp"),
        P("mp", "dp"),
        P("mp", None),
    )
    return jax.shard_map(body, mesh=mesh, in_specs=in_specs, out_specs=out_specs, check_vma=False)
```

profile of v0, /device:TPU:0, one launch (start us, length us, event | category | flops | bytes accessed | tf_op | source)
XLA Modules:
  0.0 1681.0 jit_solution(14649246761703328226)
XLA Ops:
  9.9 2.5 fusion.68
  15.7 80.3 %all-gather.13.cloned.1.call-done = bf16[1024,2048]{1,0:T(8,128)(2,1)} async-done(((bf16[256,2048]{1,0:T(8,128)(2,1)}), bf16[1024,2048]{1,0:T(8,128)(2,1)}) %all-gather.13.cloned.1.call-update) | async-done | bytes 4194320 | tf_op jit(solution)/shard_map/all_gather | solution.py:140
  96.0 46.6 %all-gather.15.cloned.1.call-done = bf16[3,2048,512]{2,1,0:T(8,128)(2,1)} async-done(((bf16[3,256,512]{2,1,0:T(8,128)(2,1)}), bf16[3,2048,512]{2,1,0:T(8,128)(2,1)}) %all-gather.15.cloned.1.call-update) | async-done | bytes 6291472 | tf_op jit(solution)/shard_map/all_gather | solution.py:133
  142.6 10.2 fusion.61
  152.8 3.1 fusion.113
  159.4 2.0 subtract_multiply_fusion.3
  161.3 2.8 copy.155
  171.8 102.9 %while.39 = (s32[]{:T(128)}, f32[4,128,128]{2,1,0:T(8,128)S(1)}, f32[16,64,4,128]{3,1,2,0:T(8,128)S(1)}, f32[16,4,128,128]{3,2,1,0:T(8,128)}, f32[16,64,4,128]{3...) while((s32[]{:T(128)}, f32[4,128,128]{2,1,0:T(8,128)S(1)}, ...), condition=%wide.region_3.4_spmd.clone, body=%wide.region_1.3_spmd.clone.sunk | while | flops 153600000 | bytes 4210841 | solution.py:58
  274.7 2.7 copy.159
  281.6 7.7 fusion.118
  289.4 3.1 convert_element_type.132
  292.6 141.6 %reduce-scatter.9.cloned.1.call-done = f32[256,2048]{1,0:T(8,128)} async-done(((f32[1024,2048]{1,0:T(8,128)}), f32[256,2048]{1,0:T(8,128)}) %reduce-scatter.9.cloned.1.call-update) | async-done | bytes 2097168 | tf_op jit(solution)/shard_map/reduce_scatter | solution.py:153
  440.7 2.3 convert_element_type.134
  443.1 61.9 %all-gather.21.cloned.1.call-done = bf16[2,2048,1408]{2,1,0:T(8,128)(2,1)} async-done(((bf16[2,256,1408]{2,1,0:T(8,128)(2,1)}), bf16[2,2048,1408]{2,1,0:T(8,128)(2,1)}) %all-gather.21.cloned.1.call-update) | async-done | bytes 11534352 | tf_op jit(solution)/shard_map/all_gather | solution.py:135
  505.0 82.8 %all-gather.19.cloned.1.call-done = bf16[1024,2048]{1,0:T(8,128)(2,1)} async-done(((bf16[256,2048]{1,0:T(8,128)(2,1)}), bf16[1024,2048]{1,0:T(8,128)(2,1)}) %all-gather.19.cloned.1.call-update) | async-done | bytes 4194320 | tf_op jit(solution)/shard_map/all_gather | solution.py:156
  587.8 18.6 %convolution_bitcast_fusion.4 = f32[2,1024,1408]{2,1,0:T(8,128)} fusion(bf16[2,2048,1408]{2,1,0:T(8,128)(2,1)} %all-gather.21.cloned.1.call-done, bf16[1024,2048]{1,0:T(8,128)(2,1)} %all-gather.19.cloned.1.call-done), kind=kOutput, calls=%fused_computation.88 | convolution fusion | flops 11811160064 | bytes 27262976 | tf_op jit(solution)/shard_map/td,jdf->jtf/dot_general | solution.py:157
  606.4 62.8 %all-gather.25.cloned.1.call-done = bf16[1024,2048]{1,0:T(8,128)(2,1)} async-done(((bf16[256,2048]{1,0:T(8,128)(2,1)}), bf16[1024,2048]{1,0:T(8,128)(2,1)}) %all-gather.25.cloned.1.call-update) | async-done | bytes 4194320 | tf_op jit(solution)/shard_map/all_gather | solution.py:174
  669.3 45.4 %all-gather.23.cloned.1.call-done = bf16[1408,2048]{1,0:T(8,128)(2,1)} async-done(((bf16[1408,256]{1,0:T(8,128)(2,1)}), bf16[1408,2048]{1,0:T(8,128)(2,1)}) %all-gather.23.cloned.1.call-update) | async-done | bytes 5767184 | tf_op jit(solution)/shard_map/all_gather | solution.py:136
  714.6 15.7 fusion.60
  732.8 16.3 bitcast_convert_fusion.1
  749.2 11.3 convolution_convert_fusion.1
  760.5 65.5 %reduce-scatter.13.cloned.1.call-done = bf16[256,2048]{1,0:T(8,128)(2,1)} async-done(((bf16[1024,2048]{1,0:T(8,128)(2,1)}), bf16[256,2048]{1,0:T(8,128)(2,1)}) %reduce-scatter.13.cloned.1.call-update) | async-done | bytes 1048592 | tf_op jit(solution)/shard_map/reduce_scatter | solution.py:185
  826.1 80.1 %reduce-scatter.11.cloned.1.call-done = bf16[256,2048]{1,0:T(8,128)(2,1)} async-done(((bf16[1024,2048]{1,0:T(8,128)(2,1)}), bf16[256,2048]{1,0:T(8,128)(2,1)}) %reduce-scatter.11.cloned.1.call-update) | async-done | bytes 1048592 | tf_op jit(solution)/shard_map/reduce_scatter | solution.py:163
  906.2 6.4 fusion.70
  914.3 10.4 convolution_convert_fusion
  926.7 69.0 %all-gather.27.cloned.1.call-done = bf16[1024,2048]{1,0:T(8,128)(2,1)} async-done(((bf16[256,2048]{1,0:T(8,128)(2,1)}), bf16[1024,2048]{1,0:T(8,128)(2,1)}) %all-gather.27.cloned.1.call-update) | async-done | bytes 4194320 | tf_op jit(solution)/shard_map/all_gather | solution.py:190
  995.7 7.8 multiply_reduce_fusion.2
  1003.5 3.1 reshape.423
  1006.5 2.6 multiply_reduce_fusion.3
  1009.3 2.2 add_add_fusion.1
  1013.1 3.8 convolution_convert_fusion.2
  1020.6 169.8 %while.40 = (s32[]{:T(128)}, f32[4,128,128]{2,1,0:T(8,128)S(1)}, f32[16,64,4,128]{3,2,1,0:T(4,128)}, f32[16,64,4,128]{3,2,1,0:T(4,128)S(1)}, f32[16,64,4,128]{3,...) while((s32[]{:T(128)}, f32[4,128,128]{2,1,0:T(8,128)S(1)}, ...), condition=%wide.region_16.17_spmd.clone, body=%wide.region_11.16_spmd.clone.sunk | while | flops 332763136 | bytes 10399947 | solution.py:58
  1190.5 2.9 copy.169
  1194.5 3.0 reshape.424
  1199.4 3.0 copy.168
  1204.3 5.3 fusion.75
  1210.9 9.2 convert_bitcast_fusion.1
  1221.9 17.4 %convert_bitcast_fusion = bf16[2,2048,1408]{1,2,0:T(8,128)(2,1)} fusion(bf16[1024,2048]{1,0:T(8,128)(2,1)} %all-gather.19.cloned.1.call-done, bf16[1,1024,1408]{2,1,0:T(8,128)(2,1)} %copy-done.58, bf16[1,1024,1408]{2,1,0:T(8,128)(2,1)S(1)} %copy-done.57), kind=kOutput, calls=%fused_computation.83 | convolution fusion | flops 11819810816 | bytes 21495808 | tf_op jit(solution)/shard_map/td,jtf->jdf/dot_general | solution.py:179
  1241.2 4.7 fusion.105
  1246.0 11.2 bitcast_convert_fusion
  1258.6 2.5 fusion.109
  1266.0 14.9 reduce-scatter.17.cloned.1.call-done
  1280.9 6.0 fusion.111
  1287.0 2.2 copy.181
  1289.2 4.1 copy.178
  1293.7 2.4 copy.179
  1296.0 76.0 %reduce-scatter.21.cloned.1.call-done = bf16[2,256,1408]{1,2,0:T(8,128)(2,1)} async-done(((bf16[2,2048,1408]{1,2,0:T(8,128)(2,1)}), bf16[2,256,1408]{1,2,0:T(8,128)(2,1)}) %reduce-scatter.21.cloned.1.call-update) | async-done | bytes 1441808 | tf_op jit(solution)/shard_map/reduce_scatter | solution.py:215
  1372.1 7.5 fusion.107
  1382.8 3.2 multiply_reduce_fusion.1
  1386.0 3.4 copy.188
  1389.4 3.5 copy.189
  1393.0 2.2 copy.190
  1395.2 3.0 copy.187
  1398.2 20.6 %all-gather.35.cloned.1.call-done = bf16[1408,2048]{1,0:T(8,128)(2,1)} async-done(((bf16[1408,256]{1,0:T(8,128)(2,1)}), bf16[1408,2048]{1,0:T(8,128)(2,1)}) %all-gather.35.cloned.1.call-update) | async-done | bytes 5767184 | tf_op jit(solution)/shard_map/all_gather | solution.py:255
  1418.9 79.6 %reduce-scatter.15.cloned.1.call-done = bf16[256,2048]{1,0:T(8,128)(2,1)} async-done(((bf16[1024,2048]{1,0:T(8,128)(2,1)}), bf16[256,2048]{1,0:T(8,128)(2,1)}) %reduce-scatter.15.cloned.1.call-update) | async-done | bytes 1048592 | tf_op jit(solution)/shard_map/reduce_scatter | solution.py:203
  1498.5 2.3 fusion.71
  1500.8 28.2 %all-gather.31.cloned.1.call-done = bf16[512,2048]{1,0:T(8,128)(2,1)} async-done(((bf16[512,256]{1,0:T(8,128)(2,1)}), bf16[512,2048]{1,0:T(8,128)(2,1)}) %all-gather.31.cloned.1.call-update) | async-done | bytes 2097168 | tf_op jit(solution)/shard_map/all_gather | solution.py:253
  1529.0 40.2 %all-reduce.1 = (f32[3]{0:T(128)S(1)}, f32[4,2048]{1,0:T(4,128)S(1)}) all-reduce(f32[3]{0:T(128)S(1)} %pad_maximum_fusion.7, f32[4,2048]{1,0:T(4,128)S(1)} %pad_maximum_fusion.6), channel_id=1, replica_groups=mesh['dp'=8,'mp'=4] {'dp','mp'}, use_global_device_ids=true, to_apply=%region_22.23 | all-reduce | flops 8195 | bytes 65560 | tf_op jit(solution)/shard_map/psum | solution.py:239
  1570.5 4.4 fusion.78
  1574.9 3.1 copy.183
  1582.7 8.7 copy.186
  1591.4 59.0 %all-gather.33.cloned.1.call-done = bf16[2,2048,1408]{1,2,0:T(8,128)(2,1)} async-done(((bf16[2,256,1408]{1,2,0:T(8,128)(2,1)}), bf16[2,2048,1408]{1,2,0:T(8,128)(2,1)}) %all-gather.33.cloned.1.call-update) | async-done | bytes 11534352 | tf_op jit(solution)/shard_map/all_gather | solution.py:254
  1650.5 16.0 copy.191
  1667.8 6.2 copy.368
  (748 shorter events, 335.8 us)
Async XLA Ops:
  7.2 88.8 %all-gather.13.cloned.1.call-start = ((), (), s32[]{:S(2)}) async-start(), calls=%async_computation.8 | async-start | bytes 5242880 | tf_op jit(solution)/shard_map/all_gather | solution.py:140
  8.2 4.2 copy-start.37
  8.2 4.3 copy-start.17
  9.8 2.5 copy-start.50
  9.9 2.5 copy-start.48
  12.4 2.1 copy-start.54
  12.4 130.2 %all-gather.15.cloned.1.call-start = ((), (), s32[]{:S(2)}) async-start(), calls=%async_computation.9 | async-start | bytes 7077888 | tf_op jit(solution)/shard_map/all_gather | solution.py:133
  13.5 268.1 %all-gather.17.cloned.1.call-start = ((), (), s32[]{:S(2)}) async-start(), calls=%async_computation.10 | async-start | bytes 2359296 | tf_op jit(solution)/shard_map/all_gather | solution.py:134
  14.3 419.9 %reduce-scatter.9.cloned.1.call-start = ((), (), s32[]{:S(2)}) async-start(), calls=%async_computation.11 | async-start | bytes 10485760 | tf_op jit(solution)/shard_map/reduce_scatter | solution.py:153
  14.4 144.9 %copy-start.44 = (f32[1,512]{1,0:T(1,128)}, f32[1,512]{1,0:T(1,128)S(1)}, u32[]{:S(2)}) copy-start(f32[1,512]{1,0:T(1,128)S(1)} %get-tuple-element.674) | copy-start | bytes 6148
  14.5 144.9 %copy-start.46 = (f32[1,512]{1,0:T(1,128)}, f32[1,512]{1,0:T(1,128)S(1)}, u32[]{:S(2)}) copy-start(f32[1,512]{1,0:T(1,128)S(1)} %get-tuple-element.675) | copy-start | bytes 6148
  15.7 143.6 %copy-start.39 = (f32[16,64]{1,0:T(8,128)}, f32[16,64]{1,0:T(8,128)S(1)}, u32[]{:S(2)}) copy-start(f32[16,64]{1,0:T(8,128)S(1)} %fusion.96) | copy-start | bytes 12292
  152.8 4.6 copy-start.9
  159.3 2.0 copy-start.5
  278.3 2.7 copy-start.16
  281.6 7.7 copy-start.30
  289.4 144.9 %copy-start.3 = (bf16[256,2048]{1,0:T(8,128)(2,1)S(1)}, bf16[256,2048]{1,0:T(8,128)(2,1)}, u32[]{:S(2)}) copy-start(bf16[256,2048]{1,0:T(8,128)(2,1)} %param.22) | copy-start | bytes 3145732
  289.4 215.6 %all-gather.21.cloned.1.call-start = ((), (), s32[]{:S(2)}) async-start(), calls=%async_computation.13 | async-start | bytes 12976128 | tf_op jit(solution)/shard_map/all_gather | solution.py:135
  292.6 295.2 %all-gather.19.cloned.1.call-start = ((), (), s32[]{:S(2)}) async-start(), calls=%async_computation.12 | async-start | bytes 5242880 | tf_op jit(solution)/shard_map/all_gather | solution.py:156
  437.5 2.0 copy-start.13
  438.7 230.6 %all-gather.25.cloned.1.call-start = ((), (), s32[]{:S(2)}) async-start(), calls=%async_computation.16 | async-start | bytes 5242880 | tf_op jit(solution)/shard_map/all_gather | solution.py:174
  440.7 274.0 %all-gather.23.cloned.1.call-start = ((), (), s32[]{:S(2)}) async-start(), calls=%async_computation.14 | async-start | bytes 6488064 | tf_op jit(solution)/shard_map/all_gather | solution.py:136
  443.0 383.0 %reduce-scatter.13.cloned.1.call-start = ((), (), s32[]{:S(2)}) async-start(), calls=%async_computation.17 | async-start | bytes 5242880 | tf_op jit(solution)/shard_map/reduce_scatter | solution.py:185
  730.3 2.5 copy-start.58
  749.1 157.0 %reduce-scatter.11.cloned.1.call-start = ((), (), s32[]{:S(2)}) async-start(), calls=%async_computation.15 | async-start | bytes 5242880 | tf_op jit(solution)/shard_map/reduce_scatter | solution.py:163
  760.5 235.2 %all-gather.27.cloned.1.call-start = ((), (), s32[]{:S(2)}) async-start(), calls=%async_computation.18 | async-start | bytes 5242880 | tf_op jit(solution)/shard_map/all_gather | solution.py:190
  826.1 86.5 %copy-start.12 = (bf16[256,2048]{1,0:T(8,128)(2,1)S(1)}, bf16[256,2048]{1,0:T(8,128)(2,1)}, u32[]{:S(2)}) copy-start(bf16[256,2048]{1,0:T(8,128)(2,1)} %reduce-scatter.13.cloned.1.call-done) | copy-start | bytes 3145732
  906.2 6.4 copy-start.1
  906.2 6.4 copy-start.14
  914.3 325.2 %reduce-scatter.23.cloned.1.call-start = ((), (), s32[]{:S(2)}) async-start(), calls=%async_computation.26 | async-start | bytes 6488064 | tf_op jit(solution)/shard_map/reduce_scatter | solution.py:218
  924.8 332.5 %reduce-scatter.19.cloned.1.call-start = ((), (), s32[]{:S(2)}) async-start(), calls=%async_computation.22 | async-start | bytes 2359296 | tf_op jit(solution)/shard_map/reduce_scatter | solution.py:212
  1006.5 2.8 copy-start.8
  1009.3 2.2 copy-start.31
  1009.3 3.8 copy-start.53
  1016.9 264.1 %reduce-scatter.17.cloned.1.call-start = ((), (), s32[]{:S(2)}) async-start(), calls=%async_computation.20 | async-start | bytes 7077888 | tf_op jit(solution)/shard_map/reduce_scatter | solution.py:209
  1190.5 7.1 copy-start.7
  1202.4 1.9 copy-start.45
  1202.4 1.9 copy-start.47
  1204.3 6.6 copy-start.32
  1204.3 6.6 copy-start.52
  1220.1 1.8 copy-start.57
  1220.2 151.9 %reduce-scatter.21.cloned.1.call-start = ((), (), s32[]{:S(2)}) async-start(), calls=%async_computation.24 | async-start | bytes 12976128 | tf_op jit(solution)/shard_map/reduce_scatter | solution.py:215
  1239.4 179.5 %all-gather.35.cloned.1.call-start = ((), (), s32[]{:S(2)}) async-start(), calls=%async_computation.27 | async-start | bytes 6488064 | tf_op jit(solution)/shard_map/all_gather | solution.py:255
  1245.9 252.6 %reduce-scatter.15.cloned.1.call-start = ((), (), s32[]{:S(2)}) async-start(), calls=%async_computation.19 | async-start | bytes 5242880 | tf_op jit(solution)/shard_map/reduce_scatter | solution.py:203
  1257.2 3.9 copy-start.18
  1257.3 271.7 %all-gather.31.cloned.1.call-start = ((), (), s32[]{:S(2)}) async-start(), calls=%async_computation.23 | async-start | bytes 2359296 | tf_op jit(solution)/shard_map/all_gather | solution.py:253
  1261.1 321.7 %all-gather.29.cloned.1.call-start = ((), (), s32[]{:S(2)}) async-start(), calls=%async_computation.21 | async-start | bytes 7077888 | tf_op jit(solution)/shard_map/all_gather | solution.py:252
  1280.9 6.1 copy-start.11
  1286.9 363.5 %all-gather.33.cloned.1.call-start = ((), (), s32[]{:S(2)}) async-start(), calls=%async_computation.25 | async-start | bytes 12976128 | tf_op jit(solution)/shard_map/all_gather | solution.py:254
  1289.2 4.4 copy-start.23
  1296.0 83.5 %copy-start.55 = (s32[8]{0:T(128)S(1)}, s32[8]{0:T(128)}, u32[]{:S(2)}) copy-start(s32[8]{0:T(128)} %param.24) | copy-start | bytes 100
  1296.0 86.7 %copy-start.40 = (f32[16,64]{1,0:T(8,128)S(1)}, f32[16,64]{1,0:T(8,128)}, u32[]{:S(2)}) copy-start(f32[16,64]{1,0:T(8,128)} %copy-done.39) | copy-start | bytes 12292
  1372.0 10.7 copy-start.6
  1389.4 3.5 copy-start.10
  1395.2 103.3 %copy-start.4 = (bf16[256,2048]{1,0:T(8,128)(2,1)S(1)}, bf16[256,2048]{1,0:T(8,128)(2,1)}, u32[]{:S(2)}) copy-start(bf16[256,2048]{1,0:T(8,128)(2,1)} %param.22) | copy-start | bytes 3145732
  1395.2 103.3 %copy-start.38 = (f32[1,2048]{1,0:T(1,128)S(1)}, f32[1,2048]{1,0:T(1,128)}, u32[]{:S(2)}) copy-start(f32[1,2048]{1,0:T(1,128)} %copy-done.37) | copy-start | bytes 24580
  1395.2 103.3 %copy-start.49 = (f32[256]{0:T(256)S(1)}, f32[256]{0:T(256)}, u32[]{:S(2)}) copy-start(f32[256]{0:T(256)} %copy-done.48) | copy-start | bytes 3076
  1398.2 171.5 %copy-start.51 = (f32[256]{0:T(256)S(1)}, f32[256]{0:T(256)}, u32[]{:S(2)}) copy-start(f32[256]{0:T(256)} %copy-done.50) | copy-start | bytes 3076
  1398.2 171.6 %copy-start.41 = (f32[4,2048]{1,0:T(4,128)S(1)}, f32[4,2048]{1,0:T(4,128)}, u32[]{:S(2)}) copy-start(f32[4,2048]{1,0:T(4,128)} %param.27) | copy-start | bytes 98308
  1398.2 171.6 %copy-start.42 = (f32[4,2048]{1,0:T(4,128)S(1)}, f32[4,2048]{1,0:T(4,128)}, u32[]{:S(2)}) copy-start(f32[4,2048]{1,0:T(4,128)} %param.26) | copy-start | bytes 98308
  1398.2 172.2 %copy-start.2 = (f32[256,2048]{1,0:T(8,128)S(1)}, f32[256,2048]{1,0:T(8,128)}, u32[]{:S(2)}) copy-start(f32[256,2048]{1,0:T(8,128)} %copy-done) | copy-start | bytes 6291460
  1569.2 5.7 copy-start.43
  1574.9 3.1 copy-start.20
  1591.4 75.0 %copy-start.24 = (bf16[512,2048]{1,0:T(8,128)(2,1)S(1)}, bf16[512,2048]{1,0:T(8,128)(2,1)}, u32[]{:S(2)}) copy-start(bf16[512,2048]{1,0:T(8,128)(2,1)} %all-gather.31.cloned.1.call-done) | copy-start | bytes 6291460
  (15 other events, 21.0 us)
Sparse Core Ops, SparseCore 0:
  12.5 83.4 all-gather.12
  98.5 44.0 all-gather.14
  145.1 28.1 all-gather.16
  289.5 144.6 reduce-scatter.8
  436.5 68.4 all-gather.20
  507.0 80.7 all-gather.18
  589.9 79.2 all-gather.24
  671.7 42.8 all-gather.22
  749.3 76.7 reduce-scatter.12
  828.9 77.2 reduce-scatter.10
  914.4 81.2 all-gather.26
  999.6 57.5 reduce-scatter.22
  1060.8 41.2 reduce-scatter.18
  1220.3 60.5 reduce-scatter.16
  1285.2 86.7 reduce-scatter.20
  1374.5 44.3 all-gather.34
  1421.7 76.7 reduce-scatter.14
  1500.2 28.7 all-gather.30
  1530.8 47.3 all-gather.28
  1580.5 69.8 all-gather.32
where the time goes:
time: 1690 us; the launch traced here: 1680 us
  waiting for transfers between devices  1010 us (60%)
  matrix products  279 us (17%)
  local copies, waits for them, and re-layouts  208 us (12%)
  other arithmetic  120 us (7%)
  blocking collectives  40.2 us (2%)
    reduce_scatter x1, waiting for transfers between devices, body(): mix = lax.psum_scatter(mix_part, 'mp', scatter_dimension=0, tiled=True)  142 us
    unnamed x138, local copies, waits for them, and re-layouts  84.9 us
    all_gather x1, waiting for transfers between devices, body(): lax.all_gather(normed_two.astype(jnp.bfloat16), 'mp', axis=0, tiled=True)  82.8 us
    all_gather x1, waiting for transfers between devices, body(): lax.all_gather(normed_one.astype(jnp.bfloat16), 'mp', axis=0, tiled=True)  80.3 us
    reduce_scatter x1, waiting for transfers between devices, body(): lax.psum_scatter(ffn_part.astype(jnp.bfloat16), 'mp', scatter_dimension=0...  80.1 us
    reduce_scatter x1, waiting for transfers between devices, body(): lax.psum_scatter(grad_one_part.astype(jnp.bfloat16), 'mp', scatter_dimens...  79.6 us
    reduce_scatter x1, waiting for transfers between devices, body(): lax.psum_scatter(grad_gate_up.astype(jnp.bfloat16), 'dp', scatter_dimensi...  76 us
    all_gather x1, waiting for transfers between devices, body(): lax.all_gather(grad_resid.astype(jnp.bfloat16), 'mp', axis=0, tiled=True)  69 us
  transfers between devices with their start and end apart: 20, of which 16 were waited for; matrix products, arithmetic and copies ran while one was open for 31% of the time, Pallas kernels for 0%

commit v1 on v0

v1 whole, which is shorter than its diff:
```python
import jax
import jax.numpy as jnp
import numpy as np
from jax import lax
from jax.experimental import pallas as pl
from jax.experimental.pallas import tpu as pltpu
from jax.sharding import PartitionSpec as P

HEAD = 128
STEP = 10
CHUNK = 128

EPS = 1e-06
BETA_ONE = 0.9
BETA_TWO = 0.95
DECAY = 0.1
ADAM_EPS = 1e-08
LEARN_RATE = 0.005

NN = ((1,), (0,))
NT = ((1,), (1,))
TN = ((0,), (0,))


def bf16(value):
    return value.astype(jnp.bfloat16)


def f32(value):
    return value.astype(jnp.float32)


def dot(left, right, dims=NN):
    return lax.dot_general(left, right, (dims, ((), ())), preferred_element_type=jnp.float32)


def dot_low(left, right, dims):
    return dot(bf16(left), bf16(right), dims)


def dot_high(left, right, dims):
    left_top, right_top = bf16(left), bf16(right)
    left_rest = bf16(left - f32(left_top))
    right_rest = bf16(right - f32(right_top))
    return (
        dot(left_top, right_top, dims)
        + dot(left_top, right_rest, dims)
        + dot(left_rest, right_top, dims)
    )


def masked_sum(mask, rows, dims):
    top = bf16(rows)
    return dot(mask, top, dims) + dot(mask, bf16(rows - f32(top)), dims)


def gates(forget_raw, lower, keep):
    sigma = jax.nn.sigmoid(forget_raw)
    forget = lower + (1.0 - lower) * sigma
    return sigma, forget, keep * jnp.log(forget), keep * (1.0 - forget)


def causal_mask(rows):
    later = lax.broadcasted_iota(jnp.int32, (rows, rows), 0)
    return later >= lax.broadcasted_iota(jnp.int32, (rows, rows), 1)


def keep_rows(block, rows, length):
    pos = block * rows + lax.broadcasted_iota(jnp.int32, (rows, 1), 0)
    return (pos < length).astype(jnp.float32)


def forward_kernel(length, place, proj, low, gain, core, rec_out, state_out, carry):
    step = pl.program_id(0)
    rows, channels = core.shape

    @pl.when(step == 0)
    def _():
        carry[...] = jnp.zeros_like(carry)

    keep = keep_rows(step, rows, length[0])
    causal = causal_mask(rows)
    ones = causal.astype(jnp.bfloat16)
    for head in range(channels // HEAD):
        cut = pl.ds(head * HEAD, HEAD)
        query_raw = proj[:, cut]
        value = proj[:, pl.ds(2 * channels + head * HEAD, HEAD)]
        lower = low[:, cut]
        forget_raw = proj[:, pl.ds(channels + head * HEAD, HEAD)]
        _, _, logf, key = gates(forget_raw, lower, keep)
        query = query_raw * jax.nn.sigmoid(query_raw)
        run = masked_sum(ones, logf, NN)
        last = run[rows - 1 :, :]
        query_up = query * jnp.exp(run)
        key_down = key * jnp.exp(-run)
        key_tail = key * jnp.exp(last - run)
        state = carry[head]
        state_out[0, head] = state
        scores = jnp.where(causal, dot_low(query_up, key_down, NT), 0.0)
        rec = dot_low(query_up, state, NT) + dot_low(scores, value, NN)
        carry[head] = state * jnp.exp(last) + dot_low(value, key_tail, TN)
        rec_out[:, cut] = rec
        scale = lax.rsqrt(jnp.mean(rec * rec, axis=-1, keepdims=True) + EPS)
        core[:, cut] = bf16(rec * scale * gain[:, cut])


def recurrence_forward(length, place, proj, lower, gain):
    total, wide = proj.shape
    channels = wide // 3
    heads = channels // HEAD
    steps = total // CHUNK
    return pl.pallas_call(
        forward_kernel,
        grid_spec=pltpu.PrefetchScalarGridSpec(
            num_scalar_prefetch=2,
            grid=(steps,),
            in_specs=[
                pl.BlockSpec((CHUNK, wide), lambda i, n, at: (at[i], 0)),
                pl.BlockSpec((1, channels), lambda i, n, at: (0, 0)),
                pl.BlockSpec((1, channels), lambda i, n, at: (0, 0)),
            ],
            out_specs=[
                pl.BlockSpec((CHUNK, channels), lambda i, n, at: (i, 0)),
                pl.BlockSpec((CHUNK, channels), lambda i, n, at: (i, 0)),
                pl.BlockSpec((1, heads, HEAD, HEAD), lambda i, n, at: (i, 0, 0, 0)),
            ],
            scratch_shapes=[pltpu.VMEM((heads, HEAD, HEAD), jnp.float32)],
        ),
        out_shape=[
            jax.ShapeDtypeStruct((total, channels), jnp.bfloat16),
            jax.ShapeDtypeStruct((total, channels), jnp.float32),
            jax.ShapeDtypeStruct((steps, heads, HEAD, HEAD), jnp.float32),
        ],
        compiler_params=pltpu.CompilerParams(vmem_limit_bytes=24 * 1024 * 1024),
        cost_estimate=pl.CostEstimate(
            flops=12 * total * channels * HEAD,
            bytes_accessed=total * channels * 18,
            transcendentals=6 * total * channels,
        ),
        name="recurrence_forward",
    )(length, place, proj, lower, gain)


def backward_kernel(
    length, place, place_core, proj, low, gain, rec_in, state_in, gcore_in, grad, sums, carry, ends
):
    step = pl.program_id(0)
    rows, channels = rec_in.shape

    @pl.when(step == 0)
    def _():
        carry[...] = jnp.zeros_like(carry)
        ends[...] = jnp.zeros_like(ends)
        sums[...] = jnp.zeros_like(sums)

    keep = keep_rows(pl.num_programs(0) - 1 - step, rows, length[0])
    causal = causal_mask(rows)
    ones = causal.astype(jnp.bfloat16)
    for head in range(channels // HEAD):
        cut = pl.ds(head * HEAD, HEAD)
        cut_forget = pl.ds(channels + head * HEAD, HEAD)
        cut_value = pl.ds(2 * channels + head * HEAD, HEAD)
        query_raw = proj[:, cut]
        value = proj[:, cut_value]
        lower = low[:, cut]
        sigma, forget, logf, key = gates(proj[:, cut_forget], lower, keep)
        sig_query = jax.nn.sigmoid(query_raw)
        query = query_raw * sig_query
        run = masked_sum(ones, logf, NN)
        last = run[rows - 1 :, :]
        up = jnp.exp(run)
        down = jnp.exp(-run)
        tail = jnp.exp(last - run)
        query_up = query * up
        key_down = key * down
        key_tail = key * tail
        rec = rec_in[:, cut]
        gcore = f32(gcore_in[:, cut])
        scale = lax.rsqrt(jnp.mean(rec * rec, axis=-1, keepdims=True) + EPS)
        normed = rec * scale
        weighted = gcore * gain[:, cut]
        grec = scale * (weighted - normed * jnp.mean(normed * weighted, axis=-1, keepdims=True))
        state = state_in[0, head]
        after = carry[head]
        scores = jnp.where(causal, dot_low(query_up, key_down, NT), 0.0)
        gscores = jnp.where(causal, dot_high(grec, value, NT), 0.0)
        gquery_up = dot_high(grec, state, NN) + dot_high(gscores, key_down, NN)
        gkey_down = dot_high(gscores, query_up, TN)
        gkey_tail = dot_high(value, after, NN)
        gvalue = dot_low(scores, grec, TN) + dot_low(key_tail, after, NT)
        carry[head] = after * jnp.exp(last) + dot_low(grec, query_up, TN)
        gquery = gquery_up * up
        gkey = gkey_down * down + gkey_tail * tail
        end = jnp.sum(ends[head] * after, axis=0, keepdims=True)
        ends[head] = state
        glogf = masked_sum(ones, query * gquery - key * gkey, TN) + end
        gforget = keep * (glogf / forget - gkey)
        rising = 1.0 - sigma
        grad[:, cut] = bf16(gquery * sig_query * (1.0 + query_raw * (1.0 - sig_query)))
        grad[:, cut_forget] = bf16(gforget * (1.0 - lower) * sigma * rising)
        grad[:, cut_value] = bf16(gvalue)
        sums[0:1, cut] += jnp.sum(gcore * normed, axis=0, keepdims=True)
        sums[1:2, cut] += jnp.sum(gforget * rising, axis=0, keepdims=True)


def recurrence_backward(length, place, place_core, proj, lower, gain, rec, states, gcore):
    total, wide = proj.shape
    channels = wide // 3
    heads = channels // HEAD
    steps = total // CHUNK
    end = steps - 1
    return pl.pallas_call(
        backward_kernel,
        grid_spec=pltpu.PrefetchScalarGridSpec(
            num_scalar_prefetch=3,
            grid=(steps,),
            in_specs=[
                pl.BlockSpec((CHUNK, wide), lambda i, n, at, ac: (at[end - i], 0)),
                pl.BlockSpec((1, channels), lambda i, n, at, ac: (0, 0)),
                pl.BlockSpec((1, channels), lambda i, n, at, ac: (0, 0)),
                pl.BlockSpec((CHUNK, channels), lambda i, n, at, ac: (end - i, 0)),
                pl.BlockSpec((1, heads, HEAD, HEAD), lambda i, n, at, ac: (end - i, 0, 0, 0)),
                pl.BlockSpec((CHUNK, channels), lambda i, n, at, ac: (ac[end - i], 0)),
            ],
            out_specs=[
                pl.BlockSpec((CHUNK, wide), lambda i, n, at, ac: (at[end - i], 0)),
                pl.BlockSpec((8, channels), lambda i, n, at, ac: (0, 0)),
            ],
            scratch_shapes=[
                pltpu.VMEM((heads, HEAD, HEAD), jnp.float32),
                pltpu.VMEM((heads, HEAD, HEAD), jnp.float32),
            ],
        ),
        out_shape=[
            jax.ShapeDtypeStruct((total, wide), jnp.bfloat16),
            jax.ShapeDtypeStruct((8, channels), jnp.float32),
        ],
        compiler_params=pltpu.CompilerParams(vmem_limit_bytes=24 * 1024 * 1024),
        cost_estimate=pl.CostEstimate(
            flops=40 * total * channels * HEAD,
            bytes_accessed=total * channels * 26,
            transcendentals=8 * total * channels,
        ),
        name="recurrence_backward",
    )(length, place, place_core, proj, lower, gain, rec, states, gcore)


class Ring:
    def __init__(self, axis):
        size = lax.axis_size(axis)
        ring = [0, *range(1, size, 2), *range(size - 2, 0, -2)]
        self.axis, self.size = axis, size
        self.ahead = [(ring[i], ring[(i + 1) % size]) for i in range(size)]
        self.back = [(to, start) for start, to in self.ahead]
        rows = np.zeros((size, size), np.int32)
        for at, me in enumerate(ring):
            slots = [me]
            for hop in range(1, size // 2):
                slots += [ring[(at - hop) % size], ring[(at + hop) % size]]
            slots.append(ring[(at + size // 2) % size])
            for slot, owner in enumerate(slots):
                rows[me, owner] = slot
        self.slot_of_owner = rows

    def send(self, value, pairs):
        return lax.ppermute(value, self.axis, pairs)

    def gather(self, own):
        slots, half = [own], own.shape[0] // 2
        one = two = own
        for _ in range(1, self.size // 2):
            one, two = self.send(one, self.ahead), self.send(two, self.back)
            slots += [one, two]
        top, bottom = self.send(one[:half], self.ahead), self.send(two[half:], self.back)
        return [*slots, jnp.concatenate([top, bottom], 0)]

    def scatter(self, parts):
        half = parts[-1].shape[0] // 2
        top = self.send(parts[-1][:half], self.ahead)
        bottom = self.send(parts[-1][half:], self.back)
        one = two = None
        for hop in range(self.size // 2 - 1, 0, -1):
            two, one = (
                parts[2 * hop - 1] if two is None else parts[2 * hop - 1] + two,
                parts[2 * hop] if one is None else parts[2 * hop] + one,
            )
            if top is not None:
                one = jnp.concatenate([one[:half] + top, one[half:]], 0)
                two = jnp.concatenate([two[:half], two[half:] + bottom], 0)
                top = None
            one, two = self.send(one, self.ahead), self.send(two, self.back)
        return f32(parts[0]) + f32(one) + f32(two)


def swap_blocks(axis, blocks):
    size, me = lax.axis_size(axis), lax.axis_index(axis)
    out = [blocks(me)]
    for shift in range(1, size):
        pairs = [(i, (i + shift) % size) for i in range(size)]
        out.append(lax.ppermute(blocks(lax.rem(me + shift, size)), axis, pairs))
    return out


def sum_all(value, axes):
    for axis in axes:
        size, bit = lax.axis_size(axis), 1
        while bit < size:
            value = value + lax.ppermute(value, axis, [(i, i ^ bit) for i in range(size)])
            bit *= 2
    return value


def norm_back(value, scale, gain, grad):
    inner = jnp.mean(value * gain * grad, axis=-1, keepdims=True)
    return scale * gain * grad - value * (scale * scale * scale) * inner


def inverse_rms(value):
    return lax.rsqrt(jnp.mean(value * value, axis=-1, keepdims=True) + EPS)


def moments(first, second, grad):
    first = BETA_ONE * first + (1.0 - BETA_ONE) * grad
    second = BETA_TWO * second + (1.0 - BETA_TWO) * grad * grad
    return (first, second)


def adamw(param, first, second, grad):
    first, second = moments(first, second, grad)
    fix_one = 1.0 - BETA_ONE**STEP
    fix_two = 1.0 - BETA_TWO**STEP
    update = first / fix_one / (jnp.sqrt(second / fix_two) + ADAM_EPS) + DECAY * param
    return (param - LEARN_RATE * update, first, second)


def body(
    block_input,
    cotangent,
    lengths,
    vectors,
    vectors_first,
    vectors_second,
    mixer_in,
    mixer_in_first,
    mixer_in_second,
    mixer_out,
    mixer_out_first,
    mixer_out_second,
    ffn_in,
    ffn_in_first,
    ffn_in_second,
    ffn_out,
    ffn_out_first,
    ffn_out_second,
):
    own_rows, width = block_input.shape
    group = lax.axis_index("dp")
    member = lax.axis_index("mp")
    members = lax.axis_size("mp")
    ring = Ring("mp")
    length = lax.dynamic_index_in_dim(lengths, group, 0, keepdims=True)
    own_pos = member * own_rows + jnp.arange(own_rows, dtype=jnp.int32)
    keep = f32(own_pos < length[0])[:, None]
    channels = mixer_in.shape[2]
    channel_start = member * channels
    group_gain = lax.dynamic_slice_in_dim(vectors[1:2], channel_start, channels, 1)
    lower = lax.dynamic_slice_in_dim(vectors[2:3], channel_start, channels, 1)

    per = own_rows // CHUNK
    blocks = jnp.arange(members * per, dtype=jnp.int32)
    slot = jnp.asarray(ring.slot_of_owner)[member][blocks // per]
    place = slot * per + blocks % per
    place_core = lax.rem(member - blocks // per + members, members) * per + blocks % per

    weight_in = lax.all_gather(bf16(mixer_in), "dp", axis=1, tiled=True)
    weight_out = lax.all_gather(bf16(mixer_out), "mp", axis=0, tiled=True)
    weight_out = lax.all_gather(weight_out, "dp", axis=1, tiled=True)
    weight_gate_up = lax.all_gather(bf16(ffn_in), "dp", axis=1, tiled=True)
    weight_down = lax.all_gather(bf16(ffn_out), "dp", axis=1, tiled=True)

    inputs = f32(block_input)
    scale_one = inverse_rms(inputs)
    normed_one = ring.gather(bf16(inputs * scale_one * vectors[0]))
    proj = jnp.concatenate(
        [jnp.concatenate([dot(rows, weight_in[j]) for j in range(3)], 1) for rows in normed_one], 0
    )
    core, rec, states = recurrence_forward(length, place, proj, lower, group_gain)
    core_own = swap_blocks(
        "mp", lambda owner: lax.dynamic_slice_in_dim(core, owner * own_rows, own_rows, 0)
    )

    def out_rows(shift):
        start = lax.rem(member - shift + members, members) * channels
        return lax.dynamic_slice_in_dim(weight_out, start, channels, 0)

    mix = sum(dot(part, out_rows(shift)) for shift, part in enumerate(core_own))
    resid = inputs + mix
    scale_two = inverse_rms(resid)

    grad_total = f32(cotangent) * keep
    grad_rows = ring.gather(bf16(grad_total))
    normed_two = ring.gather(bf16(resid * scale_two * vectors[3]))
    hidden, grad_gate, grad_up, ffn_parts, two_parts = [], [], [], [], []
    for rows, grows in zip(normed_two, grad_rows):
        gate, up = dot(rows, weight_gate_up[0]), dot(rows, weight_gate_up[1])
        sigma = jax.nn.sigmoid(gate)
        act = gate * sigma
        hidden.append(bf16(act * up))
        ghid = dot(grows, weight_down, NT)
        grad_gate.append(bf16(ghid * up * sigma * (1.0 + gate * (1.0 - sigma))))
        grad_up.append(bf16(ghid * act))
        two_parts.append(
            bf16(
                dot(grad_gate[-1], weight_gate_up[0], NT) + dot(grad_up[-1], weight_gate_up[1], NT)
            )
        )
        ffn_parts.append(bf16(dot(hidden[-1], weight_down)))
    grad_two = ring.scatter(two_parts)
    ffn = ring.scatter(ffn_parts)
    total = resid + ffn
    grad_resid = grad_total + norm_back(resid, scale_two, vectors[3], grad_two)
    gain_two = jnp.sum(grad_two * resid * scale_two, axis=0)

    grad_mix = bf16(grad_resid)
    grad_core = bf16(dot(grad_mix, weight_out, NT))
    grad_core = jnp.concatenate(
        swap_blocks(
            "mp", lambda owner: lax.dynamic_slice_in_dim(grad_core, owner * channels, channels, 1)
        ),
        0,
    )
    grad_proj, sums = recurrence_backward(
        length, place, place_core, proj, lower, group_gain, rec, states, grad_core
    )
    grad_proj_slots = [
        grad_proj[i * own_rows : (i + 1) * own_rows] for i in range(members)
    ]
    one_parts = [
        bf16(
            sum(
                dot(rows[:, j * channels : (j + 1) * channels], weight_in[j], NT) for j in range(3)
            )
        )
        for rows in grad_proj_slots
    ]
    normed_one_all = jnp.concatenate(normed_one, 0)
    sum_in = jnp.stack(
        [
            bf16(dot(normed_one_all, grad_proj[:, j * channels : (j + 1) * channels], TN))
            for j in range(3)
        ]
    )
    grad_one = ring.scatter(one_parts)
    input_grad = grad_resid + norm_back(inputs, scale_one, vectors[0], grad_one)
    gain_one = jnp.sum(grad_one * inputs * scale_one, axis=0)

    grad_all = jnp.concatenate(grad_rows, 0)
    normed_two_all = jnp.concatenate(normed_two, 0)
    sum_down = bf16(dot(jnp.concatenate(hidden, 0), grad_all, TN))
    sum_gate = bf16(dot(normed_two_all, jnp.concatenate(grad_gate, 0), TN))
    sum_up = bf16(dot(normed_two_all, jnp.concatenate(grad_up, 0), TN))
    core_rows = jnp.concatenate(core_own, 1)
    sum_out = bf16(dot(core_rows, grad_mix, TN))
    order = [lax.rem(member - q + members, members) * channels for q in range(members)]
    sum_out = jnp.concatenate(
        [lax.dynamic_slice_in_dim(sum_out, at, channels, 0) for at in order], 0
    )

    def owned(value, axis, name="dp"):
        return lax.psum_scatter(value, name, scatter_dimension=axis, tiled=True)

    shard_down = f32(owned(sum_down, 1))
    shard_gate_up = jnp.stack([f32(owned(sum_gate, 0)), f32(owned(sum_up, 0))])
    shard_out = f32(owned(owned(sum_out, 1), 0, "mp"))
    shard_in = f32(owned(sum_in, 1))

    blank = jnp.zeros((width,), jnp.float32)
    squares = jnp.stack([jnp.sum(keep * part * part) for part in (total, mix, ffn)])
    vector_part = jnp.stack(
        [
            gain_one,
            lax.dynamic_update_slice_in_dim(blank, sums[0], channel_start, 0),
            lax.dynamic_update_slice_in_dim(blank, sums[1], channel_start, 0),
            gain_two,
            lax.dynamic_update_slice_in_dim(blank, squares, 0, 0),
        ]
    )
    vector_sums = sum_all(vector_part, ("dp", "mp"))
    vectors_grad = vector_sums[:4]
    denom = f32(jnp.sum(lengths)) * width
    stats = jnp.sqrt(vector_sums[4, :3] / denom)
    vec_first, vec_second = moments(vectors_first, vectors_second, vectors_grad)

    in_new, in_first, in_second = adamw(mixer_in, mixer_in_first, mixer_in_second, shard_in)
    out_new, out_first, out_second = adamw(mixer_out, mixer_out_first, mixer_out_second, shard_out)
    gu_new, gu_first, gu_second = adamw(ffn_in, ffn_in_first, ffn_in_second, shard_gate_up)
    down_new, down_first, down_second = adamw(ffn_out, ffn_out_first, ffn_out_second, shard_down)
    in_low, out_low, gu_low, down_low = (
        lax.all_gather(bf16(new), "dp", axis=1, tiled=True)
        for new in (in_new, out_new, gu_new, down_new)
    )
    return (
        bf16(total),
        input_grad,
        stats,
        vectors_grad,
        vec_first,
        vec_second,
        shard_in,
        in_new,
        in_first,
        in_second,
        in_low,
        shard_out,
        out_new,
        out_first,
        out_second,
        out_low,
        shard_gate_up,
        gu_new,
        gu_first,
        gu_second,
        gu_low,
        shard_down,
        down_new,
        down_first,
        down_second,
        down_low,
    )


def solution(mesh):
    rows = P(("dp", "mp"), None)
    deep = P(None, "dp", "mp")
    flat = P("mp", "dp")
    in_specs = (
        (rows, rows, P(), P(), P(), P()) + (deep,) * 3 + (flat,) * 3 + (deep,) * 3 + (flat,) * 3
    )
    wide = (deep,) * 4 + (P(None, None, "mp"),)
    tall = (flat,) * 4 + (P("mp", None),)
    out_specs = (rows, rows, P(), P(), P(), P()) + wide + tall + wide + tall
    return jax.shard_map(body, mesh=mesh, in_specs=in_specs, out_specs=out_specs, check_vma=False)
```

time: 1690 us -> 1110 us (0.66)
  waiting for transfers between devices: 1010 us -> 705 us
  local copies, waits for them, and re-layouts: 208 us -> 54.3 us
  matrix products: 279 us -> 179 us
  other arithmetic: 120 us -> 71 us
  starting transfers between devices: 0.83 us -> 43.7 us
  blocking collectives: 40.2 us -> 0 us
  Pallas kernels: 0 us -> 29.7 us
    all_gather x12 -> x9, waiting for transfers between devices: 557 us -> 105 us  [the longest x4 75.9 us: body(): lax.all_gather(bf16(new), 'dp', axis=1, tiled=True)]
    ppermute x0 -> x35, waiting for transfers between devices: none -> 368 us  [the longest x24 324 us: send(): return lax.ppermute(value, self.axis, pairs)]
    reduce_scatter x8 -> x6, waiting for transfers between devices: 458 us -> 231 us  [owned(): return lax.psum_scatter(value, name, scatter_dimension=axis, tiled=True)]
    dot_general x220 -> x60, matrix products: 279 us -> 179 us  [dot(): lax.dot_general(left, right, (dims, ((), ())), preferred_element_type=jnp...]
    squeeze x81 -> x1, local copies, waits for them, and re-layouts: 64.2 us -> 0.69 us  [body(): slot = jnp.asarray(ring.slot_of_owner)[member][blocks // per]]
    unnamed x138 -> x161, local copies, waits for them, and re-layouts: 84.9 us -> 41.1 us
    ppermute x0 -> x35, starting transfers between devices: none -> 42.3 us  [the longest x24 32.3 us: send(): return lax.ppermute(value, self.axis, pairs)]
    psum x1 -> x0, blocking collectives: 40.2 us -> none  [body(): vectors_grad, square_sums = lax.psum((vector_part, squares), ('dp', 'mp'))]
  transfers between devices with their start and end apart: 20 -> 50, of which waited for: 16 -> 32; matrix products, arithmetic and copies ran while one was open for 31% -> 23% of each run, Pallas kernels for 0% -> 3%
where the time goes in v1:
time: 1110 us; the launch traced here: 1100 us
  waiting for transfers between devices  705 us (64%)
  matrix products  179 us (16%)
  other arithmetic  71 us (6%)
  local copies, waits for them, and re-layouts  54.3 us (5%)
  starting transfers between devices  43.7 us (4%)
  Pallas kernels  29.7 us (3%)
  between operations  16.1 us (1%)
    ppermute x24, waiting for transfers between devices, send(): return lax.ppermute(value, self.axis, pairs)  324 us
    reduce_scatter x6, waiting for transfers between devices, owned(): return lax.psum_scatter(value, name, scatter_dimension=axis, tiled=True)  231 us
    dot_general x60, matrix products, dot(): lax.dot_general(left, right, (dims, ((), ())), preferred_element_type=jnp...  179 us
    all_gather x4, waiting for transfers between devices, body(): lax.all_gather(bf16(new), 'dp', axis=1, tiled=True)  75.9 us
    unnamed x161, local copies, waits for them, and re-layouts  41.1 us
    ppermute x6, waiting for transfers between devices, swap_blocks(): out.append(lax.ppermute(blocks(lax.rem(me + shift, size)), axis, pairs))  33.1 us
    ppermute x24, starting transfers between devices, send(): return lax.ppermute(value, self.axis, pairs)  32.3 us
    convert_element_type x8, other arithmetic, bf16(): return value.astype(jnp.bfloat16)  31.1 us
  transfers between devices with their start and end apart: 50, of which 32 were waited for; matrix products, arithmetic and copies ran while one was open for 23% of the time, Pallas kernels for 3%

profile of v1, /device:TPU:0, one launch (start us, length us, event | category | flops | bytes accessed | tf_op | source)
XLA Modules:
  0.0 1097.9 jit_solution(6651923485385524126)
XLA Ops:
  11.6 29.3 %all-gather.12.cloned.1.call-done = bf16[2048,256]{1,0:T(8,128)(2,1)} async-done(((bf16[512,256]{1,0:T(8,128)(2,1)}), bf16[2048,256]{1,0:T(8,128)(2,1)}) %all-gather.12.cloned.1.call-update) | async-done | bytes 1048592 | tf_op jit(solution)/shard_map/all_gather | solution.py:376
  40.9 3.1 convert_element_type.194
  53.9 19.9 %collective-permute-done = bf16[256,2048]{1,0:T(8,128)(2,1)S(1)} collective-permute-done((bf16[256,2048]{1,0:T(8,128)(2,1)}, bf16[256,2048]{1,0:T(8,128)(2,1)S(1)}, u32[]{:S(2)}, u32[]{:S(2)}) %collective-permute-start) | collective-permute-done | bytes 1048608 | tf_op jit(solution)/shard_map/ppermute | solution.py:266
  76.6 19.8 %collective-permute-done.1 = bf16[256,2048]{1,0:T(8,128)(2,1)} collective-permute-done((bf16[256,2048]{1,0:T(8,128)(2,1)}, bf16[256,2048]{1,0:T(8,128)(2,1)}, u32[]{:S(2)}, u32[]{:S(2)}) %collective-permute-start.1) | collective-permute-done | bytes 1048608 | tf_op jit(solution)/shard_map/ppermute | solution.py:266
  103.2 5.5 collective-permute-done.2
  109.8 8.9 collective-permute-done.3
  119.8 2.9 fusion.107
  143.8 11.6 %maximum_maximum_fusion.proj = f32[1024,1536]{1,0:T(8,128)S(1)} fusion(f32[256,512]{1,0:T(8,128)S(1)} %fusion.104, f32[256,512]{1,0:T(8,128)} %fusion.100, f32[256,512]{1,0:T(8,128)} %fusion.96, f32[256,512]{1,0:T(8,128)S(1)} %fusion.105, f32[256,512]{1,0:T(8,128)S(1)} %fusion.101, f32[256,512]{1,0:T(8,128)S(1)} %fusion.97, f32[256,512]{1,0:T(8,128)S(1)} %fusion.106, ...), kind=kLoop, calls=%fused_computation.6 | loop fusion | flops 17301504 | bytes 12582912 | tf_op jit(solution)/shard_map/concatenate | solution.py:384
  155.3 11.5 %recurrence_forward.1 = (bf16[1024,512]{1,0:T(8,128)(2,1)S(1)}, f32[1024,512]{1,0:T(8,128)S(1)}, f32[8,4,128,128]{3,2,1,0:T(8,128)S(1)}) custom-call(s32[1]{0:T(128)} %dynamic_slice.61.length, s32[8]{0:T(128)S(1)} %multiply_add_fusion.5.place, f32[1024,1536]{1,0:T(8,128)S(1)} %maximum_maximum_fusion.proj, f32[1,512]{1,0:T(1,128)S(1)} %get-tuple-element.137.low, ...), custom_call_target="tpu_custom_call" | custom-call | flops 805306368 | bytes 9437184 | tf_op jit(solution)/shard_map/recurrence_forward/pallas_call | solution.py:112
  175.7 14.2 %collective-permute-done.4 = bf16[256,512]{1,0:T(8,128)(2,1)S(1)} collective-permute-done((bf16[256,512]{1,0:T(8,128)(2,1)S(1)}, bf16[256,512]{1,0:T(8,128)(2,1)S(1)}, u32[]{:S(2)}, u32[]{:S(2)}) %collective-permute-start.4) | collective-permute-done | bytes 262176 | tf_op jit(solution)/shard_map/ppermute | solution.py:300
  193.2 3.2 multiply_reduce_fusion.2
  197.7 4.4 collective-permute-start.8
  207.3 20.7 %collective-permute-done.8 = bf16[256,2048]{1,0:T(8,128)(2,1)S(1)} collective-permute-done((bf16[256,2048]{1,0:T(8,128)(2,1)S(1)}, bf16[256,2048]{1,0:T(8,128)(2,1)S(1)}, u32[]{:S(2)}, u32[]{:S(2)}) %collective-permute-start.8) | collective-permute-done | bytes 1048608 | tf_op jit(solution)/shard_map/ppermute | solution.py:266
  228.2 22.4 %collective-permute-done.16 = bf16[256,2048]{1,0:T(8,128)(2,1)S(1)} collective-permute-done((bf16[256,2048]{1,0:T(8,128)(2,1)S(1)}, bf16[256,2048]{1,0:T(8,128)(2,1)S(1)}, u32[]{:S(2)}, u32[]{:S(2)}) %collective-permute-start.16) | collective-permute-done | bytes 1048608 | tf_op jit(solution)/shard_map/ppermute | solution.py:266
  251.5 22.2 %collective-permute-done.15 = bf16[256,2048]{1,0:T(8,128)(2,1)S(1)} collective-permute-done((bf16[256,2048]{1,0:T(8,128)(2,1)S(1)}, bf16[256,2048]{1,0:T(8,128)(2,1)S(1)}, u32[]{:S(2)}, u32[]{:S(2)}) %collective-permute-start.15) | collective-permute-done | bytes 1048608 | tf_op jit(solution)/shard_map/ppermute | solution.py:266
  275.9 21.1 %collective-permute-done.7 = bf16[256,2048]{1,0:T(8,128)(2,1)S(1)} collective-permute-done((bf16[256,2048]{1,0:T(8,128)(2,1)S(1)}, bf16[256,2048]{1,0:T(8,128)(2,1)S(1)}, u32[]{:S(2)}, u32[]{:S(2)}) %collective-permute-start.7) | collective-permute-done | bytes 1048608 | tf_op jit(solution)/shard_map/ppermute | solution.py:266
  299.4 7.4 collective-permute-done.9
  307.8 32.0 %collective-permute-done.10 = bf16[128,2048]{1,0:T(8,128)(2,1)S(1)} collective-permute-done((bf16[128,2048]{1,0:T(8,128)(2,1)S(1)}, bf16[128,2048]{1,0:T(8,128)(2,1)S(1)}, u32[]{:S(2)}, u32[]{:S(2)}) %collective-permute-start.10) | collective-permute-done | bytes 524320 | tf_op jit(solution)/shard_map/ppermute | solution.py:266
  340.9 5.9 fusion.86
  346.8 5.9 fusion.82
  352.7 6.2 multiply_convert_fusion.3
  377.1 2.9 fusion.81
  381.9 2.9 fusion.84
  384.8 5.2 multiply_convert_fusion.1
  390.0 3.1 convolution_convert_fusion.8
  393.1 4.1 multiply_convert_fusion.5
  397.2 4.3 fusion.79
  403.4 5.0 multiply_convert_fusion.7
  408.3 3.2 fusion.80
  415.4 4.5 convolution_convert_fusion.10
  429.8 60.9 %collective-permute-done.14 = bf16[256,2048]{1,0:T(8,128)(2,1)S(1)} collective-permute-done((bf16[256,2048]{1,0:T(8,128)(2,1)S(1)}, bf16[256,2048]{1,0:T(8,128)(2,1)S(1)}, u32[]{:S(2)}, u32[]{:S(2)}) %collective-permute-start.14) | collective-permute-done | bytes 1048608 | tf_op jit(solution)/shard_map/ppermute | solution.py:266
  491.5 20.0 %collective-permute-done.22 = bf16[256,2048]{1,0:T(8,128)(2,1)S(1)} collective-permute-done((bf16[256,2048]{1,0:T(8,128)(2,1)S(1)}, bf16[256,2048]{1,0:T(8,128)(2,1)S(1)}, u32[]{:S(2)}, u32[]{:S(2)}) %collective-permute-start.22) | collective-permute-done | bytes 1048608 | tf_op jit(solution)/shard_map/ppermute | solution.py:266
  511.5 3.6 fusion.37
  517.4 3.3 convolution_convert_fusion.3
  522.2 3.9 pad_maximum_fusion
  533.6 12.1 %convolution_convert_fusion = bf16[1408,2048]{1,0:T(8,128)(2,1)} fusion(bf16[1024,2048]{1,0:T(8,128)(2,1)} %constant_dynamic-update-slice_fusion.14, bf16[256,1408]{1,0:T(8,128)(2,1)S(1)} %copy-done.59, bf16[256,1408]{1,0:T(8,128)(2,1)S(1)} %copy-done.62, bf16[256,1408]{1,0:T(8,128)(2,1)S(1)} %copy-done.60, bf16[256,1408]{1,0:T(8,128)(2,1)S(1)} %copy-done.64), kind=kOutput, calls=%fused_computation.2 | convolution fusion | flops 5919997952 | bytes 12845056 | tf_op jit(solution)/shard_map/dot_general | solution.py:34
  547.3 6.1 convolution_convert_fusion.7
  556.7 4.0 collective-permute-done.25
  560.7 14.9 %collective-permute-done.24 = bf16[256,512]{1,0:T(8,128)(2,1)S(1)} collective-permute-done((bf16[256,512]{1,0:T(8,128)(2,1)S(1)}, bf16[256,512]{1,0:T(8,128)(2,1)S(1)}, u32[]{:S(2)}, u32[]{:S(2)}) %collective-permute-start.24) | collective-permute-done | bytes 262176 | tf_op jit(solution)/shard_map/ppermute | solution.py:300
  578.5 18.2 %recurrence_backward.1 = (bf16[1024,1536]{1,0:T(8,128)(2,1)S(1)}, f32[8,512]{1,0:T(8,128)S(1)}) custom-call(s32[1]{0:T(128)} %dynamic_slice.61.length, s32[8]{0:T(128)S(1)} %multiply_add_fusion.5.place, s32[8]{0:T(128)S(1)} %fusion.130.place_core, f32[1024,1536]{1,0:T(8,128)S(1)} %copy-done.1, f32[1,512]{1,0:T(1,128)S(1)} %get-tuple-element.137.low, ...), custom_call_target="tpu_custom_call" | custom-call | flops 2684354560 | bytes 13631488 | tf_op jit(solution)/shard_map/recurrence_backward/pallas_call | solution.py:212
  597.1 4.7 fusion.25
  606.7 3.4 pad_maximum_fusion.1
  610.1 11.6 %convolution_convert_fusion.2 = bf16[2048,1408]{1,0:T(8,128)(2,1)} fusion(bf16[1024,2048]{1,0:T(8,128)(2,1)} %get-tuple-element.118, bf16[256,1408]{1,0:T(8,128)(2,1)} %copy-done.56, bf16[256,1408]{1,0:T(8,128)(2,1)} %get-tuple-element.81, bf16[256,1408]{1,0:T(8,128)(2,1)} %get-tuple-element.87, bf16[256,1408]{1,0:T(8,128)(2,1)} %get-tuple-element.84), kind=kOutput, calls=%fused_computation.4 | convolution fusion | flops 5919997952 | bytes 12845056 | tf_op jit(solution)/shard_map/dot_general | solution.py:34
  622.3 11.9 %convolution_convert_fusion.1 = bf16[2048,1408]{1,0:T(8,128)(2,1)} fusion(bf16[1024,2048]{1,0:T(8,128)(2,1)} %get-tuple-element.118, bf16[256,1408]{1,0:T(8,128)(2,1)} %copy-done.53, bf16[256,1408]{1,0:T(8,128)(2,1)} %get-tuple-element.80, bf16[256,1408]{1,0:T(8,128)(2,1)} %get-tuple-element.86, bf16[256,1408]{1,0:T(8,128)(2,1)} %copy-done.51), kind=kOutput, calls=%fused_computation.3 | convolution fusion | flops 5919997952 | bytes 12845056 | tf_op jit(solution)/shard_map/dot_general | solution.py:34
  634.2 25.1 %reduce-scatter.17.cloned.1.call-done = bf16[1408,256]{1,0:T(8,128)(2,1)} async-done(((bf16[1408,2048]{1,0:T(8,128)(2,1)}), bf16[1408,256]{1,0:T(8,128)(2,1)}) %reduce-scatter.17.cloned.1.call-update) | async-done | bytes 720912 | tf_op jit(solution)/shard_map/reduce_scatter | solution.py:470
  659.4 5.6 fusion.139
  665.0 23.8 %reduce-scatter.11.cloned.1.call-done = bf16[512,256]{1,0:T(8,128)(2,1)} async-done(((bf16[2048,256]{1,0:T(8,128)(2,1)}), bf16[512,256]{1,0:T(8,128)(2,1)}) %reduce-scatter.11.cloned.1.call-update) | async-done | bytes 262160 | tf_op jit(solution)/shard_map/reduce_scatter | solution.py:470
  688.8 2.9 fusion.144
  691.8 61.8 %reduce-scatter.7.cloned.1.call-done = bf16[3,256,512]{2,1,0:T(8,128)(2,1)} async-done(((bf16[3,2048,512]{2,1,0:T(8,128)(2,1)}), bf16[3,256,512]{2,1,0:T(8,128)(2,1)}) %reduce-scatter.7.cloned.1.call-update) | async-done | bytes 786448 | tf_op jit(solution)/shard_map/reduce_scatter | solution.py:470
  753.6 6.2 fusion.146
  759.8 56.7 %reduce-scatter.13.cloned.1.call-done = bf16[256,1408]{1,0:T(8,128)(2,1)} async-done(((bf16[2048,1408]{1,0:T(8,128)(2,1)}), bf16[256,1408]{1,0:T(8,128)(2,1)}) %reduce-scatter.13.cloned.1.call-update) | async-done | bytes 720912 | tf_op jit(solution)/shard_map/reduce_scatter | solution.py:470
  816.6 63.5 %reduce-scatter.15.cloned.1.call-done = bf16[256,1408]{1,0:T(8,128)(2,1)} async-done(((bf16[2048,1408]{1,0:T(8,128)(2,1)}), bf16[256,1408]{1,0:T(8,128)(2,1)}) %reduce-scatter.15.cloned.1.call-update) | async-done | bytes 720912 | tf_op jit(solution)/shard_map/reduce_scatter | solution.py:470
  880.1 8.2 fusion.142
  905.7 18.2 %collective-permute-done.28 = bf16[128,2048]{1,0:T(8,128)(2,1)S(1)} collective-permute-done((bf16[128,2048]{1,0:T(8,128)(2,1)S(1)}, bf16[128,2048]{1,0:T(8,128)(2,1)S(1)}, u32[]{:S(2)}, u32[]{:S(2)}) %collective-permute-start.28) | collective-permute-done | bytes 524320 | tf_op jit(solution)/shard_map/ppermute | solution.py:266
  928.0 22.5 %collective-permute-done.29 = bf16[256,2048]{1,0:T(8,128)(2,1)S(1)} collective-permute-done((bf16[256,2048]{1,0:T(8,128)(2,1)S(1)}, bf16[256,2048]{1,0:T(8,128)(2,1)S(1)}, u32[]{:S(2)}, u32[]{:S(2)}) %collective-permute-start.29) | collective-permute-done | bytes 1048608 | tf_op jit(solution)/shard_map/ppermute | solution.py:266
  950.5 21.9 %collective-permute-done.27 = bf16[256,2048]{1,0:T(8,128)(2,1)S(1)} collective-permute-done((bf16[256,2048]{1,0:T(8,128)(2,1)S(1)}, bf16[256,2048]{1,0:T(8,128)(2,1)S(1)}, u32[]{:S(2)}, u32[]{:S(2)}) %collective-permute-start.27) | collective-permute-done | bytes 1048608 | tf_op jit(solution)/shard_map/ppermute | solution.py:266
  977.9 2.9 collective-permute-done.31
  985.7 4.2 collective-permute-done.33
  990.2 5.3 fusion.45
  997.7 6.1 all-gather.20.cloned.1.call-done
  1003.8 69.8 %all-gather.24.cloned.1.call-done = bf16[2,2048,1408]{2,1,0:T(8,128)(2,1)} async-done(((bf16[2,256,1408]{2,1,0:T(8,128)(2,1)}), bf16[2,2048,1408]{2,1,0:T(8,128)(2,1)}) %all-gather.24.cloned.1.call-update) | async-done | bytes 11534352 | tf_op jit(solution)/shard_map/all_gather | solution.py:499
  1073.6 6.6 copy.65
  1080.2 4.0 copy.66
  1084.2 4.4 copy.67
  (353 shorter events, 170.3 us)
Async XLA Ops:
  7.2 33.6 %all-gather.12.cloned.1.call-start = ((), (), s32[]{:S(2)}) async-start(), calls=%async_computation.7 | async-start | bytes 1310720 | tf_op jit(solution)/shard_map/all_gather | solution.py:376
  9.0 110.8 %all-gather.10.cloned.1.call-start = ((), (), s32[]{:S(2)}) async-start(), calls=%async_computation.6 | async-start | bytes 7077888 | tf_op jit(solution)/shard_map/all_gather | solution.py:375
  11.5 161.7 %all-gather.14.cloned.1.call-start = ((), (), s32[]{:S(2)}) async-start(), calls=%async_computation.8 | async-start | bytes 9437184 | tf_op jit(solution)/shard_map/all_gather | solution.py:377
  40.9 300.0 %all-gather.16.cloned.1.call-start = ((), (), s32[]{:S(2)}) async-start(), calls=%async_computation.9 | async-start | bytes 12976128 | tf_op jit(solution)/shard_map/all_gather | solution.py:378
  44.1 308.5 %all-gather.18.cloned.1.call-start = ((), (), s32[]{:S(2)}) async-start(), calls=%async_computation.10 | async-start | bytes 6488064 | tf_op jit(solution)/shard_map/all_gather | solution.py:379
  47.3 26.6 %collective-permute-start = (bf16[256,2048]{1,0:T(8,128)(2,1)}, bf16[256,2048]{1,0:T(8,128)(2,1)S(1)}, u32[]{:S(2)}, u32[]{:S(2)}) collective-permute-start(bf16[256,2048]{1,0:T(8,128)(2,1)} %get-tuple-element.70), channel_id=1, source_target_pairs={{0,1},{1,3},{3,2},{2,0},{4,5},{5,7},{7,6},{6,4},{8,9},{9,11},{11,1... | collective-permute-start | bytes 3145736 | tf_op jit(solution)/shard_map/ppermute | solution.py:266
  48.8 47.6 %collective-permute-start.1 = (bf16[256,2048]{1,0:T(8,128)(2,1)}, bf16[256,2048]{1,0:T(8,128)(2,1)}, u32[]{:S(2)}, u32[]{:S(2)}) collective-permute-start(bf16[256,2048]{1,0:T(8,128)(2,1)} %get-tuple-element.70), channel_id=1, source_target_pairs={{1,0},{3,1},{2,3},{0,2},{5,4},{7,5},{6,7},{4,6},{9,8},{11,9},{10,1... | collective-permute-start | bytes 3145736 | tf_op jit(solution)/shard_map/ppermute | solution.py:266
  51.2 545.6 %reduce-scatter.9.cloned.1.call-start = ((), (), s32[]{:S(2)}) async-start(), calls=%async_computation.13 | async-start | bytes 9437184 | tf_op jit(solution)/shard_map/reduce_scatter | solution.py:470
  74.7 34.0 %collective-permute-start.2 = (bf16[128,2048]{1,0:T(8,128)(2,1)}, bf16[128,2048]{1,0:T(8,128)(2,1)S(1)}, u32[]{:S(2)}, u32[]{:S(2)}) collective-permute-start(bf16[128,2048]{1,0:T(8,128)(2,1)} %slice.266), channel_id=1, source_target_pairs={{0,1},{1,3},{3,2},{2,0},{4,5},{5,7},{7,6},{6,4},{8,9},{9,11},{11,1... | collective-permute-start | bytes 1572872 | tf_op jit(solution)/shard_map/ppermute | solution.py:266
  97.5 21.2 %collective-permute-start.3 = (bf16[128,2048]{1,0:T(8,128)(2,1)S(1)}, bf16[128,2048]{1,0:T(8,128)(2,1)S(1)}, u32[]{:S(2)}, u32[]{:S(2)}) collective-permute-start(bf16[128,2048]{1,0:T(8,128)(2,1)S(1)} %slice.267), channel_id=1, source_target_pairs={{1,0},{3,1},{2,3},{0,2},{5,4},{7,5},{6,7},{4,6},{9,8},{11,9},{10,1... | collective-permute-start | bytes 1572872 | tf_op jit(solution)/shard_map/ppermute | solution.py:266
  169.5 23.6 %collective-permute-start.5 = (bf16[256,512]{1,0:T(8,128)(2,1)S(1)}, bf16[256,512]{1,0:T(8,128)(2,1)}, u32[]{:S(2)}, u32[]{:S(2)}) collective-permute-start(bf16[256,512]{1,0:T(8,128)(2,1)S(1)} %get-tuple-element.114), channel_id=1, source_target_pairs={{0,2},{1,3},{2,0},{3,1},{4,6},{5,7},{6,4},{7,5},{8,10},{9,11},{10,... | collective-permute-start | bytes 786440 | tf_op jit(solution)/shard_map/ppermute | solution.py:300
  170.7 21.7 %collective-permute-start.6 = (bf16[256,512]{1,0:T(8,128)(2,1)S(1)}, bf16[256,512]{1,0:T(8,128)(2,1)S(1)}, u32[]{:S(2)}, u32[]{:S(2)}) collective-permute-start(bf16[256,512]{1,0:T(8,128)(2,1)S(1)} %get-tuple-element.115), channel_id=1, source_target_pairs={{0,3},{1,0},{2,1},{3,2},{4,7},{5,4},{6,5},{7,6},{8,11},{9,8},{10,9... | collective-permute-start | bytes 786440 | tf_op jit(solution)/shard_map/ppermute | solution.py:300
  172.7 17.2 %collective-permute-start.4 = (bf16[256,512]{1,0:T(8,128)(2,1)S(1)}, bf16[256,512]{1,0:T(8,128)(2,1)S(1)}, u32[]{:S(2)}, u32[]{:S(2)}) collective-permute-start(bf16[256,512]{1,0:T(8,128)(2,1)S(1)} %get-tuple-element.116), channel_id=1, source_target_pairs={{0,1},{1,2},{2,3},{3,0},{4,5},{5,6},{6,7},{7,4},{8,9},{9,10},{10,1... | collective-permute-start | bytes 786440 | tf_op jit(solution)/shard_map/ppermute | solution.py:300
  197.7 30.4 %copy-start.30 = (bf16[256,2048]{1,0:T(8,128)(2,1)}, bf16[256,2048]{1,0:T(8,128)(2,1)S(1)}, u32[]{:S(2)}) copy-start(bf16[256,2048]{1,0:T(8,128)(2,1)S(1)} %get-tuple-element.58) | copy-start | bytes 3145732
  197.7 30.3 %collective-permute-start.8 = (bf16[256,2048]{1,0:T(8,128)(2,1)S(1)}, bf16[256,2048]{1,0:T(8,128)(2,1)S(1)}, u32[]{:S(2)}, u32[]{:S(2)}) collective-permute-start(bf16[256,2048]{1,0:T(8,128)(2,1)S(1)} %get-tuple-element.58), channel_id=1, source_target_pairs={{0,1},{1,3},{3,2},{2,0},{4,5},{5,7},{7,6},{6,4},{8,9},{9,11},{11,1... | collective-permute-start | bytes 3145736 | tf_op jit(solution)/shard_map/ppermute | solution.py:266
  203.3 103.4 %copy-start.34 = (bf16[256,2048]{1,0:T(8,128)(2,1)}, bf16[256,2048]{1,0:T(8,128)(2,1)S(1)}, u32[]{:S(2)}) copy-start(bf16[256,2048]{1,0:T(8,128)(2,1)S(1)} %get-tuple-element.51) | copy-start | bytes 3145732
  203.3 47.3 %collective-permute-start.16 = (bf16[256,2048]{1,0:T(8,128)(2,1)S(1)}, bf16[256,2048]{1,0:T(8,128)(2,1)S(1)}, u32[]{:S(2)}, u32[]{:S(2)}) collective-permute-start(bf16[256,2048]{1,0:T(8,128)(2,1)S(1)} %get-tuple-element.51), channel_id=1, source_target_pairs={{0,1},{1,3},{3,2},{2,0},{4,5},{5,7},{7,6},{6,4},{8,9},{9,11},{11,1... | collective-permute-start | bytes 3145736 | tf_op jit(solution)/shard_map/ppermute | solution.py:266
  203.8 69.9 %collective-permute-start.15 = (bf16[256,2048]{1,0:T(8,128)(2,1)S(1)}, bf16[256,2048]{1,0:T(8,128)(2,1)S(1)}, u32[]{:S(2)}, u32[]{:S(2)}) collective-permute-start(bf16[256,2048]{1,0:T(8,128)(2,1)S(1)} %get-tuple-element.51), channel_id=1, source_target_pairs={{1,0},{3,1},{2,3},{0,2},{5,4},{7,5},{6,7},{4,6},{9,8},{11,9},{10,1... | collective-permute-start | bytes 3145736 | tf_op jit(solution)/shard_map/ppermute | solution.py:266
  206.2 90.7 %collective-permute-start.7 = (bf16[256,2048]{1,0:T(8,128)(2,1)S(1)}, bf16[256,2048]{1,0:T(8,128)(2,1)S(1)}, u32[]{:S(2)}, u32[]{:S(2)}) collective-permute-start(bf16[256,2048]{1,0:T(8,128)(2,1)S(1)} %get-tuple-element.58), channel_id=1, source_target_pairs={{1,0},{3,1},{2,3},{0,2},{5,4},{7,5},{6,7},{4,6},{9,8},{11,9},{10,1... | collective-permute-start | bytes 3145736 | tf_op jit(solution)/shard_map/ppermute | solution.py:266
  228.0 69.0 %copy-start.22 = (bf16[256,2048]{1,0:T(8,128)(2,1)}, bf16[256,2048]{1,0:T(8,128)(2,1)S(1)}, u32[]{:S(2)}) copy-start(bf16[256,2048]{1,0:T(8,128)(2,1)S(1)} %collective-permute-done.8) | copy-start | bytes 3145732
  228.1 78.6 %collective-permute-start.9 = (bf16[128,2048]{1,0:T(8,128)(2,1)S(1)}, bf16[128,2048]{1,0:T(8,128)(2,1)S(1)}, u32[]{:S(2)}, u32[]{:S(2)}) collective-permute-start(bf16[128,2048]{1,0:T(8,128)(2,1)S(1)} %slice.271), channel_id=1, source_target_pairs={{0,1},{1,3},{3,2},{2,0},{4,5},{5,7},{7,6},{6,4},{8,9},{9,11},{11,1... | collective-permute-start | bytes 1572872 | tf_op jit(solution)/shard_map/ppermute | solution.py:266
  250.6 134.2 %copy-start.17 = (bf16[256,2048]{1,0:T(8,128)(2,1)}, bf16[256,2048]{1,0:T(8,128)(2,1)S(1)}, u32[]{:S(2)}) copy-start(bf16[256,2048]{1,0:T(8,128)(2,1)S(1)} %collective-permute-done.16) | copy-start | bytes 3145732
  251.5 101.1 %collective-permute-start.17 = (bf16[128,2048]{1,0:T(8,128)(2,1)}, bf16[128,2048]{1,0:T(8,128)(2,1)}, u32[]{:S(2)}, u32[]{:S(2)}) collective-permute-start(bf16[128,2048]{1,0:T(8,128)(2,1)} %slice.279), channel_id=1, source_target_pairs={{0,1},{1,3},{3,2},{2,0},{4,5},{5,7},{7,6},{6,4},{8,9},{9,11},{11,1... | collective-permute-start | bytes 1572872 | tf_op jit(solution)/shard_map/ppermute | solution.py:266
  275.5 77.1 %collective-permute-start.18 = (bf16[128,2048]{1,0:T(8,128)(2,1)}, bf16[128,2048]{1,0:T(8,128)(2,1)}, u32[]{:S(2)}, u32[]{:S(2)}) collective-permute-start(bf16[128,2048]{1,0:T(8,128)(2,1)} %slice.280), channel_id=1, source_target_pairs={{1,0},{3,1},{2,3},{0,2},{5,4},{7,5},{6,7},{4,6},{9,8},{11,9},{10,1... | collective-permute-start | bytes 1572872 | tf_op jit(solution)/shard_map/ppermute | solution.py:266
  297.0 42.8 %collective-permute-start.10 = (bf16[128,2048]{1,0:T(8,128)(2,1)S(1)}, bf16[128,2048]{1,0:T(8,128)(2,1)S(1)}, u32[]{:S(2)}, u32[]{:S(2)}) collective-permute-start(bf16[128,2048]{1,0:T(8,128)(2,1)S(1)} %slice.272), channel_id=1, source_target_pairs={{1,0},{3,1},{2,3},{0,2},{5,4},{7,5},{6,7},{4,6},{9,8},{11,9},{10,1... | collective-permute-start | bytes 1572872 | tf_op jit(solution)/shard_map/ppermute | solution.py:266
  361.6 58.5 %collective-permute-start.11 = (bf16[128,2048]{1,0:T(8,128)(2,1)S(1)}, bf16[128,2048]{1,0:T(8,128)(2,1)S(1)}, u32[]{:S(2)}, u32[]{:S(2)}) collective-permute-start(bf16[128,2048]{1,0:T(8,128)(2,1)S(1)} %get-tuple-element.110), channel_id=1, source_target_pairs={{0,1},{1,3},{3,2},{2,0},{4,5},{5,7},{7,6},{6,4},{8,9},{9,11},{11,1... | collective-permute-start | bytes 1572872 | tf_op jit(solution)/shard_map/ppermute | solution.py:266
  363.5 56.4 %collective-permute-start.13 = (bf16[128,2048]{1,0:T(8,128)(2,1)S(1)}, bf16[128,2048]{1,0:T(8,128)(2,1)S(1)}, u32[]{:S(2)}, u32[]{:S(2)}) collective-permute-start(bf16[128,2048]{1,0:T(8,128)(2,1)S(1)} %get-tuple-element.111), channel_id=1, source_target_pairs={{1,0},{3,1},{2,3},{0,2},{5,4},{7,5},{6,7},{4,6},{9,8},{11,9},{10,1... | collective-permute-start | bytes 1572872 | tf_op jit(solution)/shard_map/ppermute | solution.py:266
  368.4 54.4 %collective-permute-start.19 = (bf16[128,2048]{1,0:T(8,128)(2,1)S(1)}, bf16[128,2048]{1,0:T(8,128)(2,1)S(1)}, u32[]{:S(2)}, u32[]{:S(2)}) collective-permute-start(bf16[128,2048]{1,0:T(8,128)(2,1)S(1)} %get-tuple-element.104), channel_id=1, source_target_pairs={{0,1},{1,3},{3,2},{2,0},{4,5},{5,7},{7,6},{6,4},{8,9},{9,11},{11,1... | collective-permute-start | bytes 1572872 | tf_op jit(solution)/shard_map/ppermute | solution.py:266
  369.4 54.5 %collective-permute-start.21 = (bf16[128,2048]{1,0:T(8,128)(2,1)S(1)}, bf16[128,2048]{1,0:T(8,128)(2,1)S(1)}, u32[]{:S(2)}, u32[]{:S(2)}) collective-permute-start(bf16[128,2048]{1,0:T(8,128)(2,1)S(1)} %get-tuple-element.105), channel_id=1, source_target_pairs={{1,0},{3,1},{2,3},{0,2},{5,4},{7,5},{6,7},{4,6},{9,8},{11,9},{10,1... | collective-permute-start | bytes 1572872 | tf_op jit(solution)/shard_map/ppermute | solution.py:266
  420.1 70.6 %collective-permute-start.14 = (bf16[256,2048]{1,0:T(8,128)(2,1)S(1)}, bf16[256,2048]{1,0:T(8,128)(2,1)S(1)}, u32[]{:S(2)}, u32[]{:S(2)}) collective-permute-start(bf16[256,2048]{1,0:T(8,128)(2,1)S(1)} %pad_maximum_fusion.3), channel_id=1, source_target_pairs={{1,0},{3,1},{2,3},{0,2},{5,4},{7,5},{6,7},{4,6},{9,8},{11,9},{10,1... | collective-permute-start | bytes 3145736 | tf_op jit(solution)/shard_map/ppermute | solution.py:266
  420.3 70.4 %collective-permute-start.12 = (bf16[256,2048]{1,0:T(8,128)(2,1)S(1)}, bf16[256,2048]{1,0:T(8,128)(2,1)S(1)}, u32[]{:S(2)}, u32[]{:S(2)}) collective-permute-start(bf16[256,2048]{1,0:T(8,128)(2,1)S(1)} %pad_maximum_fusion.2), channel_id=1, source_target_pairs={{0,1},{1,3},{3,2},{2,0},{4,5},{5,7},{7,6},{6,4},{8,9},{9,11},{11,1... | collective-permute-start | bytes 3145736 | tf_op jit(solution)/shard_map/ppermute | solution.py:266
  423.0 68.5 %collective-permute-start.20 = (bf16[256,2048]{1,0:T(8,128)(2,1)S(1)}, bf16[256,2048]{1,0:T(8,128)(2,1)S(1)}, u32[]{:S(2)}, u32[]{:S(2)}) collective-permute-start(bf16[256,2048]{1,0:T(8,128)(2,1)S(1)} %pad_maximum_fusion.4), channel_id=1, source_target_pairs={{0,1},{1,3},{3,2},{2,0},{4,5},{5,7},{7,6},{6,4},{8,9},{9,11},{11,1... | collective-permute-start | bytes 3145736 | tf_op jit(solution)/shard_map/ppermute | solution.py:266
  424.1 87.4 %collective-permute-start.22 = (bf16[256,2048]{1,0:T(8,128)(2,1)S(1)}, bf16[256,2048]{1,0:T(8,128)(2,1)S(1)}, u32[]{:S(2)}, u32[]{:S(2)}) collective-permute-start(bf16[256,2048]{1,0:T(8,128)(2,1)S(1)} %pad_maximum_fusion.5), channel_id=1, source_target_pairs={{1,0},{3,1},{2,3},{0,2},{5,4},{7,5},{6,7},{4,6},{9,8},{11,9},{10,1... | collective-permute-start | bytes 3145736 | tf_op jit(solution)/shard_map/ppermute | solution.py:266
  428.0 83.5 %copy-start.13 = (f32[256,2048]{1,0:T(8,128)S(1)}, f32[256,2048]{1,0:T(8,128)}, u32[]{:S(2)}) copy-start(f32[256,2048]{1,0:T(8,128)} %get-tuple-element.134) | copy-start | bytes 6291460
  526.1 133.3 %reduce-scatter.17.cloned.1.call-start = ((), (), s32[]{:S(2)}) async-start(), calls=%async_computation.19 | async-start | bytes 6488064 | tf_op jit(solution)/shard_map/reduce_scatter | solution.py:470
  545.7 143.1 %reduce-scatter.11.cloned.1.call-start = ((), (), s32[]{:S(2)}) async-start(), calls=%async_computation.14 | async-start | bytes 1310720 | tf_op jit(solution)/shard_map/reduce_scatter | solution.py:470
  553.4 22.3 %copy-start.3 = (f32[1024,512]{1,0:T(8,128)S(1)}, f32[1024,512]{1,0:T(8,128)}, u32[]{:S(2)}) copy-start(f32[1024,512]{1,0:T(8,128)} %copy-done.2) | copy-start | bytes 6291460
  553.4 22.3 %copy-start.5 = (f32[8,4,128,128]{3,2,1,0:T(8,128)S(1)}, f32[8,4,128,128]{3,2,1,0:T(8,128)}, u32[]{:S(2)}) copy-start(f32[8,4,128,128]{3,2,1,0:T(8,128)} %copy-done.4) | copy-start | bytes 6291460
  553.6 7.1 collective-permute-start.25
  553.6 22.0 %collective-permute-start.24 = (bf16[256,512]{1,0:T(8,128)(2,1)S(1)}, bf16[256,512]{1,0:T(8,128)(2,1)S(1)}, u32[]{:S(2)}, u32[]{:S(2)}) collective-permute-start(bf16[256,512]{1,0:T(8,128)(2,1)S(1)} %get-tuple-element.100), channel_id=1, source_target_pairs={{0,2},{1,3},{2,0},{3,1},{4,6},{5,7},{6,4},{7,5},{8,10},{9,11},{10,... | collective-permute-start | bytes 786440 | tf_op jit(solution)/shard_map/ppermute | solution.py:300
  555.3 20.3 %collective-permute-start.23 = (bf16[256,512]{1,0:T(8,128)(2,1)S(1)}, bf16[256,512]{1,0:T(8,128)(2,1)S(1)}, u32[]{:S(2)}, u32[]{:S(2)}) collective-permute-start(bf16[256,512]{1,0:T(8,128)(2,1)S(1)} %get-tuple-element.101), channel_id=1, source_target_pairs={{0,1},{1,2},{2,3},{3,0},{4,5},{5,6},{6,7},{7,4},{8,9},{9,10},{10,1... | collective-permute-start | bytes 786440 | tf_op jit(solution)/shard_map/ppermute | solution.py:300
  596.8 156.8 %reduce-scatter.7.cloned.1.call-start = ((), (), s32[]{:S(2)}) async-start(), calls=%async_computation.11 | async-start | bytes 7077888 | tf_op jit(solution)/shard_map/reduce_scatter | solution.py:470
  610.1 206.5 %reduce-scatter.13.cloned.1.call-start = ((), (), s32[]{:S(2)}) async-start(), calls=%async_computation.16 | async-start | bytes 6488064 | tf_op jit(solution)/shard_map/reduce_scatter | solution.py:470
  621.8 258.2 %reduce-scatter.15.cloned.1.call-start = ((), (), s32[]{:S(2)}) async-start(), calls=%async_computation.17 | async-start | bytes 6488064 | tf_op jit(solution)/shard_map/reduce_scatter | solution.py:470
  634.2 363.5 %all-gather.26.cloned.1.call-start = ((), (), s32[]{:S(2)}) async-start(), calls=%async_computation.20 | async-start | bytes 6488064 | tf_op jit(solution)/shard_map/all_gather | solution.py:499
  665.0 332.7 %all-gather.22.cloned.1.call-start = ((), (), s32[]{:S(2)}) async-start(), calls=%async_computation.15 | async-start | bytes 2359296 | tf_op jit(solution)/shard_map/all_gather | solution.py:499
  691.7 312.1 %all-gather.20.cloned.1.call-start = ((), (), s32[]{:S(2)}) async-start(), calls=%async_computation.12 | async-start | bytes 7077888 | tf_op jit(solution)/shard_map/all_gather | solution.py:499
  759.8 313.8 %all-gather.24.cloned.1.call-start = ((), (), s32[]{:S(2)}) async-start(), calls=%async_computation.18 | async-start | bytes 12976128 | tf_op jit(solution)/shard_map/all_gather | solution.py:499
  898.0 27.7 %collective-permute-start.26 = (bf16[128,2048]{1,0:T(8,128)(2,1)S(1)}, bf16[128,2048]{1,0:T(8,128)(2,1)S(1)}, u32[]{:S(2)}, u32[]{:S(2)}) collective-permute-start(bf16[128,2048]{1,0:T(8,128)(2,1)S(1)} %get-tuple-element.94), channel_id=1, source_target_pairs={{0,1},{1,3},{3,2},{2,0},{4,5},{5,7},{7,6},{6,4},{8,9},{9,11},{11,1... | collective-permute-start | bytes 1572872 | tf_op jit(solution)/shard_map/ppermute | solution.py:266
  899.5 24.3 %collective-permute-start.28 = (bf16[128,2048]{1,0:T(8,128)(2,1)S(1)}, bf16[128,2048]{1,0:T(8,128)(2,1)S(1)}, u32[]{:S(2)}, u32[]{:S(2)}) collective-permute-start(bf16[128,2048]{1,0:T(8,128)(2,1)S(1)} %get-tuple-element.95), channel_id=1, source_target_pairs={{1,0},{3,1},{2,3},{0,2},{5,4},{7,5},{6,7},{4,6},{9,8},{11,9},{10,1... | collective-permute-start | bytes 1572872 | tf_op jit(solution)/shard_map/ppermute | solution.py:266
  924.0 26.5 %collective-permute-start.29 = (bf16[256,2048]{1,0:T(8,128)(2,1)S(1)}, bf16[256,2048]{1,0:T(8,128)(2,1)S(1)}, u32[]{:S(2)}, u32[]{:S(2)}) collective-permute-start(bf16[256,2048]{1,0:T(8,128)(2,1)S(1)} %pad_maximum_fusion.8), channel_id=1, source_target_pairs={{1,0},{3,1},{2,3},{0,2},{5,4},{7,5},{6,7},{4,6},{9,8},{11,9},{10,1... | collective-permute-start | bytes 3145736 | tf_op jit(solution)/shard_map/ppermute | solution.py:266
  925.9 46.5 %collective-permute-start.27 = (bf16[256,2048]{1,0:T(8,128)(2,1)S(1)}, bf16[256,2048]{1,0:T(8,128)(2,1)S(1)}, u32[]{:S(2)}, u32[]{:S(2)}) collective-permute-start(bf16[256,2048]{1,0:T(8,128)(2,1)S(1)} %pad_maximum_fusion.7), channel_id=1, source_target_pairs={{0,1},{1,3},{3,2},{2,0},{4,5},{5,7},{7,6},{6,4},{8,9},{9,11},{11,1... | collective-permute-start | bytes 3145736 | tf_op jit(solution)/shard_map/ppermute | solution.py:266
  927.2 45.2 %copy-start.10 = (bf16[256,2048]{1,0:T(8,128)(2,1)S(1)}, bf16[256,2048]{1,0:T(8,128)(2,1)}, u32[]{:S(2)}) copy-start(bf16[256,2048]{1,0:T(8,128)(2,1)} %param.19) | copy-start | bytes 3145732
  927.2 45.2 %copy-start.41 = (f32[1,2048]{1,0:T(1,128)S(1)}, f32[1,2048]{1,0:T(1,128)}, u32[]{:S(2)}) copy-start(f32[1,2048]{1,0:T(1,128)} %copy-done.40) | copy-start | bytes 24580
  927.2 45.2 %copy-start.46 = (f32[256]{0:T(256)S(1)}, f32[256]{0:T(256)}, u32[]{:S(2)}) copy-start(f32[256]{0:T(256)} %copy-done.45) | copy-start | bytes 3076
  928.0 54.2 %copy-start.50 = (s32[8]{0:T(128)S(1)}, s32[8]{0:T(128)}, u32[]{:S(2)}) copy-start(s32[8]{0:T(128)} %param.21) | copy-start | bytes 100
  928.0 62.2 %copy-start.47 = (f32[256]{0:T(256)S(1)}, f32[256]{0:T(256)}, u32[]{:S(2)}) copy-start(f32[256]{0:T(256)} %get-tuple-element.130) | copy-start | bytes 3076
  950.5 24.5 %copy-start.32 = (bf16[256,2048]{1,0:T(8,128)(2,1)}, bf16[256,2048]{1,0:T(8,128)(2,1)S(1)}, u32[]{:S(2)}) copy-start(bf16[256,2048]{1,0:T(8,128)(2,1)S(1)} %collective-permute-done.29) | copy-start | bytes 3145732
  975.1 1.3 collective-permute-start.30
  976.4 4.3 collective-permute-start.31
  980.8 4.9 collective-permute-start.32
  985.7 4.3 collective-permute-start.33
  990.0 5.9 collective-permute-start.34
  997.0 83.1 %copy-start.39 = (f32[4,2048]{1,0:T(4,128)}, f32[4,2048]{1,0:T(4,128)S(1)}, u32[]{:S(2)}) copy-start(f32[4,2048]{1,0:T(4,128)S(1)} %get-tuple-element.167) | copy-start | bytes 98308
  (60 other events, 284.5 us)
Sparse Core Ops, SparseCore 0:
  10.2 30.6 all-gather.11
  43.3 45.0 all-gather.9
  90.3 55.9 all-gather.13
  148.6 67.7 all-gather.15
  218.6 44.3 all-gather.17
  526.2 70.2 reduce-scatter.8
  600.3 58.9 reduce-scatter.16
  661.6 27.1 reduce-scatter.10
  693.1 60.4 reduce-scatter.6
  757.5 59.0 reduce-scatter.12
  821.0 59.0 reduce-scatter.14
  881.8 44.3 all-gather.25
  928.0 28.1 all-gather.21
  958.0 45.7 all-gather.19
  1006.1 67.4 all-gather.23

commit v2 on v1

v2 whole, which is shorter than its diff:
```python
import functools

import jax
import jax.numpy as jnp
import numpy as np
from jax import lax
from jax.experimental import pallas as pl
from jax.experimental.pallas import tpu as pltpu
from jax.sharding import PartitionSpec as P

HEAD = 128
STEP = 10
CHUNK = 128

EPS = 1e-06
BETA_ONE = 0.9
BETA_TWO = 0.95
DECAY = 0.1
ADAM_EPS = 1e-08
LEARN_RATE = 0.005

NN = ((1,), (0,))
NT = ((1,), (1,))
TN = ((0,), (0,))


def bf16(value):
    return value.astype(jnp.bfloat16)


def f32(value):
    return value.astype(jnp.float32)


def dot(left, right, dims=NN):
    return lax.dot_general(left, right, (dims, ((), ())), preferred_element_type=jnp.float32)


def dot_low(left, right, dims):
    return dot(bf16(left), bf16(right), dims)


def dot_high(left, right, dims):
    left_top, right_top = bf16(left), bf16(right)
    left_rest = bf16(left - f32(left_top))
    right_rest = bf16(right - f32(right_top))
    return (
        dot(left_top, right_top, dims)
        + dot(left_top, right_rest, dims)
        + dot(left_rest, right_top, dims)
    )


def masked_sum(mask, rows, dims):
    top = bf16(rows)
    return dot(mask, top, dims) + dot(mask, bf16(rows - f32(top)), dims)


def gates(forget_raw, lower, keep):
    sigma = jax.nn.sigmoid(forget_raw)
    forget = lower + (1.0 - lower) * sigma
    return sigma, forget, keep * jnp.log(forget), keep * (1.0 - forget)


def causal_mask(rows):
    later = lax.broadcasted_iota(jnp.int32, (rows, rows), 0)
    return later >= lax.broadcasted_iota(jnp.int32, (rows, rows), 1)


def keep_rows(block, rows, length):
    pos = block * rows + lax.broadcasted_iota(jnp.int32, (rows, 1), 0)
    return (pos < length).astype(jnp.float32)


def forward_kernel(count, length, slot, part, core_at, *refs):
    parts, refs = refs[:count], refs[-7:]
    low, gain, core, rec_out, state_out, proj, carry = refs
    step = pl.program_id(0)
    rows, channels = core.shape

    @pl.when(step == 0)
    def _():
        carry[...] = jnp.zeros_like(carry)

    for index in range(count):

        @pl.when(slot[step] == index)
        def _(index=index):
            proj[...] = parts[index][...]

    keep = keep_rows(step, rows, length[0])
    causal = causal_mask(rows)
    ones = causal.astype(jnp.bfloat16)
    for head in range(channels // HEAD):
        cut = pl.ds(head * HEAD, HEAD)
        query_raw = proj[:, cut]
        value = proj[:, pl.ds(2 * channels + head * HEAD, HEAD)]
        lower = low[:, cut]
        forget_raw = proj[:, pl.ds(channels + head * HEAD, HEAD)]
        _, _, logf, key = gates(forget_raw, lower, keep)
        query = query_raw * jax.nn.sigmoid(query_raw)
        run = masked_sum(ones, logf, NN)
        last = run[rows - 1 :, :]
        query_up = query * jnp.exp(run)
        key_down = key * jnp.exp(-run)
        key_tail = key * jnp.exp(last - run)
        state = carry[head]
        state_out[0, head] = state
        scores = jnp.where(causal, dot_low(query_up, key_down, NT), 0.0)
        rec = dot_low(query_up, state, NT) + dot_low(scores, value, NN)
        carry[head] = state * jnp.exp(last) + dot_low(value, key_tail, TN)
        rec_out[:, cut] = rec
        scale = lax.rsqrt(jnp.mean(rec * rec, axis=-1, keepdims=True) + EPS)
        core[:, cut] = bf16(rec * scale * gain[:, cut])


def part_spec(index, wide, last):
    return pl.BlockSpec((CHUNK, wide), lambda i, n, slot, part, *_: (part[index * (last + 1) + i], 0))


def recurrence_forward(length, slot, part, core_at, parts, lower, gain, needed):
    wide = parts[0].shape[1]
    total = len(parts) * parts[0].shape[0]
    channels = wide // 3
    heads = channels // HEAD
    steps = total // CHUNK
    return pl.pallas_call(
        functools.partial(forward_kernel, len(parts)),
        grid_spec=pltpu.PrefetchScalarGridSpec(
            num_scalar_prefetch=4,
            grid=(steps,),
            in_specs=[
                *(part_spec(index, wide, steps - 1) for index in range(len(parts))),
                *(pl.BlockSpec(memory_space=pl.ANY) for _ in needed),
                pl.BlockSpec((1, channels), lambda i, *_: (0, 0)),
                pl.BlockSpec((1, channels), lambda i, *_: (0, 0)),
            ],
            out_specs=[
                pl.BlockSpec((CHUNK, channels), lambda i, n, slot, part, at: (at[i], 0)),
                pl.BlockSpec((CHUNK, channels), lambda i, *_: (i, 0)),
                pl.BlockSpec((1, heads, HEAD, HEAD), lambda i, *_: (i, 0, 0, 0)),
            ],
            scratch_shapes=[
                pltpu.VMEM((CHUNK, wide), jnp.float32),
                pltpu.VMEM((heads, HEAD, HEAD), jnp.float32),
            ],
        ),
        out_shape=[
            jax.ShapeDtypeStruct((total, channels), jnp.bfloat16),
            jax.ShapeDtypeStruct((total, channels), jnp.float32),
            jax.ShapeDtypeStruct((steps, heads, HEAD, HEAD), jnp.float32),
        ],
        compiler_params=pltpu.CompilerParams(vmem_limit_bytes=32 * 1024 * 1024),
        cost_estimate=pl.CostEstimate(
            flops=12 * total * channels * HEAD,
            bytes_accessed=total * channels * 18,
            transcendentals=6 * total * channels,
        ),
        name="recurrence_forward",
    )(length, slot, part, core_at, *parts, *needed, lower, gain)


def backward_kernel(count, length, slot, part, place, slot_core, part_core, *refs):
    parts, gcores, refs = refs[:count], refs[count : 2 * count], refs[-10:]
    low, gain, rec_in, state_in, grad, sums, proj, gcore_in, carry, ends = refs
    step = pl.program_id(0)
    rows, channels = rec_in.shape

    for index in range(count):

        @pl.when(slot[pl.num_programs(0) - 1 - step] == index)
        def _(index=index):
            proj[...] = parts[index][...]

        @pl.when(slot_core[pl.num_programs(0) - 1 - step] == index)
        def _(index=index):
            gcore_in[...] = f32(gcores[index][...])

    @pl.when(step == 0)
    def _():
        carry[...] = jnp.zeros_like(carry)
        ends[...] = jnp.zeros_like(ends)
        sums[...] = jnp.zeros_like(sums)

    keep = keep_rows(pl.num_programs(0) - 1 - step, rows, length[0])
    causal = causal_mask(rows)
    ones = causal.astype(jnp.bfloat16)
    for head in range(channels // HEAD):
        cut = pl.ds(head * HEAD, HEAD)
        cut_forget = pl.ds(channels + head * HEAD, HEAD)
        cut_value = pl.ds(2 * channels + head * HEAD, HEAD)
        query_raw = proj[:, cut]
        value = proj[:, cut_value]
        lower = low[:, cut]
        sigma, forget, logf, key = gates(proj[:, cut_forget], lower, keep)
        sig_query = jax.nn.sigmoid(query_raw)
        query = query_raw * sig_query
        run = masked_sum(ones, logf, NN)
        last = run[rows - 1 :, :]
        up = jnp.exp(run)
        down = jnp.exp(-run)
        tail = jnp.exp(last - run)
        query_up = query * up
        key_down = key * down
        key_tail = key * tail
        rec = rec_in[:, cut]
        gcore = gcore_in[:, cut]
        scale = lax.rsqrt(jnp.mean(rec * rec, axis=-1, keepdims=True) + EPS)
        normed = rec * scale
        weighted = gcore * gain[:, cut]
        grec = scale * (weighted - normed * jnp.mean(normed * weighted, axis=-1, keepdims=True))
        state = state_in[0, head]
        after = carry[head]
        scores = jnp.where(causal, dot_low(query_up, key_down, NT), 0.0)
        gscores = jnp.where(causal, dot_high(grec, value, NT), 0.0)
        gquery_up = dot_high(grec, state, NN) + dot_high(gscores, key_down, NN)
        gkey_down = dot_high(gscores, query_up, TN)
        gkey_tail = dot_high(value, after, NN)
        gvalue = dot_low(scores, grec, TN) + dot_low(key_tail, after, NT)
        carry[head] = after * jnp.exp(last) + dot_low(grec, query_up, TN)
        gquery = gquery_up * up
        gkey = gkey_down * down + gkey_tail * tail
        end = jnp.sum(ends[head] * after, axis=0, keepdims=True)
        ends[head] = state
        glogf = masked_sum(ones, query * gquery - key * gkey, TN) + end
        gforget = keep * (glogf / forget - gkey)
        rising = 1.0 - sigma
        grad[:, cut] = bf16(gquery * sig_query * (1.0 + query_raw * (1.0 - sig_query)))
        grad[:, cut_forget] = bf16(gforget * (1.0 - lower) * sigma * rising)
        grad[:, cut_value] = bf16(gvalue)
        sums[0:1, cut] += jnp.sum(gcore * normed, axis=0, keepdims=True)
        sums[1:2, cut] += jnp.sum(gforget * rising, axis=0, keepdims=True)


def recurrence_backward(length, tables, parts, gcores, lower, gain, rec, states, needed):
    wide = parts[0].shape[1]
    total = len(parts) * parts[0].shape[0]
    channels = wide // 3
    heads = channels // HEAD
    steps = total // CHUNK
    end = steps - 1

    def proj_spec(index):
        return pl.BlockSpec(
            (CHUNK, wide), lambda i, n, slot, part, *_: (part[index * steps + end - i], 0)
        )

    def core_spec(index):
        return pl.BlockSpec(
            (CHUNK, channels),
            lambda i, n, slot, part, place, sc, pc: (pc[index * steps + end - i], 0),
        )

    return pl.pallas_call(
        functools.partial(backward_kernel, len(parts)),
        grid_spec=pltpu.PrefetchScalarGridSpec(
            num_scalar_prefetch=6,
            grid=(steps,),
            in_specs=[
                *(proj_spec(index) for index in range(len(parts))),
                *(core_spec(index) for index in range(len(parts))),
                *(pl.BlockSpec(memory_space=pl.ANY) for _ in needed),
                pl.BlockSpec((1, channels), lambda i, *_: (0, 0)),
                pl.BlockSpec((1, channels), lambda i, *_: (0, 0)),
                pl.BlockSpec((CHUNK, channels), lambda i, *_: (end - i, 0)),
                pl.BlockSpec((1, heads, HEAD, HEAD), lambda i, *_: (end - i, 0, 0, 0)),
            ],
            out_specs=[
                pl.BlockSpec((CHUNK, wide), lambda i, n, slot, part, place, *_: (place[end - i], 0)),
                pl.BlockSpec((8, channels), lambda i, *_: (0, 0)),
            ],
            scratch_shapes=[
                pltpu.VMEM((CHUNK, wide), jnp.float32),
                pltpu.VMEM((CHUNK, channels), jnp.float32),
                pltpu.VMEM((heads, HEAD, HEAD), jnp.float32),
                pltpu.VMEM((heads, HEAD, HEAD), jnp.float32),
            ],
        ),
        out_shape=[
            jax.ShapeDtypeStruct((total, wide), jnp.bfloat16),
            jax.ShapeDtypeStruct((8, channels), jnp.float32),
        ],
        compiler_params=pltpu.CompilerParams(vmem_limit_bytes=32 * 1024 * 1024),
        cost_estimate=pl.CostEstimate(
            flops=40 * total * channels * HEAD,
            bytes_accessed=total * channels * 26,
            transcendentals=8 * total * channels,
        ),
        name="recurrence_backward",
    )(length, *tables, *parts, *gcores, *needed, lower, gain, rec, states)


class Ring:
    def __init__(self, axis):
        size = lax.axis_size(axis)
        ring = [0, *range(1, size, 2), *range(size - 2, 0, -2)]
        self.axis, self.size = axis, size
        self.ahead = [(ring[i], ring[(i + 1) % size]) for i in range(size)]
        self.owner_of_slot = np.zeros((size, size), np.int32)
        for at, me in enumerate(ring):
            self.owner_of_slot[me] = [ring[at - slot] for slot in range(size)]

    def send(self, value):
        return lax.ppermute(value, self.axis, self.ahead)

    def gather(self, own, held=lambda slots: ()):
        slots = [own]
        for _ in range(1, self.size):
            got = self.send(slots[-1])
            slots.append(after(got, *held(slots)))
        return slots

    def scatter(self, parts):
        total = self.send(parts[1])
        for step in range(2, self.size):
            needed = (yield total) or ()
            total = self.send(bf16(f32(after(parts[step], *needed)) + f32(total)))
        needed = (yield total) or ()
        yield f32(after(parts[0], *needed)) + f32(total)


def flip(value, axis, bit):
    return lax.ppermute(value, axis, [(i, i ^ (1 << bit)) for i in range(lax.axis_size(axis))])


class Halving:
    def __init__(self, value, axis, order):
        size = lax.axis_size(axis)
        bits = size.bit_length() - 1
        self.axis, self.order, self.left = axis, list(order), list(range(bits - 1, -1, -1))
        self.value = value.reshape((2,) * bits + (value.shape[0] // size, value.shape[1]))

    def step(self, *needed):
        bit = self.order.pop(0)
        at, mine = self.left.index(bit), (lax.axis_index(self.axis) >> bit) & 1
        sent = lax.dynamic_index_in_dim(self.value, 1 - mine, at, keepdims=False)
        kept = lax.dynamic_index_in_dim(self.value, mine, at, keepdims=False)
        got = flip(after(sent, *needed), self.axis, bit)
        self.left.pop(at)
        total = f32(kept) + f32(got)
        self.value = bf16(total) if self.order else total
        return got


class HalvingColumns:
    def __init__(self, value, axis, order):
        self.axis, self.order, self.value = axis, list(order), value

    def step(self, *needed):
        bit, half = self.order.pop(0), self.value.shape[1] // 2
        got = flip(after(self.value[:, half:], *needed), self.axis, bit)
        total = f32(self.value[:, :half]) + f32(got)
        self.value = bf16(total) if self.order else total
        return got


def after(value, *needed):
    return lax.optimization_barrier((value, needed))[0] if needed else value


def behind(value, mark):
    return jnp.where(mark > 3.0e38, mark, value)


def permute_kernel(blocks, order, value, out):
    block = value.shape[1] // blocks
    for i in range(blocks):
        cut = pl.ds(pl.multiple_of(order[i] * block, block), block)
        out[:, pl.ds(i * block, block)] = value[:, cut]


def permute_columns(value, order):
    blocks = order.shape[0]
    whole = pl.BlockSpec(value.shape, lambda i, *_: (0, 0))
    return pl.pallas_call(
        functools.partial(permute_kernel, blocks),
        grid_spec=pltpu.PrefetchScalarGridSpec(
            num_scalar_prefetch=1, grid=(1,), in_specs=[whole], out_specs=whole
        ),
        out_shape=jax.ShapeDtypeStruct(value.shape, value.dtype),
        name="permute_columns",
    )(order, value)


def column_order(axis, order):
    size, me = lax.axis_size(axis), lax.axis_index(axis)
    bits = size.bit_length() - 1
    offsets = [
        sum(((at >> (bits - 1 - i)) & 1) << bit for i, bit in enumerate(order)) for at in range(size)
    ]
    return jnp.asarray(np.array(offsets, np.int32)) ^ me.astype(jnp.int32)


def bit_orders(axis):
    upper = list(range(1, lax.axis_size(axis).bit_length() - 1))
    return [0, *upper], [0, *upper[::-1]]


def sum_all(value, axes):
    for axis in axes:
        for bit in range(lax.axis_size(axis).bit_length() - 1):
            value = value + flip(value, axis, bit)
    return value


def copy_kernel(value, out):
    out[...] = value[...]


def copied(value):
    outer, rows, width = value.shape
    spec = pl.BlockSpec((1, rows // 4, width), lambda i, j: (i, j, 0))
    return pl.pallas_call(
        copy_kernel,
        grid=(outer, 4),
        in_specs=[spec],
        out_specs=spec,
        out_shape=jax.ShapeDtypeStruct(value.shape, value.dtype),
        name="copied",
    )(value)


def by_slot(value, size):
    rows = value.shape[0] // size
    return [value[slot * rows : (slot + 1) * rows] for slot in range(size)]


def norm_back(value, scale, gain, grad):
    inner = jnp.mean(value * gain * grad, axis=-1, keepdims=True)
    return scale * gain * grad - value * (scale * scale * scale) * inner


def inverse_rms(value):
    return lax.rsqrt(jnp.mean(value * value, axis=-1, keepdims=True) + EPS)


def moments(first, second, grad):
    first = BETA_ONE * first + (1.0 - BETA_ONE) * grad
    second = BETA_TWO * second + (1.0 - BETA_TWO) * grad * grad
    return (first, second)


def adamw(param, first, second, grad):
    first, second = moments(first, second, grad)
    fix_one = 1.0 - BETA_ONE**STEP
    fix_two = 1.0 - BETA_TWO**STEP
    update = first / fix_one / (jnp.sqrt(second / fix_two) + ADAM_EPS) + DECAY * param
    return (param - LEARN_RATE * update, first, second)


def body(
    block_input,
    cotangent,
    lengths,
    vectors,
    vectors_first,
    vectors_second,
    mixer_in,
    mixer_in_first,
    mixer_in_second,
    mixer_out,
    mixer_out_first,
    mixer_out_second,
    ffn_in,
    ffn_in_first,
    ffn_in_second,
    ffn_out,
    ffn_out_first,
    ffn_out_second,
):
    own_rows, width = block_input.shape
    group = lax.axis_index("dp")
    member = lax.axis_index("mp")
    members = lax.axis_size("mp")
    ring = Ring("mp")
    length = lax.dynamic_index_in_dim(lengths, group, 0, keepdims=True)
    own_pos = member * own_rows + jnp.arange(own_rows, dtype=jnp.int32)
    keep = f32(own_pos < length[0])[:, None]
    channels = mixer_in.shape[2]
    channel_start = member * channels
    group_gain = lax.dynamic_slice_in_dim(vectors[1:2], channel_start, channels, 1)
    lower = lax.dynamic_slice_in_dim(vectors[2:3], channel_start, channels, 1)

    per = own_rows // CHUNK
    blocks = jnp.arange(members * per, dtype=jnp.int32)
    owner_of_slot = jnp.asarray(ring.owner_of_slot)[member]
    slot = jnp.asarray(np.argsort(ring.owner_of_slot, 1).astype(np.int32))[member][blocks // per]
    part = jnp.clip(blocks[None, :] - owner_of_slot[:, None] * per, 0, per - 1).reshape(-1)
    place = slot * per + blocks % per

    in_shard = jnp.concatenate([bf16(mixer_in[j]) for j in range(3)], 1)
    half_in = 3 * channels // 2
    halves_in = (slice(0, half_in), slice(half_in, None))
    order_one, order_two = bit_orders("dp")
    inputs = f32(block_input)
    scale_one = inverse_rms(inputs)
    own_one = bf16(inputs * scale_one * vectors[0])
    weight_in = lax.all_gather(in_shard, "dp", axis=0, tiled=True)
    order_out = column_order("dp", order_one)
    weight_out = lax.all_gather(bf16(mixer_out), "dp", axis=1, tiled=True)
    weight_gate_up = lax.all_gather(bf16(ffn_in), "dp", axis=1, tiled=True)
    weight_down = lax.all_gather(bf16(ffn_out), "dp", axis=1, tiled=True)
    proj = []

    def project(slots):
        if len(slots) > 2:
            proj.append(dot(slots[len(proj)], weight_in))
        return proj[-1:]

    normed_one = ring.gather(own_one, project)
    while len(proj) < members:
        project(normed_one)

    grad_total = f32(cotangent) * keep
    grad_rows = ring.gather(after(bf16(grad_total), normed_one[-1]))
    core, rec, states = recurrence_forward(length, slot, part, place, proj, lower, group_gain, ())
    mix_parts = by_slot(bf16(dot(core, weight_out)), members)
    mix_parts[1] = after(mix_parts[1], grad_rows[1])
    steps = ring.scatter(mix_parts)
    for _ in range(members - 1):
        next(steps)
    mix = next(steps)
    resid = inputs + mix
    scale_two = inverse_rms(resid)

    hidden, grad_gate, grad_up, two_parts = [], [], [], []

    def feed(slots):
        rows, grows = slots[-1], grad_rows[len(slots) - 1]
        gate, up = dot(rows, weight_gate_up[0]), dot(rows, weight_gate_up[1])
        sigma = jax.nn.sigmoid(gate)
        act = gate * sigma
        hidden.append(bf16(act * up))
        ghid = dot(grows, weight_down, NT)
        grad_gate.append(bf16(ghid * up * sigma * (1.0 + gate * (1.0 - sigma))))
        grad_up.append(bf16(ghid * act))
        two_parts.append(
            bf16(
                dot(grad_gate[-1], weight_gate_up[0], NT) + dot(grad_up[-1], weight_gate_up[1], NT)
            )
        )
        return two_parts[-1:]

    normed_two = ring.gather(bf16(resid * scale_two * vectors[3]), feed)
    steps = ring.scatter(two_parts)
    normed_two[-1] = after(normed_two[-1], next(steps))
    feed(normed_two)
    for _ in range(members - 4):
        steps.send(())
    came = steps.send(())
    normed_two_all = jnp.concatenate(normed_two, 0)
    sum_gate_up = jnp.stack(
        [
            bf16(dot(normed_two_all, after(jnp.concatenate(part, 0), *two_parts), TN))
            for part in (grad_gate, grad_up)
        ]
    )
    shard_gate_up = lax.psum_scatter(sum_gate_up, "dp", scatter_dimension=1, tiled=True)
    hidden_all = after(jnp.concatenate(hidden, 0), came)
    sum_down = bf16(dot(hidden_all, jnp.concatenate(grad_rows, 0), TN))
    shard_down = lax.psum_scatter(sum_down, "dp", scatter_dimension=1, tiled=True)
    ffn_parts = by_slot(bf16(dot(hidden_all, weight_down)), members)
    steps.send(())
    grad_two = steps.send((sum_gate_up,))

    grad_resid = grad_total + norm_back(resid, scale_two, vectors[3], grad_two)
    gain_two = jnp.sum(grad_two * resid * scale_two, axis=0)

    weight_out = permute_columns(weight_out, order_out)
    grad_core = []

    def pull(slots):
        grad_core.append(bf16(dot(slots[-1], weight_out, NT)))
        return [*grad_core[-1:], *ffn_parts[: len(slots) // 2]]

    grad_mix = ring.gather(permute_columns(bf16(grad_resid), order_out), pull)
    grad_core.append(bf16(dot(grad_mix[-1], weight_out, NT)))
    grad_proj, sums = recurrence_backward(
        length,
        (slot, part, place, slot, part),
        proj,
        grad_core,
        lower,
        group_gain,
        rec,
        states,
        (),
    )
    sum_out = bf16(dot(core, jnp.concatenate(grad_mix, 0), TN))
    out_sum = HalvingColumns(sum_out, "dp", order_one)
    shard_gate_up = behind(f32(shard_gate_up), sums[0, 0])
    gu_new, gu_first, gu_second = adamw(ffn_in, ffn_in_first, ffn_in_second, shard_gate_up)
    gu_sent = bf16(gu_new)

    ffn_parts[1] = after(ffn_parts[1], grad_mix[-1])
    steps = ring.scatter(ffn_parts)
    one = next(steps)
    done = [out_sum.step(grad_mix[-1])]

    two = steps.send((grad_proj, *done))
    grad_proj = after(grad_proj, one)
    normed_one_all = jnp.concatenate(normed_one, 0)
    sum_in = [bf16(dot(normed_one_all, grad_proj[:, cut], TN)) for cut in halves_in]
    in_sums = [Halving(piece, "dp", order) for piece, order in zip(sum_in, (order_one, order_two))]
    done = [out_sum.step(one), *(item.step() for item in in_sums)]

    shard_down = behind(f32(shard_down), sums[0, 0])
    down_new, down_first, down_second = adamw(ffn_out, ffn_out_first, ffn_out_second, shard_down)
    down_sent = bf16(down_new)

    three = steps.send((*sum_in, gu_sent))
    grad_proj = after(grad_proj, two)
    one_parts = by_slot(bf16(dot(grad_proj, weight_in, NT)), members)
    done += [item.step(two) for item in in_sums]
    while out_sum.order:
        done.append(out_sum.step(two))
    for _ in range(members - 4):
        three = steps.send(())
    ffn = steps.send((*one_parts, *done, down_sent))
    total = resid + ffn
    one_parts[1] = after(one_parts[1], ffn)

    steps = ring.scatter(one_parts)
    one = next(steps)
    while in_sums[0].order:
        done = [item.step(three) for item in in_sums]
    shard_out = after(out_sum.value, three)
    out_new, out_first, out_second = adamw(mixer_out, mixer_out_first, mixer_out_second, shard_out)
    out_sent = bf16(out_new)
    gain_one = sum(
        jnp.sum(f32(weight_in[:, cut]) * f32(piece), axis=1)
        for cut, piece in zip(halves_in, after(sum_in, three))
    )
    blank = jnp.zeros((width,), jnp.float32)
    squares = jnp.stack([jnp.sum(keep * piece * piece) for piece in (total, mix, ffn)])
    vector_part = jnp.stack(
        [
            gain_one / vectors[0],
            lax.dynamic_update_slice_in_dim(blank, sums[0], channel_start, 0),
            lax.dynamic_update_slice_in_dim(blank, sums[1], channel_start, 0),
            gain_two,
            lax.dynamic_update_slice_in_dim(blank, squares, 0, 0),
        ]
    )


    two = steps.send((vector_part, out_sent, *done))
    shard_in = jnp.concatenate([after(item.value, one) for item in in_sums], 1)
    shard_in = jnp.stack([shard_in[:, j * channels : (j + 1) * channels] for j in range(3)])
    in_new, in_first, in_second = adamw(mixer_in, mixer_in_first, mixer_in_second, shard_in)
    in_sent = bf16(in_new)
    vector_sums = sum_all(after(vector_part, one), ("dp",))

    gu_low = copied(lax.all_gather(gu_sent, "dp", axis=1, tiled=True))
    one_parts[-1] = behind(one_parts[-1], gu_low[0, 0, 0])
    three = steps.send((in_sent, vector_sums))
    for _ in range(members - 4):
        three = steps.send(())
    grad_one = steps.send(())
    vector_sums = sum_all(after(vector_sums, three), ("mp",))
    input_grad = grad_resid + norm_back(inputs, scale_one, vectors[0], grad_one)
    vectors_grad = vector_sums[:4]
    denom = f32(jnp.sum(lengths)) * width
    stats = jnp.sqrt(vector_sums[4, :3] / denom)
    vec_first, vec_second = moments(vectors_first, vectors_second, vectors_grad)

    down_low, out_low, in_low = (
        lax.all_gather(new, "dp", axis=1, tiled=True) for new in (down_sent, out_sent, in_sent)
    )
    return (
        bf16(total),
        input_grad,
        stats,
        vectors_grad,
        vec_first,
        vec_second,
        shard_in,
        in_new,
        in_first,
        in_second,
        in_low,
        shard_out,
        out_new,
        out_first,
        out_second,
        out_low,
        shard_gate_up,
        gu_new,
        gu_first,
        gu_second,
        gu_low,
        shard_down,
        down_new,
        down_first,
        down_second,
        down_low,
    )


def solution(mesh):
    rows = P(("dp", "mp"), None)
    deep = P(None, "dp", "mp")
    flat = P("mp", "dp")
    in_specs = (
        (rows, rows, P(), P(), P(), P()) + (deep,) * 3 + (flat,) * 3 + (deep,) * 3 + (flat,) * 3
    )
    wide = (deep,) * 4 + (P(None, None, "mp"),)
    tall = (flat,) * 4 + (P("mp", None),)
    out_specs = (rows, rows, P(), P(), P(), P()) + wide + tall + wide + tall
    return jax.shard_map(body, mesh=mesh, in_specs=in_specs, out_specs=out_specs, check_vma=False)
```

time: 1110 us -> 788 us (0.71)
  waiting for transfers between devices: 705 us -> 368 us
  other arithmetic: 71 us -> 98.9 us
  Pallas kernels: 29.7 us -> 49.3 us
  local copies, waits for them, and re-layouts: 54.3 us -> 36.9 us
  matrix products: 179 us -> 163 us
    reduce_scatter x6 -> x2, waiting for transfers between devices: 231 us -> 22.4 us  [the longest x1 22.4 us: body(): lax.psum_scatter(sum_down, 'dp', scatter_dimension=1, tiled=True)]
    all_gather x7 -> x6, waiting for transfers between devices: 105 us -> 0.06 us  [the longest x3 0.04 us: body(): lax.all_gather(new, 'dp', axis=1, tiled=True)]
    ppermute x35 -> x38, waiting for transfers between devices: 368 us -> 346 us  [the longest x24 311 us: send(): return lax.ppermute(value, self.axis, self.ahead)]
    pallas_call x2 -> x5, Pallas kernels: 29.7 us -> 49.3 us  [the longest x1 19.2 us: recurrence_backward(): pl.pallas_call(functools.partial(backward_kernel, len(parts)), grid_spec=...]
    unnamed x161 -> x175, local copies, waits for them, and re-layouts: 41.1 us -> 22.4 us
    dot_general x60 -> x37, matrix products: 179 us -> 163 us  [dot(): lax.dot_general(left, right, (dims, ((), ())), preferred_element_type=jnp...]
    convert_element_type x8 -> x23, other arithmetic: 31.1 us -> 45.7 us  [bf16(): return value.astype(jnp.bfloat16)]
    ppermute x35 -> x38, starting transfers between devices: 42.3 us -> 43.7 us  [the longest x24 29.3 us: send(): return lax.ppermute(value, self.axis, self.ahead)]
  transfers between devices with their start and end apart: 50 -> 48, of which waited for: 32 -> 31; matrix products, arithmetic and copies ran while one was open for 23% -> 32% of each run, Pallas kernels for 3% -> 6%
where the time goes in v2:
time: 788 us; the launch traced here: 779 us
  waiting for transfers between devices  368 us (47%)
  matrix products  163 us (21%)
  other arithmetic  98.9 us (13%)
  Pallas kernels  49.3 us (6%)
  starting transfers between devices  44.3 us (6%)
  local copies, waits for them, and re-layouts  36.9 us (5%)
  between operations  17.7 us (2%)
    ppermute x24, waiting for transfers between devices, send(): return lax.ppermute(value, self.axis, self.ahead)  311 us
    dot_general x37, matrix products, dot(): lax.dot_general(left, right, (dims, ((), ())), preferred_element_type=jnp...  163 us
    convert_element_type x23, other arithmetic, bf16(): return value.astype(jnp.bfloat16)  45.7 us
    ppermute x14, waiting for transfers between devices, flip(): lax.ppermute(value, axis, [(i, i ^ 1 << bit) for i in range(lax.axis_size...  34.4 us
    ppermute x24, starting transfers between devices, send(): return lax.ppermute(value, self.axis, self.ahead)  29.3 us
    unnamed x175, local copies, waits for them, and re-layouts  22.4 us
    reduce_scatter x1, waiting for transfers between devices, body(): lax.psum_scatter(sum_down, 'dp', scatter_dimension=1, tiled=True)  22.4 us
    pallas_call x1, Pallas kernels, recurrence_backward(): pl.pallas_call(functools.partial(backward_kernel, len(parts)), grid_spec=...  19.2 us
  transfers between devices with their start and end apart: 48, of which 31 were waited for; matrix products, arithmetic and copies ran while one was open for 32% of the time, Pallas kernels for 6%

profile of v2, /device:TPU:0, one launch (start us, length us, event | category | flops | bytes accessed | tf_op | source)
XLA Modules:
  0.0 778.6 jit_solution(2552738306074380438)
XLA Ops:
  11.7 3.1 convert_element_type.374
  19.5 24.3 %collective-permute-done = bf16[256,2048]{1,0:T(8,128)(2,1)} collective-permute-done((bf16[256,2048]{1,0:T(8,128)(2,1)S(1)}, bf16[256,2048]{1,0:T(8,128)(2,1)}, u32[]{:S(2)}, u32[]{:S(2)}) %collective-permute-start) | collective-permute-done | bytes 1048608 | tf_op jit(solution)/shard_map/ppermute | solution.py:304
  48.0 21.3 %collective-permute-done.1 = bf16[256,2048]{1,0:T(8,128)(2,1)} collective-permute-done((bf16[256,2048]{1,0:T(8,128)(2,1)}, bf16[256,2048]{1,0:T(8,128)(2,1)}, u32[]{:S(2)}, u32[]{:S(2)}) %collective-permute-start.1) | collective-permute-done | bytes 1048608 | tf_op jit(solution)/shard_map/ppermute | solution.py:304
  71.0 4.7 fusion.88.refs_0_
  75.8 18.2 %collective-permute-done.2 = bf16[256,2048]{1,0:T(8,128)(2,1)} collective-permute-done((bf16[256,2048]{1,0:T(8,128)(2,1)}, bf16[256,2048]{1,0:T(8,128)(2,1)}, u32[]{:S(2)}, u32[]{:S(2)}) %collective-permute-start.2) | collective-permute-done | bytes 1048608 | tf_op jit(solution)/shard_map/ppermute | solution.py:304
  97.2 3.6 fusion.90.refs_2_
  100.8 3.6 fusion.91.refs_3_
  104.4 12.1 %recurrence_forward.1 = (bf16[1024,512]{1,0:T(8,128)(2,1)S(1)}, f32[1024,512]{1,0:T(8,128)S(1)}, f32[8,4,128,128]{3,2,1,0:T(8,128)S(1)}) custom-call(s32[1]{0:T(128)} %dynamic_slice.56.length, s32[8]{0:T(128)S(1)} %gather_fusion, s32[32]{0:T(128)S(1)} %min.12.part.part_core, s32[8]{0:T(128)S(1)} %fusion.64.core_at.place, f32[256,1536]{1,0:T(8,128)S(1)} %fusion.88.refs_0_, ...), custom_call_target="tpu_custom_call" | custom-call | flops 805306368 | bytes 9437184 | tf_op jit(solution)/shard_map/recurrence_forward/pallas_call | solution.py:127
  119.0 4.3 convolution_convert_fusion.5
  123.5 3.4 collective-permute-start.4
  126.9 20.4 %collective-permute-done.4 = bf16[256,2048]{1,0:T(8,128)(2,1)S(1)} collective-permute-done((bf16[256,2048]{1,0:T(8,128)(2,1)S(1)}, bf16[256,2048]{1,0:T(8,128)(2,1)S(1)}, u32[]{:S(2)}, u32[]{:S(2)}) %collective-permute-start.4) | collective-permute-done | bytes 1048608 | tf_op jit(solution)/shard_map/ppermute | solution.py:304
  150.8 23.9 %collective-permute-done.5 = bf16[256,2048]{1,0:T(8,128)(2,1)S(1)} collective-permute-done((bf16[256,2048]{1,0:T(8,128)(2,1)S(1)}, bf16[256,2048]{1,0:T(8,128)(2,1)S(1)}, u32[]{:S(2)}, u32[]{:S(2)}) %collective-permute-start.5) | collective-permute-done | bytes 1048608 | tf_op jit(solution)/shard_map/ppermute | solution.py:304
  177.9 6.0 fusion.92
  183.9 4.3 fusion.93
  188.2 9.1 %collective-permute-done.10 = bf16[256,2048]{1,0:T(8,128)(2,1)} collective-permute-done((bf16[256,2048]{1,0:T(8,128)(2,1)}, bf16[256,2048]{1,0:T(8,128)(2,1)}, u32[]{:S(2)}, u32[]{:S(2)}) %collective-permute-start.10) | collective-permute-done | bytes 1048608 | tf_op jit(solution)/shard_map/ppermute | solution.py:304
  198.9 20.8 %collective-permute-done.6 = bf16[256,2048]{1,0:T(8,128)(2,1)S(1)} collective-permute-done((bf16[256,2048]{1,0:T(8,128)(2,1)}, bf16[256,2048]{1,0:T(8,128)(2,1)S(1)}, u32[]{:S(2)}, u32[]{:S(2)}) %collective-permute-start.6) | collective-permute-done | bytes 1048608 | tf_op jit(solution)/shard_map/ppermute | solution.py:304
  226.0 4.9 fusion.56
  230.9 6.5 multiply_convert_fusion.12
  241.1 19.4 %collective-permute-done.7 = bf16[256,2048]{1,0:T(8,128)(2,1)} collective-permute-done((bf16[256,2048]{1,0:T(8,128)(2,1)}, bf16[256,2048]{1,0:T(8,128)(2,1)}, u32[]{:S(2)}, u32[]{:S(2)}) %collective-permute-start.7) | collective-permute-done | bytes 1048608 | tf_op jit(solution)/shard_map/ppermute | solution.py:304
  266.3 4.3 multiply_convert_fusion.9
  275.0 13.0 %collective-permute-done.8 = bf16[256,2048]{1,0:T(8,128)(2,1)S(1)} collective-permute-done((bf16[256,2048]{1,0:T(8,128)(2,1)}, bf16[256,2048]{1,0:T(8,128)(2,1)S(1)}, u32[]{:S(2)}, u32[]{:S(2)}) %collective-permute-start.8) | collective-permute-done | bytes 1048608 | tf_op jit(solution)/shard_map/ppermute | solution.py:304
  295.8 5.3 multiply_convert_fusion.6
  304.3 6.2 collective-permute-done.11
  310.4 4.5 add_convert_fusion.6
  316.6 16.3 %collective-permute-done.9 = bf16[256,2048]{1,0:T(8,128)(2,1)S(1)} collective-permute-done((bf16[256,2048]{1,0:T(8,128)(2,1)S(1)}, bf16[256,2048]{1,0:T(8,128)(2,1)S(1)}, u32[]{:S(2)}, u32[]{:S(2)}) %collective-permute-start.9) | collective-permute-done | bytes 1048608 | tf_op jit(solution)/shard_map/ppermute | solution.py:304
  336.5 4.5 multiply_convert_fusion.1
  341.1 5.0 pad_maximum_fusion.5
  346.0 4.8 pad_maximum_fusion.4
  350.8 4.5 fusion.49
  355.3 5.8 add_convert_fusion.5
  361.1 8.3 %fusion.1 = bf16[1,2048,1408]{2,1,0:T(8,128)(2,1)S(1)} fusion(bf16[1024,1408]{1,0:T(8,128)(2,1)S(1)} %pad_maximum_fusion.5, bf16[256,2048]{1,0:T(8,128)(2,1)S(1)} %collective-permute-done.9, bf16[256,2048]{1,0:T(8,128)(2,1)S(1)} %collective-permute-done.8, bf16[256,2048]{1,0:T(8,128)(2,1)} %collective-permute-done.7, bf16[256,2048]{1,0:T(8,128)(2,1)} %multiply_convert_fusion), kind=kOutput, calls=%fused_computation.6 | convolution fusion | flops 5925240832 | bytes 12845056 | tf_op jit(solution)/shard_map/dot_general | solution.py:36
  369.5 8.6 %fusion = bf16[1,2048,1408]{2,1,0:T(8,128)(2,1)S(1)} fusion(bf16[1024,1408]{1,0:T(8,128)(2,1)S(1)} %pad_maximum_fusion.4, bf16[256,2048]{1,0:T(8,128)(2,1)S(1)} %collective-permute-done.9, bf16[256,2048]{1,0:T(8,128)(2,1)S(1)} %collective-permute-done.8, bf16[256,2048]{1,0:T(8,128)(2,1)} %collective-permute-done.7, bf16[256,2048]{1,0:T(8,128)(2,1)} %multiply_convert_fusion), kind=kOutput, calls=%fused_computation.5 | convolution fusion | flops 5925240832 | bytes 12845056 | tf_op jit(solution)/shard_map/dot_general | solution.py:36
  378.1 5.0 pad_maximum_fusion
  386.8 9.7 %convolution_convert_fusion = bf16[1408,2048]{1,0:T(8,128)(2,1)} fusion(bf16[1024,1408]{1,0:T(8,128)(2,1)S(1)} %pad_maximum_fusion.3, bf16[256,2048]{1,0:T(8,128)(2,1)} %collective-permute-done.13, bf16[256,2048]{1,0:T(8,128)(2,1)} %collective-permute-done.10, bf16[256,2048]{1,0:T(8,128)(2,1)} %collective-permute-done.3, bf16[256,2048]{1,0:T(8,128)(2,1)} %fusion.38), kind=kOutput, calls=%fused_computation.2 | convolution fusion | flops 5925240832 | bytes 12845056 | tf_op jit(solution)/shard_map/dot_general | solution.py:36
  397.7 3.5 collective-permute-done.14
  401.2 3.3 multiply_reduce_fusion.2
  404.6 3.8 fusion.85
  412.1 4.0 permute_columns.3
  418.7 17.7 %collective-permute-done.15 = bf16[256,2048]{1,0:T(8,128)(2,1)} collective-permute-done((bf16[256,2048]{1,0:T(8,128)(2,1)}, bf16[256,2048]{1,0:T(8,128)(2,1)}, u32[]{:S(2)}, u32[]{:S(2)}) %collective-permute-start.15) | collective-permute-done | bytes 1048608 | tf_op jit(solution)/shard_map/ppermute | solution.py:304
  436.4 9.2 %convolution_convert_fusion.4 = bf16[1024,2048]{1,0:T(8,128)(2,1)S(1)} fusion(bf16[1024,1408]{1,0:T(8,128)(2,1)S(1)} %copy-done.41, bf16[1408,2048]{1,0:T(8,128)(2,1)} %all-gather.15.cloned.1.call-done), kind=kOutput, calls=%fused_computation.35 | convolution fusion | flops 5907677184 | bytes 12845056 | tf_op jit(solution)/shard_map/dot_general | solution.py:36
  450.5 12.2 %collective-permute-done.16 = bf16[256,2048]{1,0:T(8,128)(2,1)S(1)} collective-permute-done((bf16[256,2048]{1,0:T(8,128)(2,1)}, bf16[256,2048]{1,0:T(8,128)(2,1)S(1)}, u32[]{:S(2)}, u32[]{:S(2)}) %collective-permute-start.16) | collective-permute-done | bytes 1048608 | tf_op jit(solution)/shard_map/ppermute | solution.py:304
  463.4 14.9 %collective-permute-done.17 = bf16[256,2048]{1,0:T(8,128)(2,1)S(1)} collective-permute-done((bf16[256,2048]{1,0:T(8,128)(2,1)S(1)}, bf16[256,2048]{1,0:T(8,128)(2,1)S(1)}, u32[]{:S(2)}, u32[]{:S(2)}) %collective-permute-start.17) | collective-permute-done | bytes 1048608 | tf_op jit(solution)/shard_map/ppermute | solution.py:304
  479.4 19.2 %recurrence_backward.1 = (bf16[1024,1536]{1,0:T(8,128)(2,1)S(1)}, f32[8,512]{1,0:T(8,128)S(1)}) custom-call(s32[1]{0:T(128)} %dynamic_slice.56.length, s32[8]{0:T(128)S(1)} %gather_fusion, s32[32]{0:T(128)S(1)} %min.12.part.part_core, s32[8]{0:T(128)S(1)} %fusion.64.core_at.place, s32[8]{0:T(128)S(1)} %gather_fusion, s32[32]{0:T(128)S(1)} %min.12.part.part_core, ...), custom_call_target="tpu_custom_call" | custom-call | flops 2684354560 | bytes 13631488 | tf_op jit(solution)/shard_map/recurrence_backward/pallas_call | solution.py:254
  501.4 9.2 %fusion.83 = (bf16[2,256,1408]{2,1,0:T(8,128)(2,1)}, f32[2,256,1408]{2,1,0:T(8,128)}, f32[2,256,1408]{2,1,0:T(8,128)}, f32[2,256,1408]{2,1,0:T(8,128)}, f32[2,256,1408]{2,1,0:T(8,128)}) fusion(f32[2,256,1408]{2,1,0:T(8,128)} %param.33, f32[2,256,1408]{2,1,0:T(8,128)} %param.34, f32[2,256,1408]{2,1,0:T(8,128)} %param.35, ...), kind=kLoop, calls=%fused_computation.218 | loop fusion | flops 12976128 | bytes 23068676 | tf_op jit(solution)/shard_map/convert_element_type | solution.py:28
  510.8 22.4 %reduce-scatter.3.cloned.1.call-done = bf16[1408,256]{1,0:T(8,128)(2,1)} async-done(((bf16[1408,2048]{1,0:T(8,128)(2,1)}), bf16[1408,256]{1,0:T(8,128)(2,1)}) %reduce-scatter.3.cloned.1.call-update) | async-done | bytes 720912 | tf_op jit(solution)/shard_map/reduce_scatter | solution.py:561
  533.1 5.9 fusion.81
  539.3 4.5 fusion.19
  549.1 23.8 %collective-permute-done.18 = bf16[256,2048]{1,0:T(8,128)(2,1)S(1)} collective-permute-done((bf16[256,2048]{1,0:T(8,128)(2,1)}, bf16[256,2048]{1,0:T(8,128)(2,1)S(1)}, u32[]{:S(2)}, u32[]{:S(2)}) %collective-permute-start.18) | collective-permute-done | bytes 1048608 | tf_op jit(solution)/shard_map/ppermute | solution.py:304
  577.5 5.4 convolution_convert_fusion.7
  586.2 7.2 convolution_convert_fusion.6
  593.5 5.6 collective-permute-done.20
  615.1 10.6 %collective-permute-done.27 = bf16[256,2048]{1,0:T(8,128)(2,1)} collective-permute-done((bf16[256,2048]{1,0:T(8,128)(2,1)}, bf16[256,2048]{1,0:T(8,128)(2,1)}, u32[]{:S(2)}, u32[]{:S(2)}) %collective-permute-start.27) | collective-permute-done | bytes 1048608 | tf_op jit(solution)/shard_map/ppermute | solution.py:304
  627.3 11.2 %convolution_convert_fusion.3 = bf16[1024,2048]{1,0:T(8,128)(2,1)} fusion(bf16[1024,1536]{1,0:T(8,128)(2,1)S(1)} %copy-done.11, bf16[2048,1536]{1,0:T(8,128)(2,1)} %all-gather.9.cloned.1.call-done), kind=kOutput, calls=%fused_computation.34 | convolution fusion | flops 6444548096 | bytes 13631488 | tf_op jit(solution)/shard_map/dot_general | solution.py:36
  644.2 10.9 %copied.1 = bf16[2,2048,1408]{2,1,0:T(8,128)(2,1)} custom-call(bf16[2,2048,1408]{2,1,0:T(8,128)(2,1)} %all-gather.17.cloned.1.call-done.value), custom_call_target="tpu_custom_call" | custom-call | tf_op jit(solution)/shard_map/copied/pallas_call | solution.py:413
  656.9 4.1 broadcast_select_fusion
  662.3 15.3 %collective-permute-done.25 = bf16[2,256,768]{2,1,0:T(8,128)(2,1)S(1)} collective-permute-done((bf16[2,256,768]{2,1,0:T(8,128)(2,1)}, bf16[2,256,768]{2,1,0:T(8,128)(2,1)S(1)}, u32[]{:S(2)}, u32[]{:S(2)}) %collective-permute-start.25) | collective-permute-done | bytes 786464 | tf_op jit(solution)/shard_map/ppermute | solution.py:323
  679.2 3.7 collective-permute-done.28
  688.0 3.6 fusion.77
  691.7 4.8 multiply_reduce_fusion
  697.4 4.4 fusion.27
  715.7 11.6 %collective-permute-done.34 = bf16[256,2048]{1,0:T(8,128)(2,1)S(1)} collective-permute-done((bf16[256,2048]{1,0:T(8,128)(2,1)S(1)}, bf16[256,2048]{1,0:T(8,128)(2,1)S(1)}, u32[]{:S(2)}, u32[]{:S(2)}) %collective-permute-start.34) | collective-permute-done | bytes 1048608 | tf_op jit(solution)/shard_map/ppermute | solution.py:304
  730.6 18.5 %collective-permute-done.35 = bf16[256,2048]{1,0:T(8,128)(2,1)} collective-permute-done((bf16[256,2048]{1,0:T(8,128)(2,1)}, bf16[256,2048]{1,0:T(8,128)(2,1)}, u32[]{:S(2)}, u32[]{:S(2)}) %collective-permute-start.35) | collective-permute-done | bytes 1048608 | tf_op jit(solution)/shard_map/ppermute | solution.py:304
  755.9 3.6 fusion.35
  761.4 6.1 copy.65
  (352 shorter events, 160.9 us)
Async XLA Ops:
  7.2 63.8 %all-gather.9.cloned.1.call-start = ((), (), s32[]{:S(2)}) async-start(), calls=%async_computation.2 | async-start | bytes 7077888 | tf_op jit(solution)/shard_map/all_gather | solution.py:498
  9.8 109.2 %all-gather.11.cloned.1.call-start = ((), (), s32[]{:S(2)}) async-start(), calls=%async_computation.3 | async-start | bytes 2359296 | tf_op jit(solution)/shard_map/all_gather | solution.py:500
  10.6 167.3 %all-gather.15.cloned.1.call-start = ((), (), s32[]{:S(2)}) async-start(), calls=%async_computation.5 | async-start | bytes 6488064 | tf_op jit(solution)/shard_map/all_gather | solution.py:502
  11.6 214.4 %all-gather.13.cloned.1.call-start = ((), (), s32[]{:S(2)}) async-start(), calls=%async_computation.4 | async-start | bytes 12976128 | tf_op jit(solution)/shard_map/all_gather | solution.py:501
  14.8 30.5 %copy-start.75 = (s32[8]{0:T(128)S(1)}, s32[8]{0:T(128)}, u32[]{:S(2)}) copy-start(s32[8]{0:T(128)} %param.23) | copy-start | bytes 100
  14.9 55.0 %copy-start.32 = (bf16[256,2048]{1,0:T(8,128)(2,1)S(1)}, bf16[256,2048]{1,0:T(8,128)(2,1)}, u32[]{:S(2)}) copy-start(bf16[256,2048]{1,0:T(8,128)(2,1)} %param.22) | copy-start | bytes 3145732
  14.9 486.6 %reduce-scatter.5.cloned.1.call-start = ((), (), s32[]{:S(2)}) async-start(), calls=%async_computation.7 | async-start | bytes 12976128 | tf_op jit(solution)/shard_map/reduce_scatter | solution.py:558
  15.8 31.4 %copy-start.69 = (f32[256]{0:T(256)}, f32[256]{0:T(256)S(1)}, u32[]{:S(2)}) copy-start(f32[256]{0:T(256)S(1)} %get-tuple-element.175) | copy-start | bytes 3076
  16.5 59.3 %copy-start.55 = (bf16[256,2048]{1,0:T(8,128)(2,1)}, bf16[256,2048]{1,0:T(8,128)(2,1)S(1)}, u32[]{:S(2)}) copy-start(bf16[256,2048]{1,0:T(8,128)(2,1)S(1)} %fusion.32) | copy-start | bytes 3145732
  16.5 27.3 %collective-permute-start = (bf16[256,2048]{1,0:T(8,128)(2,1)S(1)}, bf16[256,2048]{1,0:T(8,128)(2,1)}, u32[]{:S(2)}, u32[]{:S(2)}) collective-permute-start(bf16[256,2048]{1,0:T(8,128)(2,1)S(1)} %fusion.32), channel_id=1, source_target_pairs={{0,1},{1,3},{3,2},{2,0},{4,5},{5,7},{7,6},{6,4},{8,9},{9,11},{11,1... | collective-permute-start | bytes 3145736 | tf_op jit(solution)/shard_map/ppermute | solution.py:304
  43.8 25.6 %collective-permute-start.1 = (bf16[256,2048]{1,0:T(8,128)(2,1)}, bf16[256,2048]{1,0:T(8,128)(2,1)}, u32[]{:S(2)}, u32[]{:S(2)}) collective-permute-start(bf16[256,2048]{1,0:T(8,128)(2,1)} %collective-permute-done), channel_id=1, source_target_pairs={{0,1},{1,3},{3,2},{2,0},{4,5},{5,7},{7,6},{6,4},{8,9},{9,11},{11,1... | collective-permute-start | bytes 3145736 | tf_op jit(solution)/shard_map/ppermute | solution.py:304
  47.9 27.8 %copy-start.66 = (f32[256]{0:T(256)}, f32[256]{0:T(256)S(1)}, u32[]{:S(2)}) copy-start(f32[256]{0:T(256)S(1)} %compare_convert_fusion) | copy-start | bytes 3076
  69.3 24.6 %collective-permute-start.2 = (bf16[256,2048]{1,0:T(8,128)(2,1)}, bf16[256,2048]{1,0:T(8,128)(2,1)}, u32[]{:S(2)}, u32[]{:S(2)}) collective-permute-start(bf16[256,2048]{1,0:T(8,128)(2,1)} %collective-permute-done.1), channel_id=1, source_target_pairs={{0,1},{1,3},{3,2},{2,0},{4,5},{5,7},{7,6},{6,4},{8,9},{9,11},{11,1... | collective-permute-start | bytes 3145736 | tf_op jit(solution)/shard_map/ppermute | solution.py:304
  75.8 28.6 %copy-start = (f32[256,1536]{1,0:T(8,128)}, f32[256,1536]{1,0:T(8,128)S(1)}, u32[]{:S(2)}) copy-start(f32[256,1536]{1,0:T(8,128)S(1)} %fusion.88.refs_0_) | copy-start | bytes 4718596
  94.0 29.5 %collective-permute-start.3 = (bf16[256,2048]{1,0:T(8,128)(2,1)}, bf16[256,2048]{1,0:T(8,128)(2,1)}, u32[]{:S(2)}, u32[]{:S(2)}) collective-permute-start(bf16[256,2048]{1,0:T(8,128)(2,1)} %fusion.38), channel_id=1, source_target_pairs={{0,1},{1,3},{3,2},{2,0},{4,5},{5,7},{7,6},{6,4},{8,9},{9,11},{11,1... | collective-permute-start | bytes 3145736 | tf_op jit(solution)/shard_map/ppermute | solution.py:304
  123.4 51.4 %copy-start.24 = (bf16[1024,2048]{1,0:T(8,128)(2,1)}, bf16[1024,2048]{1,0:T(8,128)(2,1)S(1)}, u32[]{:S(2)}) copy-start(bf16[1024,2048]{1,0:T(8,128)(2,1)S(1)} %convolution_convert_fusion.5) | copy-start | bytes 12582916
  123.5 23.8 %collective-permute-start.4 = (bf16[256,2048]{1,0:T(8,128)(2,1)S(1)}, bf16[256,2048]{1,0:T(8,128)(2,1)S(1)}, u32[]{:S(2)}, u32[]{:S(2)}) collective-permute-start(bf16[256,2048]{1,0:T(8,128)(2,1)S(1)} %slice.189), channel_id=1, source_target_pairs={{0,1},{1,3},{3,2},{2,0},{4,5},{5,7},{7,6},{6,4},{8,9},{9,11},{11,1... | collective-permute-start | bytes 3145736 | tf_op jit(solution)/shard_map/ppermute | solution.py:304
  147.7 27.0 %collective-permute-start.5 = (bf16[256,2048]{1,0:T(8,128)(2,1)S(1)}, bf16[256,2048]{1,0:T(8,128)(2,1)S(1)}, u32[]{:S(2)}, u32[]{:S(2)}) collective-permute-start(bf16[256,2048]{1,0:T(8,128)(2,1)S(1)} %add_convert_fusion.8), channel_id=1, source_target_pairs={{0,1},{1,3},{3,2},{2,0},{4,5},{5,7},{7,6},{6,4},{8,9},{9,11},{11,1... | collective-permute-start | bytes 3145736 | tf_op jit(solution)/shard_map/ppermute | solution.py:304
  150.2 47.1 %collective-permute-start.10 = (bf16[256,2048]{1,0:T(8,128)(2,1)}, bf16[256,2048]{1,0:T(8,128)(2,1)}, u32[]{:S(2)}, u32[]{:S(2)}) collective-permute-start(bf16[256,2048]{1,0:T(8,128)(2,1)} %collective-permute-done.3), channel_id=1, source_target_pairs={{0,1},{1,3},{3,2},{2,0},{4,5},{5,7},{7,6},{6,4},{8,9},{9,11},{11,1... | collective-permute-start | bytes 3145736 | tf_op jit(solution)/shard_map/ppermute | solution.py:304
  176.1 43.6 %collective-permute-start.6 = (bf16[256,2048]{1,0:T(8,128)(2,1)}, bf16[256,2048]{1,0:T(8,128)(2,1)S(1)}, u32[]{:S(2)}, u32[]{:S(2)}) collective-permute-start(bf16[256,2048]{1,0:T(8,128)(2,1)} %add_convert_fusion.7), channel_id=1, source_target_pairs={{0,1},{1,3},{3,2},{2,0},{4,5},{5,7},{7,6},{6,4},{8,9},{9,11},{11,1... | collective-permute-start | bytes 3145736 | tf_op jit(solution)/shard_map/ppermute | solution.py:304
  183.9 35.8 %copy-start.18 = (bf16[256,2048]{1,0:T(8,128)(2,1)S(1)}, bf16[256,2048]{1,0:T(8,128)(2,1)}, u32[]{:S(2)}) copy-start(bf16[256,2048]{1,0:T(8,128)(2,1)} %param.21) | copy-start | bytes 3145732
  197.3 139.2 %collective-permute-start.13 = (bf16[256,2048]{1,0:T(8,128)(2,1)}, bf16[256,2048]{1,0:T(8,128)(2,1)}, u32[]{:S(2)}, u32[]{:S(2)}) collective-permute-start(bf16[256,2048]{1,0:T(8,128)(2,1)} %collective-permute-done.10), channel_id=1, source_target_pairs={{0,1},{1,3},{3,2},{2,0},{4,5},{5,7},{7,6},{6,4},{8,9},{9,11},{11,1... | collective-permute-start | bytes 3145736 | tf_op jit(solution)/shard_map/ppermute | solution.py:304
  224.4 36.1 %collective-permute-start.7 = (bf16[256,2048]{1,0:T(8,128)(2,1)}, bf16[256,2048]{1,0:T(8,128)(2,1)}, u32[]{:S(2)}, u32[]{:S(2)}) collective-permute-start(bf16[256,2048]{1,0:T(8,128)(2,1)} %multiply_convert_fusion), channel_id=1, source_target_pairs={{0,1},{1,3},{3,2},{2,0},{4,5},{5,7},{7,6},{6,4},{8,9},{9,11},{11,1... | collective-permute-start | bytes 3145736 | tf_op jit(solution)/shard_map/ppermute | solution.py:304
  260.5 27.4 %collective-permute-start.8 = (bf16[256,2048]{1,0:T(8,128)(2,1)}, bf16[256,2048]{1,0:T(8,128)(2,1)S(1)}, u32[]{:S(2)}, u32[]{:S(2)}) collective-permute-start(bf16[256,2048]{1,0:T(8,128)(2,1)} %collective-permute-done.7), channel_id=1, source_target_pairs={{0,1},{1,3},{3,2},{2,0},{4,5},{5,7},{7,6},{6,4},{8,9},{9,11},{11,1... | collective-permute-start | bytes 3145736 | tf_op jit(solution)/shard_map/ppermute | solution.py:304
  274.3 36.1 %collective-permute-start.11 = (bf16[256,2048]{1,0:T(8,128)(2,1)S(1)}, bf16[256,2048]{1,0:T(8,128)(2,1)S(1)}, u32[]{:S(2)}, u32[]{:S(2)}) collective-permute-start(bf16[256,2048]{1,0:T(8,128)(2,1)S(1)} %fusion.24), channel_id=1, source_target_pairs={{0,1},{1,3},{3,2},{2,0},{4,5},{5,7},{7,6},{6,4},{8,9},{9,11},{11,1... | collective-permute-start | bytes 3145736 | tf_op jit(solution)/shard_map/ppermute | solution.py:304
  288.0 44.9 %collective-permute-start.9 = (bf16[256,2048]{1,0:T(8,128)(2,1)S(1)}, bf16[256,2048]{1,0:T(8,128)(2,1)S(1)}, u32[]{:S(2)}, u32[]{:S(2)}) collective-permute-start(bf16[256,2048]{1,0:T(8,128)(2,1)S(1)} %collective-permute-done.8), channel_id=1, source_target_pairs={{0,1},{1,3},{3,2},{2,0},{4,5},{5,7},{7,6},{6,4},{8,9},{9,11},{11,1... | collective-permute-start | bytes 3145736 | tf_op jit(solution)/shard_map/ppermute | solution.py:304
  314.9 40.4 %collective-permute-start.12 = (bf16[256,2048]{1,0:T(8,128)(2,1)}, bf16[256,2048]{1,0:T(8,128)(2,1)}, u32[]{:S(2)}, u32[]{:S(2)}) collective-permute-start(bf16[256,2048]{1,0:T(8,128)(2,1)} %add_convert_fusion.6), channel_id=1, source_target_pairs={{0,1},{1,3},{3,2},{2,0},{4,5},{5,7},{7,6},{6,4},{8,9},{9,11},{11,1... | collective-permute-start | bytes 3145736 | tf_op jit(solution)/shard_map/ppermute | solution.py:304
  383.1 150.0 %reduce-scatter.3.cloned.1.call-start = ((), (), s32[]{:S(2)}) async-start(), calls=%async_computation.6 | async-start | bytes 6488064 | tf_op jit(solution)/shard_map/reduce_scatter | solution.py:561
  385.2 16.1 %collective-permute-start.14 = (bf16[256,2048]{1,0:T(8,128)(2,1)}, bf16[256,2048]{1,0:T(8,128)(2,1)}, u32[]{:S(2)}, u32[]{:S(2)}) collective-permute-start(bf16[256,2048]{1,0:T(8,128)(2,1)} %add_convert_fusion.5), channel_id=1, source_target_pairs={{0,1},{1,3},{3,2},{2,0},{4,5},{5,7},{7,6},{6,4},{8,9},{9,11},{11,1... | collective-permute-start | bytes 3145736 | tf_op jit(solution)/shard_map/ppermute | solution.py:304
  396.5 247.6 %all-gather.17.cloned.1.call-start = ((), (), s32[]{:S(2)}) async-start(), calls=%async_computation.8 | async-start | bytes 12976128 | tf_op jit(solution)/shard_map/all_gather | solution.py:654
  411.4 24.9 %collective-permute-start.15 = (bf16[256,2048]{1,0:T(8,128)(2,1)}, bf16[256,2048]{1,0:T(8,128)(2,1)}, u32[]{:S(2)}, u32[]{:S(2)}) collective-permute-start(bf16[256,2048]{1,0:T(8,128)(2,1)} %permute_columns.2), channel_id=1, source_target_pairs={{0,1},{1,3},{3,2},{2,0},{4,5},{5,7},{7,6},{6,4},{8,9},{9,11},{11,1... | collective-permute-start | bytes 3145736 | tf_op jit(solution)/shard_map/ppermute | solution.py:304
  436.4 26.3 %collective-permute-start.16 = (bf16[256,2048]{1,0:T(8,128)(2,1)}, bf16[256,2048]{1,0:T(8,128)(2,1)S(1)}, u32[]{:S(2)}, u32[]{:S(2)}) collective-permute-start(bf16[256,2048]{1,0:T(8,128)(2,1)} %collective-permute-done.15), channel_id=1, source_target_pairs={{0,1},{1,3},{3,2},{2,0},{4,5},{5,7},{7,6},{6,4},{8,9},{9,11},{11,1... | collective-permute-start | bytes 3145736 | tf_op jit(solution)/shard_map/ppermute | solution.py:304
  448.3 31.0 %copy-start.9 = (f32[8,4,128,128]{3,2,1,0:T(8,128)S(1)}, f32[8,4,128,128]{3,2,1,0:T(8,128)}, u32[]{:S(2)}) copy-start(f32[8,4,128,128]{3,2,1,0:T(8,128)} %copy-done.8) | copy-start | bytes 6291460
  462.6 15.7 %collective-permute-start.17 = (bf16[256,2048]{1,0:T(8,128)(2,1)S(1)}, bf16[256,2048]{1,0:T(8,128)(2,1)S(1)}, u32[]{:S(2)}, u32[]{:S(2)}) collective-permute-start(bf16[256,2048]{1,0:T(8,128)(2,1)S(1)} %collective-permute-done.16), channel_id=1, source_target_pairs={{0,1},{1,3},{3,2},{2,0},{4,5},{5,7},{7,6},{6,4},{8,9},{9,11},{11,1... | collective-permute-start | bytes 3145736 | tf_op jit(solution)/shard_map/ppermute | solution.py:304
  510.7 28.5 %copy-start.13 = (bf16[1024,512]{1,0:T(8,128)(2,1)S(1)}, bf16[1024,512]{1,0:T(8,128)(2,1)}, u32[]{:S(2)}) copy-start(bf16[1024,512]{1,0:T(8,128)(2,1)} %copy-done.12) | copy-start | bytes 3145732
  510.7 219.9 %all-gather.23.cloned.1.call-start = ((), (), s32[]{:S(2)}) async-start(), calls=%async_computation.11 | async-start | bytes 6488064 | tf_op jit(solution)/shard_map/all_gather | solution.py:668
  539.0 191.6 %all-gather.21.cloned.1.call-start = ((), (), s32[]{:S(2)}) async-start(), calls=%async_computation.10 | async-start | bytes 2359296 | tf_op jit(solution)/shard_map/all_gather | solution.py:668
  546.2 2.9 collective-permute-start.19
  546.2 26.7 %collective-permute-start.18 = (bf16[256,2048]{1,0:T(8,128)(2,1)}, bf16[256,2048]{1,0:T(8,128)(2,1)S(1)}, u32[]{:S(2)}, u32[]{:S(2)}) collective-permute-start(bf16[256,2048]{1,0:T(8,128)(2,1)} %get-tuple-element.86), channel_id=1, source_target_pairs={{0,1},{1,3},{3,2},{2,0},{4,5},{5,7},{7,6},{6,4},{8,9},{9,11},{11,1... | collective-permute-start | bytes 3145736 | tf_op jit(solution)/shard_map/ppermute | solution.py:304
  547.7 26.3 %copy-start.43 = (bf16[512,2048]{1,0:T(8,128)(2,1)S(1)}, bf16[512,2048]{1,0:T(8,128)(2,1)}, u32[]{:S(2)}) copy-start(bf16[512,2048]{1,0:T(8,128)(2,1)} %copy-done.42) | copy-start | bytes 6291460
  573.3 25.7 %collective-permute-start.20 = (bf16[256,2048]{1,0:T(8,128)(2,1)S(1)}, bf16[256,2048]{1,0:T(8,128)(2,1)S(1)}, u32[]{:S(2)}, u32[]{:S(2)}) collective-permute-start(bf16[256,2048]{1,0:T(8,128)(2,1)S(1)} %add_convert_fusion.4), channel_id=1, source_target_pairs={{0,1},{1,3},{3,2},{2,0},{4,5},{5,7},{7,6},{6,4},{8,9},{9,11},{11,1... | collective-permute-start | bytes 3145736 | tf_op jit(solution)/shard_map/ppermute | solution.py:304
  576.0 25.5 %collective-permute-start.21 = (bf16[512,512]{1,0:T(8,128)(2,1)S(1)}, bf16[512,512]{1,0:T(8,128)(2,1)S(1)}, u32[]{:S(2)}, u32[]{:S(2)}) collective-permute-start(bf16[512,512]{1,0:T(8,128)(2,1)S(1)} %slice.201), channel_id=1, source_target_pairs={{0,8},{4,12},{8,0},{12,4},{16,24},{20,28},{24,16},{28,20},{1,9},{5... | collective-permute-start | bytes 1572872 | tf_op jit(solution)/shard_map/ppermute | solution.py:323
  586.2 24.4 %collective-permute-start.22 = (bf16[2,2,256,768]{3,2,0,1:T(8,128)(2,1)}, bf16[2,2,256,768]{3,2,0,1:T(8,128)(2,1)}, u32[]{:S(2)}, u32[]{:S(2)}) collective-permute-start(bf16[2,2,256,768]{3,2,0,1:T(8,128)(2,1)} %bitcast.149), channel_id=1, source_target_pairs={{0,4},{4,0},{8,12},{12,8},{16,20},{20,16},{24,28},{28,24},{1,5},{5... | collective-permute-start | bytes 4718600 | tf_op jit(solution)/shard_map/ppermute | solution.py:323
  600.4 25.3 %collective-permute-start.27 = (bf16[256,2048]{1,0:T(8,128)(2,1)}, bf16[256,2048]{1,0:T(8,128)(2,1)}, u32[]{:S(2)}, u32[]{:S(2)}) collective-permute-start(bf16[256,2048]{1,0:T(8,128)(2,1)} %add_convert_fusion.2), channel_id=1, source_target_pairs={{0,1},{1,3},{3,2},{2,0},{4,5},{5,7},{7,6},{6,4},{8,9},{9,11},{11,1... | collective-permute-start | bytes 3145736 | tf_op jit(solution)/shard_map/ppermute | solution.py:304
  602.5 7.0 collective-permute-start.26
  606.8 31.6 %collective-permute-start.23 = (bf16[2,2,256,768]{3,2,1,0:T(8,128)(2,1)}, bf16[2,2,256,768]{3,2,1,0:T(8,128)(2,1)}, u32[]{:S(2)}, u32[]{:S(2)}) collective-permute-start(bf16[2,2,256,768]{3,2,1,0:T(8,128)(2,1)} %dynamic-slice_bitcast_fusion), channel_id=1, source_target_pairs={{0,4},{4,0},{8,12},{12,8},{16,20},{20,16},{24,28},{28,24},{1,5},{5... | collective-permute-start | bytes 4718600 | tf_op jit(solution)/shard_map/ppermute | solution.py:323
  613.7 29.1 %collective-permute-start.24 = (bf16[2,256,768]{2,1,0:T(8,128)(2,1)}, bf16[2,256,768]{2,1,0:T(8,128)(2,1)}, u32[]{:S(2)}, u32[]{:S(2)}) collective-permute-start(bf16[2,256,768]{2,1,0:T(8,128)(2,1)} %dynamic-slice_bitcast_fusion.2), channel_id=1, source_target_pairs={{0,8},{4,12},{8,0},{12,4},{16,24},{20,28},{24,16},{28,20},{1,9},{5... | collective-permute-start | bytes 2359304 | tf_op jit(solution)/shard_map/ppermute | solution.py:323
  627.2 134.2 %all-gather.19.cloned.1.call-start = ((), (), s32[]{:S(2)}) async-start(), calls=%async_computation.9 | async-start | bytes 7077888 | tf_op jit(solution)/shard_map/all_gather | solution.py:668
  641.4 36.1 %collective-permute-start.25 = (bf16[2,256,768]{2,1,0:T(8,128)(2,1)}, bf16[2,256,768]{2,1,0:T(8,128)(2,1)S(1)}, u32[]{:S(2)}, u32[]{:S(2)}) collective-permute-start(bf16[2,256,768]{2,1,0:T(8,128)(2,1)} %dynamic-slice_bitcast_fusion.1), channel_id=1, source_target_pairs={{0,16},{4,20},{8,24},{12,28},{16,0},{20,4},{24,8},{28,12},{1,17},{... | collective-permute-start | bytes 2359304 | tf_op jit(solution)/shard_map/ppermute | solution.py:323
  661.0 24.7 %collective-permute-start.29 = (bf16[256,2048]{1,0:T(8,128)(2,1)S(1)}, bf16[256,2048]{1,0:T(8,128)(2,1)}, u32[]{:S(2)}, u32[]{:S(2)}) collective-permute-start(bf16[256,2048]{1,0:T(8,128)(2,1)S(1)} %get-tuple-element.99), channel_id=1, source_target_pairs={{0,1},{1,3},{3,2},{2,0},{4,5},{5,7},{7,6},{6,4},{8,9},{9,11},{11,1... | collective-permute-start | bytes 3145736 | tf_op jit(solution)/shard_map/ppermute | solution.py:304
  661.5 21.4 %collective-permute-start.28 = (bf16[256,768]{1,0:T(8,128)(2,1)S(1)}, bf16[256,768]{1,0:T(8,128)(2,1)S(1)}, u32[]{:S(2)}, u32[]{:S(2)}) collective-permute-start(bf16[256,768]{1,0:T(8,128)(2,1)S(1)} %dynamic-slice_bitcast_fusion.4), channel_id=1, source_target_pairs={{0,16},{4,20},{8,24},{12,28},{16,0},{20,4},{24,8},{28,12},{1,17},{... | collective-permute-start | bytes 1179656 | tf_op jit(solution)/shard_map/ppermute | solution.py:323
  677.8 7.8 %collective-permute-start.30 = (bf16[256,768]{1,0:T(8,128)(2,1)S(1)}, bf16[256,768]{1,0:T(8,128)(2,1)S(1)}, u32[]{:S(2)}, u32[]{:S(2)}) collective-permute-start(bf16[256,768]{1,0:T(8,128)(2,1)S(1)} %dynamic-slice_bitcast_fusion.3), channel_id=1, source_target_pairs={{0,8},{4,12},{8,0},{12,4},{16,24},{20,28},{24,16},{28,20},{1,9},{5... | collective-permute-start | bytes 1179656 | tf_op jit(solution)/shard_map/ppermute | solution.py:323
  705.5 44.0 %copy-start.19 = (bf16[256,2048]{1,0:T(8,128)(2,1)S(1)}, bf16[256,2048]{1,0:T(8,128)(2,1)}, u32[]{:S(2)}) copy-start(bf16[256,2048]{1,0:T(8,128)(2,1)} %param.21) | copy-start | bytes 3145732
  705.5 44.0 %copy-start.60 = (f32[1,2048]{1,0:T(1,128)S(1)}, f32[1,2048]{1,0:T(1,128)}, u32[]{:S(2)}) copy-start(f32[1,2048]{1,0:T(1,128)} %copy-done.59) | copy-start | bytes 24580
  705.6 21.8 %collective-permute-start.34 = (bf16[256,2048]{1,0:T(8,128)(2,1)S(1)}, bf16[256,2048]{1,0:T(8,128)(2,1)S(1)}, u32[]{:S(2)}, u32[]{:S(2)}) collective-permute-start(bf16[256,2048]{1,0:T(8,128)(2,1)S(1)} %add_convert_fusion.1), channel_id=1, source_target_pairs={{0,1},{1,3},{3,2},{2,0},{4,5},{5,7},{7,6},{6,4},{8,9},{9,11},{11,1... | collective-permute-start | bytes 3145736 | tf_op jit(solution)/shard_map/ppermute | solution.py:304
  705.6 1.4 collective-permute-start.31
  707.0 4.3 collective-permute-start.32
  711.4 4.3 collective-permute-start.33
  728.7 27.2 %copy-start.23 = (f32[256,2048]{1,0:T(8,128)S(1)}, f32[256,2048]{1,0:T(8,128)}, u32[]{:S(2)}) copy-start(f32[256,2048]{1,0:T(8,128)} %get-tuple-element.139) | copy-start | bytes 6291460
  728.7 27.2 %copy-start.70 = (f32[256]{0:T(256)S(1)}, f32[256]{0:T(256)}, u32[]{:S(2)}) copy-start(f32[256]{0:T(256)} %copy-done.69) | copy-start | bytes 3076
  728.7 27.2 %copy-start.71 = (f32[256]{0:T(256)S(1)}, f32[256]{0:T(256)}, u32[]{:S(2)}) copy-start(f32[256]{0:T(256)} %get-tuple-element.174) | copy-start | bytes 3076
  728.7 20.3 %collective-permute-start.35 = (bf16[256,2048]{1,0:T(8,128)(2,1)}, bf16[256,2048]{1,0:T(8,128)(2,1)}, u32[]{:S(2)}, u32[]{:S(2)}) collective-permute-start(bf16[256,2048]{1,0:T(8,128)(2,1)} %add_convert_fusion), channel_id=1, source_target_pairs={{0,1},{1,3},{3,2},{2,0},{4,5},{5,7},{7,6},{6,4},{8,9},{9,11},{11,1... | collective-permute-start | bytes 3145736 | tf_op jit(solution)/shard_map/ppermute | solution.py:304
  749.1 4.3 collective-permute-start.36
  753.3 6.2 collective-permute-start.37
  (70 other events, 558.5 us)
Sparse Core Ops, SparseCore 0:
  10.5 48.2 all-gather.8
  61.2 28.1 all-gather.10
  91.9 44.3 all-gather.14
  138.6 67.6 all-gather.12
  383.3 86.8 reduce-scatter.4
  474.0 59.0 reduce-scatter.2
  535.8 78.4 all-gather.16
  616.3 63.9 all-gather.22
  682.3 28.2 all-gather.20
  712.5 45.4 all-gather.18

commit v3 on v2

--- a/solution.py
+++ b/solution.py
@@ -354,6 +354,18 @@
         return got
 
 
+def doubled(value, axis, order):
+    known = []
+    for bit in order:
+        got = flip(value, axis, bit)
+        mine = ((lax.axis_index(axis) >> bit) & 1) == 1
+        at = sum(other > bit for other in known)
+        value = jnp.stack([jnp.where(mine, got, value), jnp.where(mine, value, got)], at)
+        known.append(bit)
+        needed = yield value
+        value = after(value, *(needed or ()))
+
+
 def after(value, *needed):
     return lax.optimization_barrier((value, needed))[0] if needed else value
 
@@ -586,16 +598,17 @@
         states,
         (),
     )
-    sum_out = bf16(dot(core, jnp.concatenate(grad_mix, 0), TN))
+    mark = sums[0, 0]
+    ffn_parts[1] = after(ffn_parts[1], grad_mix[-1])
+    ffn_parts[2] = behind(ffn_parts[2], bf16(mark))
+    steps = ring.scatter(ffn_parts)
+    one = next(steps)
+    sum_out = bf16(dot(behind(core, bf16(mark)), jnp.concatenate(grad_mix, 0), TN))
     out_sum = HalvingColumns(sum_out, "dp", order_one)
-    shard_gate_up = behind(f32(shard_gate_up), sums[0, 0])
+    shard_gate_up = behind(f32(shard_gate_up), mark)
     gu_new, gu_first, gu_second = adamw(ffn_in, ffn_in_first, ffn_in_second, shard_gate_up)
     gu_sent = bf16(gu_new)
-
-    ffn_parts[1] = after(ffn_parts[1], grad_mix[-1])
-    steps = ring.scatter(ffn_parts)
-    one = next(steps)
-    done = [out_sum.step(grad_mix[-1])]
+    done = [out_sum.step()]
 
     two = steps.send((grad_proj, *done))
     grad_proj = after(grad_proj, one)
@@ -604,7 +617,7 @@
     in_sums = [Halving(piece, "dp", order) for piece, order in zip(sum_in, (order_one, order_two))]
     done = [out_sum.step(one), *(item.step() for item in in_sums)]
 
-    shard_down = behind(f32(shard_down), sums[0, 0])
+    shard_down = behind(f32(shard_down), f32(sum_in[0][0, 0]))
     down_new, down_first, down_second = adamw(ffn_out, ffn_out_first, ffn_out_second, shard_down)
     down_sent = bf16(down_new)
 
@@ -649,23 +662,32 @@
     shard_in = jnp.stack([shard_in[:, j * channels : (j + 1) * channels] for j in range(3)])
     in_new, in_first, in_second = adamw(mixer_in, mixer_in_first, mixer_in_second, shard_in)
     in_sent = bf16(in_new)
-    vector_sums = sum_all(after(vector_part, one), ("dp",))
+    half = channels // 2
+    spread = [
+        doubled(piece, "dp", order[::-1])
+        for piece, order in zip((in_sent[:, :, :half], in_sent[:, :, half:]), (order_one, order_two))
+    ]
+    for _ in order_one[1:]:
+        in_low = [next(piece) for piece in spread]
+    vector_sums = sum_all(behind(vector_part, f32(two[0, 0])), ("dp",))
 
     gu_low = copied(lax.all_gather(gu_sent, "dp", axis=1, tiled=True))
     one_parts[-1] = behind(one_parts[-1], gu_low[0, 0, 0])
-    three = steps.send((in_sent, vector_sums))
+    three = steps.send(in_low)
     for _ in range(members - 4):
         three = steps.send(())
     grad_one = steps.send(())
     vector_sums = sum_all(after(vector_sums, three), ("mp",))
+    in_low = jnp.concatenate([next(piece) for piece in spread], -1)
+    in_low = jnp.moveaxis(in_low, len(order_one), 0).reshape(3, width, channels)
     input_grad = grad_resid + norm_back(inputs, scale_one, vectors[0], grad_one)
     vectors_grad = vector_sums[:4]
     denom = f32(jnp.sum(lengths)) * width
     stats = jnp.sqrt(vector_sums[4, :3] / denom)
     vec_first, vec_second = moments(vectors_first, vectors_second, vectors_grad)
 
-    down_low, out_low, in_low = (
-        lax.all_gather(new, "dp", axis=1, tiled=True) for new in (down_sent, out_sent, in_sent)
+    down_low, out_low = (
+        lax.all_gather(new, "dp", axis=1, tiled=True) for new in (down_sent, out_sent)
     )
     return (
         bf16(total),

time: 788 us -> 780 us (0.990)
  waiting for transfers between devices: 368 us -> 353 us
    ppermute x14 -> x20, waiting for transfers between devices: 34.4 us -> 84.1 us  [flip(): lax.ppermute(value, axis, [(i, i ^ 1 << bit) for i in range(lax.axis_size...]
    ppermute x24, waiting for transfers between devices: 311 us -> 269 us  [send(): return lax.ppermute(value, self.axis, self.ahead)]
    reduce_scatter x1, waiting for transfers between devices: 22.4 us -> 0.02 us  [body(): lax.psum_scatter(sum_down, 'dp', scatter_dimension=1, tiled=True)]
    ppermute x14 -> x20, starting transfers between devices: 14.4 us -> 17.1 us  [flip(): lax.ppermute(value, axis, [(i, i ^ 1 << bit) for i in range(lax.axis_size...]
    unnamed x175 -> x210, local copies, waits for them, and re-layouts: 22.4 us -> 20.8 us
  transfers between devices with their start and end apart: 48 -> 53, of which waited for: 31 -> 29; matrix products, arithmetic and copies ran while one was open for 32% -> 32% of each run, Pallas kernels for 6% -> 6%
where the time goes in v3:
time: 780 us; the launch traced here: 771 us
  waiting for transfers between devices  353 us (45%)
  matrix products  158 us (20%)
  other arithmetic  106 us (14%)
  Pallas kernels  49.3 us (6%)
  starting transfers between devices  44.2 us (6%)
  local copies, waits for them, and re-layouts  39.4 us (5%)
  between operations  21.2 us (3%)
    ppermute x24, waiting for transfers between devices, send(): return lax.ppermute(value, self.axis, self.ahead)  269 us
    dot_general x37, matrix products, dot(): lax.dot_general(left, right, (dims, ((), ())), preferred_element_type=jnp...  158 us
    ppermute x20, waiting for transfers between devices, flip(): lax.ppermute(value, axis, [(i, i ^ 1 << bit) for i in range(lax.axis_size...  84.1 us
    convert_element_type x23, other arithmetic, bf16(): return value.astype(jnp.bfloat16)  45.7 us
    ppermute x24, starting transfers between devices, send(): return lax.ppermute(value, self.axis, self.ahead)  26.5 us
    unnamed x210, local copies, waits for them, and re-layouts  20.8 us
    pallas_call x1, Pallas kernels, recurrence_backward(): pl.pallas_call(functools.partial(backward_kernel, len(parts)), grid_spec=...  19.3 us
    ppermute x20, starting transfers between devices, flip(): lax.ppermute(value, axis, [(i, i ^ 1 << bit) for i in range(lax.axis_size...  17.1 us
  transfers between devices with their start and end apart: 53, of which 29 were waited for; matrix products, arithmetic and copies ran while one was open for 32% of the time, Pallas kernels for 6%

profile of v3, /device:TPU:0, one launch (start us, length us, event | category | flops | bytes accessed | tf_op | source)
XLA Modules:
  0.0 770.7 jit_solution(3942782657677123808)
XLA Ops:
  19.5 24.3 %collective-permute-done = bf16[256,2048]{1,0:T(8,128)(2,1)} collective-permute-done((bf16[256,2048]{1,0:T(8,128)(2,1)S(1)}, bf16[256,2048]{1,0:T(8,128)(2,1)}, u32[]{:S(2)}, u32[]{:S(2)}) %collective-permute-start) | collective-permute-done | bytes 1048608 | tf_op jit(solution)/shard_map/ppermute | solution.py:304
  48.0 21.3 %collective-permute-done.1 = bf16[256,2048]{1,0:T(8,128)(2,1)} collective-permute-done((bf16[256,2048]{1,0:T(8,128)(2,1)}, bf16[256,2048]{1,0:T(8,128)(2,1)}, u32[]{:S(2)}, u32[]{:S(2)}) %collective-permute-start.1) | collective-permute-done | bytes 1048608 | tf_op jit(solution)/shard_map/ppermute | solution.py:304
  71.0 4.7 fusion.92.refs_0_
  75.8 18.2 %collective-permute-done.2 = bf16[256,2048]{1,0:T(8,128)(2,1)} collective-permute-done((bf16[256,2048]{1,0:T(8,128)(2,1)}, bf16[256,2048]{1,0:T(8,128)(2,1)}, u32[]{:S(2)}, u32[]{:S(2)}) %collective-permute-start.2) | collective-permute-done | bytes 1048608 | tf_op jit(solution)/shard_map/ppermute | solution.py:304
  97.2 3.6 fusion.94.refs_2_
  100.8 3.6 fusion.95.refs_3_
  104.4 12.1 %recurrence_forward.1 = (bf16[1024,512]{1,0:T(8,128)(2,1)S(1)}, f32[1024,512]{1,0:T(8,128)S(1)}, f32[8,4,128,128]{3,2,1,0:T(8,128)S(1)}) custom-call(s32[1]{0:T(128)} %dynamic_slice.56.length, s32[8]{0:T(128)S(1)} %gather_fusion, s32[32]{0:T(128)S(1)} %min.12.part.part_core, s32[8]{0:T(128)S(1)} %fusion.67.core_at.place, f32[256,1536]{1,0:T(8,128)S(1)} %fusion.92.refs_0_, ...), custom_call_target="tpu_custom_call" | custom-call | flops 805306368 | bytes 9437184 | tf_op jit(solution)/shard_map/recurrence_forward/pallas_call | solution.py:127
  119.0 4.3 convolution_convert_fusion.5
  123.5 3.4 collective-permute-start.4
  126.9 20.4 %collective-permute-done.4 = bf16[256,2048]{1,0:T(8,128)(2,1)S(1)} collective-permute-done((bf16[256,2048]{1,0:T(8,128)(2,1)S(1)}, bf16[256,2048]{1,0:T(8,128)(2,1)S(1)}, u32[]{:S(2)}, u32[]{:S(2)}) %collective-permute-start.4) | collective-permute-done | bytes 1048608 | tf_op jit(solution)/shard_map/ppermute | solution.py:304
  150.8 24.0 %collective-permute-done.5 = bf16[256,2048]{1,0:T(8,128)(2,1)S(1)} collective-permute-done((bf16[256,2048]{1,0:T(8,128)(2,1)S(1)}, bf16[256,2048]{1,0:T(8,128)(2,1)S(1)}, u32[]{:S(2)}, u32[]{:S(2)}) %collective-permute-start.5) | collective-permute-done | bytes 1048608 | tf_op jit(solution)/shard_map/ppermute | solution.py:304
  177.9 6.0 fusion.96
  183.9 4.3 fusion.97
  188.2 9.1 %collective-permute-done.10 = bf16[256,2048]{1,0:T(8,128)(2,1)} collective-permute-done((bf16[256,2048]{1,0:T(8,128)(2,1)}, bf16[256,2048]{1,0:T(8,128)(2,1)}, u32[]{:S(2)}, u32[]{:S(2)}) %collective-permute-start.10) | collective-permute-done | bytes 1048608 | tf_op jit(solution)/shard_map/ppermute | solution.py:304
  198.9 20.8 %collective-permute-done.6 = bf16[256,2048]{1,0:T(8,128)(2,1)S(1)} collective-permute-done((bf16[256,2048]{1,0:T(8,128)(2,1)}, bf16[256,2048]{1,0:T(8,128)(2,1)S(1)}, u32[]{:S(2)}, u32[]{:S(2)}) %collective-permute-start.6) | collective-permute-done | bytes 1048608 | tf_op jit(solution)/shard_map/ppermute | solution.py:304
  226.0 4.9 fusion.58
  230.9 6.5 multiply_convert_fusion.12
  241.1 19.4 %collective-permute-done.7 = bf16[256,2048]{1,0:T(8,128)(2,1)} collective-permute-done((bf16[256,2048]{1,0:T(8,128)(2,1)}, bf16[256,2048]{1,0:T(8,128)(2,1)}, u32[]{:S(2)}, u32[]{:S(2)}) %collective-permute-start.7) | collective-permute-done | bytes 1048608 | tf_op jit(solution)/shard_map/ppermute | solution.py:304
  266.3 4.3 multiply_convert_fusion.9
  274.9 13.0 %collective-permute-done.8 = bf16[256,2048]{1,0:T(8,128)(2,1)S(1)} collective-permute-done((bf16[256,2048]{1,0:T(8,128)(2,1)}, bf16[256,2048]{1,0:T(8,128)(2,1)S(1)}, u32[]{:S(2)}, u32[]{:S(2)}) %collective-permute-start.8) | collective-permute-done | bytes 1048608 | tf_op jit(solution)/shard_map/ppermute | solution.py:304
  295.8 5.3 multiply_convert_fusion.6
  304.3 6.2 collective-permute-done.11
  310.4 4.5 add_convert_fusion.6
  316.6 16.3 %collective-permute-done.9 = bf16[256,2048]{1,0:T(8,128)(2,1)S(1)} collective-permute-done((bf16[256,2048]{1,0:T(8,128)(2,1)S(1)}, bf16[256,2048]{1,0:T(8,128)(2,1)S(1)}, u32[]{:S(2)}, u32[]{:S(2)}) %collective-permute-start.9) | collective-permute-done | bytes 1048608 | tf_op jit(solution)/shard_map/ppermute | solution.py:304
  336.5 4.5 multiply_convert_fusion.1
  341.1 5.0 pad_maximum_fusion.5
  346.0 4.8 pad_maximum_fusion.4
  350.8 4.5 fusion.51
  355.3 5.8 add_convert_fusion.5
  361.1 8.3 %fusion.1 = bf16[1,2048,1408]{2,1,0:T(8,128)(2,1)S(1)} fusion(bf16[1024,1408]{1,0:T(8,128)(2,1)S(1)} %pad_maximum_fusion.5, bf16[256,2048]{1,0:T(8,128)(2,1)S(1)} %collective-permute-done.9, bf16[256,2048]{1,0:T(8,128)(2,1)S(1)} %collective-permute-done.8, bf16[256,2048]{1,0:T(8,128)(2,1)} %collective-permute-done.7, bf16[256,2048]{1,0:T(8,128)(2,1)} %multiply_convert_fusion), kind=kOutput, calls=%fused_computation.6 | convolution fusion | flops 5925240832 | bytes 12845056 | tf_op jit(solution)/shard_map/dot_general | solution.py:36
  369.5 8.6 %fusion = bf16[1,2048,1408]{2,1,0:T(8,128)(2,1)S(1)} fusion(bf16[1024,1408]{1,0:T(8,128)(2,1)S(1)} %pad_maximum_fusion.4, bf16[256,2048]{1,0:T(8,128)(2,1)S(1)} %collective-permute-done.9, bf16[256,2048]{1,0:T(8,128)(2,1)S(1)} %collective-permute-done.8, bf16[256,2048]{1,0:T(8,128)(2,1)} %collective-permute-done.7, bf16[256,2048]{1,0:T(8,128)(2,1)} %multiply_convert_fusion), kind=kOutput, calls=%fused_computation.5 | convolution fusion | flops 5925240832 | bytes 12845056 | tf_op jit(solution)/shard_map/dot_general | solution.py:36
  378.1 5.0 pad_maximum_fusion
  386.8 9.7 %convolution_convert_fusion = bf16[1408,2048]{1,0:T(8,128)(2,1)} fusion(bf16[1024,1408]{1,0:T(8,128)(2,1)S(1)} %pad_maximum_fusion.3, bf16[256,2048]{1,0:T(8,128)(2,1)} %collective-permute-done.13, bf16[256,2048]{1,0:T(8,128)(2,1)} %collective-permute-done.10, bf16[256,2048]{1,0:T(8,128)(2,1)} %collective-permute-done.3, bf16[256,2048]{1,0:T(8,128)(2,1)} %fusion.38), kind=kOutput, calls=%fused_computation.2 | convolution fusion | flops 5925240832 | bytes 12845056 | tf_op jit(solution)/shard_map/dot_general | solution.py:36
  397.7 3.6 collective-permute-done.14
  404.1 3.8 fusion.88
  411.6 4.0 permute_columns.3
  418.2 17.6 %collective-permute-done.15 = bf16[256,2048]{1,0:T(8,128)(2,1)} collective-permute-done((bf16[256,2048]{1,0:T(8,128)(2,1)}, bf16[256,2048]{1,0:T(8,128)(2,1)}, u32[]{:S(2)}, u32[]{:S(2)}) %collective-permute-start.15) | collective-permute-done | bytes 1048608 | tf_op jit(solution)/shard_map/ppermute | solution.py:304
  435.8 9.2 %convolution_convert_fusion.4 = bf16[1024,2048]{1,0:T(8,128)(2,1)S(1)} fusion(bf16[1024,1408]{1,0:T(8,128)(2,1)S(1)} %copy-done.51, bf16[1408,2048]{1,0:T(8,128)(2,1)} %all-gather.14.cloned.1.call-done), kind=kOutput, calls=%fused_computation.36 | convolution fusion | flops 5907677184 | bytes 12845056 | tf_op jit(solution)/shard_map/dot_general | solution.py:36
  450.4 11.7 %collective-permute-done.16 = bf16[256,2048]{1,0:T(8,128)(2,1)S(1)} collective-permute-done((bf16[256,2048]{1,0:T(8,128)(2,1)}, bf16[256,2048]{1,0:T(8,128)(2,1)S(1)}, u32[]{:S(2)}, u32[]{:S(2)}) %collective-permute-start.16) | collective-permute-done | bytes 1048608 | tf_op jit(solution)/shard_map/ppermute | solution.py:304
  462.9 14.9 %collective-permute-done.17 = bf16[256,2048]{1,0:T(8,128)(2,1)S(1)} collective-permute-done((bf16[256,2048]{1,0:T(8,128)(2,1)S(1)}, bf16[256,2048]{1,0:T(8,128)(2,1)S(1)}, u32[]{:S(2)}, u32[]{:S(2)}) %collective-permute-start.17) | collective-permute-done | bytes 1048608 | tf_op jit(solution)/shard_map/ppermute | solution.py:304
  478.8 19.3 %recurrence_backward.1 = (bf16[1024,1536]{1,0:T(8,128)(2,1)S(1)}, f32[8,512]{1,0:T(8,128)S(1)}) custom-call(s32[1]{0:T(128)} %dynamic_slice.56.length, s32[8]{0:T(128)S(1)} %gather_fusion, s32[32]{0:T(128)S(1)} %min.12.part.part_core, s32[8]{0:T(128)S(1)} %fusion.67.core_at.place, s32[8]{0:T(128)S(1)} %gather_fusion, s32[32]{0:T(128)S(1)} %min.12.part.part_core, ...), custom_call_target="tpu_custom_call" | custom-call | flops 2684354560 | bytes 13631488 | tf_op jit(solution)/shard_map/recurrence_backward/pallas_call | solution.py:254
  500.8 9.2 %fusion.86 = (bf16[2,256,1408]{2,1,0:T(8,128)(2,1)}, f32[2,256,1408]{2,1,0:T(8,128)}, f32[2,256,1408]{2,1,0:T(8,128)}, f32[2,256,1408]{2,1,0:T(8,128)}, f32[2,256,1408]{2,1,0:T(8,128)}) fusion(f32[2,256,1408]{2,1,0:T(8,128)} %param.33, f32[2,256,1408]{2,1,0:T(8,128)} %param.34, f32[2,256,1408]{2,1,0:T(8,128)} %param.35, ...), kind=kLoop, calls=%fused_computation.240 | loop fusion | flops 12976128 | bytes 23068676 | tf_op jit(solution)/shard_map/convert_element_type | solution.py:28
  510.9 3.2 fusion.89
  514.3 3.8 fusion.19
  519.2 10.7 %collective-permute-done.18 = bf16[256,2048]{1,0:T(8,128)(2,1)S(1)} collective-permute-done((bf16[256,2048]{1,0:T(8,128)(2,1)S(1)}, bf16[256,2048]{1,0:T(8,128)(2,1)S(1)}, u32[]{:S(2)}, u32[]{:S(2)}) %collective-permute-start.18) | collective-permute-done | bytes 1048608 | tf_op jit(solution)/shard_map/ppermute | solution.py:304
  530.9 5.5 convolution_convert_fusion.7
  539.9 5.2 fusion.84
  545.5 3.5 constant_dynamic-slice_fusion
  551.4 5.4 convolution_convert_fusion.6
  563.5 3.2 collective-permute-start.21
  566.8 21.8 %collective-permute-done.21 = bf16[512,512]{1,0:T(8,128)(2,1)} collective-permute-done((bf16[512,512]{1,0:T(8,128)(2,1)}, bf16[512,512]{1,0:T(8,128)(2,1)}, u32[]{:S(2)}, u32[]{:S(2)}) %collective-permute-start.21) | collective-permute-done | bytes 524320 | tf_op jit(solution)/shard_map/ppermute | solution.py:323
  600.5 8.2 %convolution_convert_fusion.3 = bf16[1024,2048]{1,0:T(8,128)(2,1)} fusion(bf16[1024,1536]{1,0:T(8,128)(2,1)S(1)} %copy-done.13, bf16[2048,1536]{1,0:T(8,128)(2,1)S(1)} %bitcast.186), kind=kOutput, calls=%fused_computation.35 | convolution fusion | flops 6444548096 | bytes 13631488 | tf_op jit(solution)/shard_map/dot_general | solution.py:36
  609.6 16.3 %collective-permute-done.24 = bf16[2,256,768]{2,1,0:T(8,128)(2,1)S(1)} collective-permute-done((bf16[2,256,768]{2,1,0:T(8,128)(2,1)S(1)}, bf16[2,256,768]{2,1,0:T(8,128)(2,1)S(1)}, u32[]{:S(2)}, u32[]{:S(2)}) %collective-permute-start.24) | collective-permute-done | bytes 786464 | tf_op jit(solution)/shard_map/ppermute | solution.py:323
  631.0 10.9 %copied.1 = bf16[2,2048,1408]{2,1,0:T(8,128)(2,1)} custom-call(bf16[2,2048,1408]{2,1,0:T(8,128)(2,1)} %all-gather.16.cloned.1.call-done.value), custom_call_target="tpu_custom_call" | custom-call | tf_op jit(solution)/shard_map/copied/pallas_call | solution.py:425
  643.8 3.8 broadcast_select_fusion
  653.1 11.9 %collective-permute-done.30 = bf16[256,768]{1,0:T(8,128)(2,1)} collective-permute-done((bf16[256,768]{1,0:T(8,128)(2,1)}, bf16[256,768]{1,0:T(8,128)(2,1)}, u32[]{:S(2)}, u32[]{:S(2)}) %collective-permute-start.30) | collective-permute-done | bytes 393248 | tf_op jit(solution)/shard_map/ppermute | solution.py:323
  666.3 6.3 collective-permute-done.29
  672.9 3.4 fusion.80
  679.9 4.0 fusion.27
  692.2 21.2 %collective-permute-done.32 = bf16[2,3,256,256]{3,2,1,0:T(8,128)(2,1)S(1)} collective-permute-done((bf16[2,3,256,256]{3,2,1,0:T(8,128)(2,1)S(1)}, bf16[2,3,256,256]{3,2,1,0:T(8,128)(2,1)S(1)}, u32[]{:S(2)}, u32[]{:S(2)}) %collective-permute-start.32) | collective-permute-done | bytes 786464 | tf_op jit(solution)/shard_map/ppermute | solution.py:323
  721.9 3.8 collective-permute-done.38
  730.6 11.1 %collective-permute-done.36 = bf16[256,2048]{1,0:T(8,128)(2,1)} collective-permute-done((bf16[256,2048]{1,0:T(8,128)(2,1)}, bf16[256,2048]{1,0:T(8,128)(2,1)}, u32[]{:S(2)}, u32[]{:S(2)}) %collective-permute-start.36) | collective-permute-done | bytes 1048608 | tf_op jit(solution)/shard_map/ppermute | solution.py:304
  746.8 3.7 fusion.35
  755.9 3.8 copy.56
  (414 shorter events, 168.8 us)
Async XLA Ops:
  7.2 63.8 %all-gather.8.cloned.1.call-start = ((), (), s32[]{:S(2)}) async-start(), calls=%async_computation.2 | async-start | bytes 7077888 | tf_op jit(solution)/shard_map/all_gather | solution.py:510
  9.8 109.2 %all-gather.10.cloned.1.call-start = ((), (), s32[]{:S(2)}) async-start(), calls=%async_computation.3 | async-start | bytes 2359296 | tf_op jit(solution)/shard_map/all_gather | solution.py:512
  10.6 167.3 %all-gather.14.cloned.1.call-start = ((), (), s32[]{:S(2)}) async-start(), calls=%async_computation.5 | async-start | bytes 6488064 | tf_op jit(solution)/shard_map/all_gather | solution.py:514
  11.6 214.4 %all-gather.12.cloned.1.call-start = ((), (), s32[]{:S(2)}) async-start(), calls=%async_computation.4 | async-start | bytes 12976128 | tf_op jit(solution)/shard_map/all_gather | solution.py:513
  14.8 30.5 %copy-start.91 = (s32[8]{0:T(128)S(1)}, s32[8]{0:T(128)}, u32[]{:S(2)}) copy-start(s32[8]{0:T(128)} %param.23) | copy-start | bytes 100
  14.9 55.0 %copy-start.41 = (bf16[256,2048]{1,0:T(8,128)(2,1)S(1)}, bf16[256,2048]{1,0:T(8,128)(2,1)}, u32[]{:S(2)}) copy-start(bf16[256,2048]{1,0:T(8,128)(2,1)} %param.22) | copy-start | bytes 3145732
  14.9 486.0 %reduce-scatter.5.cloned.1.call-start = ((), (), s32[]{:S(2)}) async-start(), calls=%async_computation.7 | async-start | bytes 12976128 | tf_op jit(solution)/shard_map/reduce_scatter | solution.py:570
  15.8 31.4 %copy-start.83 = (f32[256]{0:T(256)}, f32[256]{0:T(256)S(1)}, u32[]{:S(2)}) copy-start(f32[256]{0:T(256)S(1)} %get-tuple-element.186) | copy-start | bytes 3076
  16.4 59.3 %copy-start.65 = (bf16[256,2048]{1,0:T(8,128)(2,1)}, bf16[256,2048]{1,0:T(8,128)(2,1)S(1)}, u32[]{:S(2)}) copy-start(bf16[256,2048]{1,0:T(8,128)(2,1)S(1)} %fusion.32) | copy-start | bytes 3145732
  16.4 27.3 %collective-permute-start = (bf16[256,2048]{1,0:T(8,128)(2,1)S(1)}, bf16[256,2048]{1,0:T(8,128)(2,1)}, u32[]{:S(2)}, u32[]{:S(2)}) collective-permute-start(bf16[256,2048]{1,0:T(8,128)(2,1)S(1)} %fusion.32), channel_id=1, source_target_pairs={{0,1},{1,3},{3,2},{2,0},{4,5},{5,7},{7,6},{6,4},{8,9},{9,11},{11,1... | collective-permute-start | bytes 3145736 | tf_op jit(solution)/shard_map/ppermute | solution.py:304
  43.7 25.6 %collective-permute-start.1 = (bf16[256,2048]{1,0:T(8,128)(2,1)}, bf16[256,2048]{1,0:T(8,128)(2,1)}, u32[]{:S(2)}, u32[]{:S(2)}) collective-permute-start(bf16[256,2048]{1,0:T(8,128)(2,1)} %collective-permute-done), channel_id=1, source_target_pairs={{0,1},{1,3},{3,2},{2,0},{4,5},{5,7},{7,6},{6,4},{8,9},{9,11},{11,1... | collective-permute-start | bytes 3145736 | tf_op jit(solution)/shard_map/ppermute | solution.py:304
  69.3 24.6 %collective-permute-start.2 = (bf16[256,2048]{1,0:T(8,128)(2,1)}, bf16[256,2048]{1,0:T(8,128)(2,1)}, u32[]{:S(2)}, u32[]{:S(2)}) collective-permute-start(bf16[256,2048]{1,0:T(8,128)(2,1)} %collective-permute-done.1), channel_id=1, source_target_pairs={{0,1},{1,3},{3,2},{2,0},{4,5},{5,7},{7,6},{6,4},{8,9},{9,11},{11,1... | collective-permute-start | bytes 3145736 | tf_op jit(solution)/shard_map/ppermute | solution.py:304
  93.9 29.5 %collective-permute-start.3 = (bf16[256,2048]{1,0:T(8,128)(2,1)}, bf16[256,2048]{1,0:T(8,128)(2,1)}, u32[]{:S(2)}, u32[]{:S(2)}) collective-permute-start(bf16[256,2048]{1,0:T(8,128)(2,1)} %fusion.38), channel_id=1, source_target_pairs={{0,1},{1,3},{3,2},{2,0},{4,5},{5,7},{7,6},{6,4},{8,9},{9,11},{11,1... | collective-permute-start | bytes 3145736 | tf_op jit(solution)/shard_map/ppermute | solution.py:304
  123.4 51.4 %copy-start.35 = (bf16[1024,2048]{1,0:T(8,128)(2,1)}, bf16[1024,2048]{1,0:T(8,128)(2,1)S(1)}, u32[]{:S(2)}) copy-start(bf16[1024,2048]{1,0:T(8,128)(2,1)S(1)} %convolution_convert_fusion.5) | copy-start | bytes 12582916
  123.5 23.8 %collective-permute-start.4 = (bf16[256,2048]{1,0:T(8,128)(2,1)S(1)}, bf16[256,2048]{1,0:T(8,128)(2,1)S(1)}, u32[]{:S(2)}, u32[]{:S(2)}) collective-permute-start(bf16[256,2048]{1,0:T(8,128)(2,1)S(1)} %slice.204), channel_id=1, source_target_pairs={{0,1},{1,3},{3,2},{2,0},{4,5},{5,7},{7,6},{6,4},{8,9},{9,11},{11,1... | collective-permute-start | bytes 3145736 | tf_op jit(solution)/shard_map/ppermute | solution.py:304
  147.7 27.0 %collective-permute-start.5 = (bf16[256,2048]{1,0:T(8,128)(2,1)S(1)}, bf16[256,2048]{1,0:T(8,128)(2,1)S(1)}, u32[]{:S(2)}, u32[]{:S(2)}) collective-permute-start(bf16[256,2048]{1,0:T(8,128)(2,1)S(1)} %add_convert_fusion.8), channel_id=1, source_target_pairs={{0,1},{1,3},{3,2},{2,0},{4,5},{5,7},{7,6},{6,4},{8,9},{9,11},{11,1... | collective-permute-start | bytes 3145736 | tf_op jit(solution)/shard_map/ppermute | solution.py:304
  150.2 47.1 %collective-permute-start.10 = (bf16[256,2048]{1,0:T(8,128)(2,1)}, bf16[256,2048]{1,0:T(8,128)(2,1)}, u32[]{:S(2)}, u32[]{:S(2)}) collective-permute-start(bf16[256,2048]{1,0:T(8,128)(2,1)} %collective-permute-done.3), channel_id=1, source_target_pairs={{0,1},{1,3},{3,2},{2,0},{4,5},{5,7},{7,6},{6,4},{8,9},{9,11},{11,1... | collective-permute-start | bytes 3145736 | tf_op jit(solution)/shard_map/ppermute | solution.py:304
  176.1 43.6 %collective-permute-start.6 = (bf16[256,2048]{1,0:T(8,128)(2,1)}, bf16[256,2048]{1,0:T(8,128)(2,1)S(1)}, u32[]{:S(2)}, u32[]{:S(2)}) collective-permute-start(bf16[256,2048]{1,0:T(8,128)(2,1)} %add_convert_fusion.7), channel_id=1, source_target_pairs={{0,1},{1,3},{3,2},{2,0},{4,5},{5,7},{7,6},{6,4},{8,9},{9,11},{11,1... | collective-permute-start | bytes 3145736 | tf_op jit(solution)/shard_map/ppermute | solution.py:304
  183.9 35.8 %copy-start.20 = (bf16[256,2048]{1,0:T(8,128)(2,1)S(1)}, bf16[256,2048]{1,0:T(8,128)(2,1)}, u32[]{:S(2)}) copy-start(bf16[256,2048]{1,0:T(8,128)(2,1)} %param.21) | copy-start | bytes 3145732
  197.3 139.2 %collective-permute-start.13 = (bf16[256,2048]{1,0:T(8,128)(2,1)}, bf16[256,2048]{1,0:T(8,128)(2,1)}, u32[]{:S(2)}, u32[]{:S(2)}) collective-permute-start(bf16[256,2048]{1,0:T(8,128)(2,1)} %collective-permute-done.10), channel_id=1, source_target_pairs={{0,1},{1,3},{3,2},{2,0},{4,5},{5,7},{7,6},{6,4},{8,9},{9,11},{11,1... | collective-permute-start | bytes 3145736 | tf_op jit(solution)/shard_map/ppermute | solution.py:304
  224.4 36.1 %collective-permute-start.7 = (bf16[256,2048]{1,0:T(8,128)(2,1)}, bf16[256,2048]{1,0:T(8,128)(2,1)}, u32[]{:S(2)}, u32[]{:S(2)}) collective-permute-start(bf16[256,2048]{1,0:T(8,128)(2,1)} %multiply_convert_fusion), channel_id=1, source_target_pairs={{0,1},{1,3},{3,2},{2,0},{4,5},{5,7},{7,6},{6,4},{8,9},{9,11},{11,1... | collective-permute-start | bytes 3145736 | tf_op jit(solution)/shard_map/ppermute | solution.py:304
  260.5 27.4 %collective-permute-start.8 = (bf16[256,2048]{1,0:T(8,128)(2,1)}, bf16[256,2048]{1,0:T(8,128)(2,1)S(1)}, u32[]{:S(2)}, u32[]{:S(2)}) collective-permute-start(bf16[256,2048]{1,0:T(8,128)(2,1)} %collective-permute-done.7), channel_id=1, source_target_pairs={{0,1},{1,3},{3,2},{2,0},{4,5},{5,7},{7,6},{6,4},{8,9},{9,11},{11,1... | collective-permute-start | bytes 3145736 | tf_op jit(solution)/shard_map/ppermute | solution.py:304
  274.3 36.1 %collective-permute-start.11 = (bf16[256,2048]{1,0:T(8,128)(2,1)S(1)}, bf16[256,2048]{1,0:T(8,128)(2,1)S(1)}, u32[]{:S(2)}, u32[]{:S(2)}) collective-permute-start(bf16[256,2048]{1,0:T(8,128)(2,1)S(1)} %fusion.24), channel_id=1, source_target_pairs={{0,1},{1,3},{3,2},{2,0},{4,5},{5,7},{7,6},{6,4},{8,9},{9,11},{11,1... | collective-permute-start | bytes 3145736 | tf_op jit(solution)/shard_map/ppermute | solution.py:304
  288.0 44.9 %collective-permute-start.9 = (bf16[256,2048]{1,0:T(8,128)(2,1)S(1)}, bf16[256,2048]{1,0:T(8,128)(2,1)S(1)}, u32[]{:S(2)}, u32[]{:S(2)}) collective-permute-start(bf16[256,2048]{1,0:T(8,128)(2,1)S(1)} %collective-permute-done.8), channel_id=1, source_target_pairs={{0,1},{1,3},{3,2},{2,0},{4,5},{5,7},{7,6},{6,4},{8,9},{9,11},{11,1... | collective-permute-start | bytes 3145736 | tf_op jit(solution)/shard_map/ppermute | solution.py:304
  314.9 40.4 %collective-permute-start.12 = (bf16[256,2048]{1,0:T(8,128)(2,1)}, bf16[256,2048]{1,0:T(8,128)(2,1)}, u32[]{:S(2)}, u32[]{:S(2)}) collective-permute-start(bf16[256,2048]{1,0:T(8,128)(2,1)} %add_convert_fusion.6), channel_id=1, source_target_pairs={{0,1},{1,3},{3,2},{2,0},{4,5},{5,7},{7,6},{6,4},{8,9},{9,11},{11,1... | collective-permute-start | bytes 3145736 | tf_op jit(solution)/shard_map/ppermute | solution.py:304
  383.1 156.8 %reduce-scatter.3.cloned.1.call-start = ((), (), s32[]{:S(2)}) async-start(), calls=%async_computation.6 | async-start | bytes 6488064 | tf_op jit(solution)/shard_map/reduce_scatter | solution.py:573
  385.2 16.1 %collective-permute-start.14 = (bf16[256,2048]{1,0:T(8,128)(2,1)}, bf16[256,2048]{1,0:T(8,128)(2,1)}, u32[]{:S(2)}, u32[]{:S(2)}) collective-permute-start(bf16[256,2048]{1,0:T(8,128)(2,1)} %add_convert_fusion.5), channel_id=1, source_target_pairs={{0,1},{1,3},{3,2},{2,0},{4,5},{5,7},{7,6},{6,4},{8,9},{9,11},{11,1... | collective-permute-start | bytes 3145736 | tf_op jit(solution)/shard_map/ppermute | solution.py:304
  396.5 234.4 %all-gather.16.cloned.1.call-start = ((), (), s32[]{:S(2)}) async-start(), calls=%async_computation.8 | async-start | bytes 12976128 | tf_op jit(solution)/shard_map/all_gather | solution.py:674
  410.9 24.9 %collective-permute-start.15 = (bf16[256,2048]{1,0:T(8,128)(2,1)}, bf16[256,2048]{1,0:T(8,128)(2,1)}, u32[]{:S(2)}, u32[]{:S(2)}) collective-permute-start(bf16[256,2048]{1,0:T(8,128)(2,1)} %permute_columns.2), channel_id=1, source_target_pairs={{0,1},{1,3},{3,2},{2,0},{4,5},{5,7},{7,6},{6,4},{8,9},{9,11},{11,1... | collective-permute-start | bytes 3145736 | tf_op jit(solution)/shard_map/ppermute | solution.py:304
  435.8 26.3 %collective-permute-start.16 = (bf16[256,2048]{1,0:T(8,128)(2,1)}, bf16[256,2048]{1,0:T(8,128)(2,1)S(1)}, u32[]{:S(2)}, u32[]{:S(2)}) collective-permute-start(bf16[256,2048]{1,0:T(8,128)(2,1)} %collective-permute-done.15), channel_id=1, source_target_pairs={{0,1},{1,3},{3,2},{2,0},{4,5},{5,7},{7,6},{6,4},{8,9},{9,11},{11,1... | collective-permute-start | bytes 3145736 | tf_op jit(solution)/shard_map/ppermute | solution.py:304
  448.1 30.6 %copy-start.9 = (f32[8,4,128,128]{3,2,1,0:T(8,128)S(1)}, f32[8,4,128,128]{3,2,1,0:T(8,128)}, u32[]{:S(2)}) copy-start(f32[8,4,128,128]{3,2,1,0:T(8,128)} %copy-done.8) | copy-start | bytes 6291460
  462.1 15.7 %collective-permute-start.17 = (bf16[256,2048]{1,0:T(8,128)(2,1)S(1)}, bf16[256,2048]{1,0:T(8,128)(2,1)S(1)}, u32[]{:S(2)}, u32[]{:S(2)}) collective-permute-start(bf16[256,2048]{1,0:T(8,128)(2,1)S(1)} %collective-permute-done.16), channel_id=1, source_target_pairs={{0,1},{1,3},{3,2},{2,0},{4,5},{5,7},{7,6},{6,4},{8,9},{9,11},{11,1... | collective-permute-start | bytes 3145736 | tf_op jit(solution)/shard_map/ppermute | solution.py:304
  510.1 217.7 %all-gather.20.cloned.1.call-start = ((), (), s32[]{:S(2)}) async-start(), calls=%async_computation.10 | async-start | bytes 6488064 | tf_op jit(solution)/shard_map/all_gather | solution.py:690
  514.1 15.8 %collective-permute-start.18 = (bf16[256,2048]{1,0:T(8,128)(2,1)S(1)}, bf16[256,2048]{1,0:T(8,128)(2,1)S(1)}, u32[]{:S(2)}, u32[]{:S(2)}) collective-permute-start(bf16[256,2048]{1,0:T(8,128)(2,1)S(1)} %get-tuple-element.84), channel_id=1, source_target_pairs={{0,1},{1,3},{3,2},{2,0},{4,5},{5,7},{7,6},{6,4},{8,9},{9,11},{11,1... | collective-permute-start | bytes 3145736 | tf_op jit(solution)/shard_map/ppermute | solution.py:304
  519.2 26.3 %collective-permute-start.19 = (bf16[512,1024]{1,0:T(8,128)(2,1)}, bf16[512,1024]{1,0:T(8,128)(2,1)}, u32[]{:S(2)}, u32[]{:S(2)}) collective-permute-start(bf16[512,1024]{1,0:T(8,128)(2,1)} %slice.210), channel_id=1, source_target_pairs={{0,4},{4,0},{8,12},{12,8},{16,20},{20,16},{24,28},{28,24},{1,5},{5... | collective-permute-start | bytes 3145736 | tf_op jit(solution)/shard_map/ppermute | solution.py:323
  545.2 182.6 %all-gather.18.cloned.1.call-start = ((), (), s32[]{:S(2)}) async-start(), calls=%async_computation.9 | async-start | bytes 2359296 | tf_op jit(solution)/shard_map/all_gather | solution.py:690
  550.2 41.1 %collective-permute-start.22 = (bf16[2,2,256,768]{3,2,0,1:T(8,128)(2,1)}, bf16[2,2,256,768]{3,2,0,1:T(8,128)(2,1)}, u32[]{:S(2)}, u32[]{:S(2)}) collective-permute-start(bf16[2,2,256,768]{3,2,0,1:T(8,128)(2,1)} %bitcast.181), channel_id=1, source_target_pairs={{0,4},{4,0},{8,12},{12,8},{16,20},{20,16},{24,28},{28,24},{1,5},{5... | collective-permute-start | bytes 4718600 | tf_op jit(solution)/shard_map/ppermute | solution.py:323
  558.1 37.9 %collective-permute-start.23 = (bf16[2,2,256,768]{3,2,1,0:T(8,128)(2,1)}, bf16[2,2,256,768]{3,2,1,0:T(8,128)(2,1)}, u32[]{:S(2)}, u32[]{:S(2)}) collective-permute-start(bf16[2,2,256,768]{3,2,1,0:T(8,128)(2,1)} %dynamic-slice_bitcast_fusion), channel_id=1, source_target_pairs={{0,4},{4,0},{8,12},{12,8},{16,20},{20,16},{24,28},{28,24},{1,5},{5... | collective-permute-start | bytes 4718600 | tf_op jit(solution)/shard_map/ppermute | solution.py:323
  560.2 29.6 %collective-permute-start.20 = (bf16[256,2048]{1,0:T(8,128)(2,1)}, bf16[256,2048]{1,0:T(8,128)(2,1)}, u32[]{:S(2)}, u32[]{:S(2)}) collective-permute-start(bf16[256,2048]{1,0:T(8,128)(2,1)} %add_convert_fusion.4), channel_id=1, source_target_pairs={{0,1},{1,3},{3,2},{2,0},{4,5},{5,7},{7,6},{6,4},{8,9},{9,11},{11,1... | collective-permute-start | bytes 3145736 | tf_op jit(solution)/shard_map/ppermute | solution.py:304
  560.9 39.5 %slice-start = ((s8[6291456]{0:T(1024)(128)(4,1)}), s8[2097152]{0:T(1024)(128)(4,1)S(1)}, s32[]{:S(2)}) async-start(s8[6291456]{0:T(1024)(128)(4,1)} %bitcast.185), calls=%async_computation.11 | async-start | bytes 4194304
  563.5 25.0 %collective-permute-start.21 = (bf16[512,512]{1,0:T(8,128)(2,1)}, bf16[512,512]{1,0:T(8,128)(2,1)}, u32[]{:S(2)}, u32[]{:S(2)}) collective-permute-start(bf16[512,512]{1,0:T(8,128)(2,1)} %slice.216), channel_id=1, source_target_pairs={{0,8},{4,12},{8,0},{12,4},{16,24},{20,28},{24,16},{28,20},{1,9},{5... | collective-permute-start | bytes 1572872 | tf_op jit(solution)/shard_map/ppermute | solution.py:323
  589.8 18.9 %collective-permute-start.26 = (bf16[512,256]{1,0:T(8,128)(2,1)S(1)}, bf16[512,256]{1,0:T(8,128)(2,1)S(1)}, u32[]{:S(2)}, u32[]{:S(2)}) collective-permute-start(bf16[512,256]{1,0:T(8,128)(2,1)S(1)} %slice.218), channel_id=1, source_target_pairs={{0,16},{4,20},{8,24},{12,28},{16,0},{20,4},{24,8},{28,12},{1,17},{... | collective-permute-start | bytes 786440 | tf_op jit(solution)/shard_map/ppermute | solution.py:323
  593.4 32.4 %collective-permute-start.24 = (bf16[2,256,768]{2,1,0:T(8,128)(2,1)S(1)}, bf16[2,256,768]{2,1,0:T(8,128)(2,1)S(1)}, u32[]{:S(2)}, u32[]{:S(2)}) collective-permute-start(bf16[2,256,768]{2,1,0:T(8,128)(2,1)S(1)} %dynamic-slice_bitcast_fusion.2), channel_id=1, source_target_pairs={{0,8},{4,12},{8,0},{12,4},{16,24},{20,28},{24,16},{28,20},{1,9},{5... | collective-permute-start | bytes 2359304 | tf_op jit(solution)/shard_map/ppermute | solution.py:323
  597.9 28.2 %collective-permute-start.25 = (bf16[2,256,768]{2,1,0:T(8,128)(2,1)S(1)}, bf16[2,256,768]{2,1,0:T(8,128)(2,1)S(1)}, u32[]{:S(2)}, u32[]{:S(2)}) collective-permute-start(bf16[2,256,768]{2,1,0:T(8,128)(2,1)S(1)} %dynamic-slice_bitcast_fusion.1), channel_id=1, source_target_pairs={{0,16},{4,20},{8,24},{12,28},{16,0},{20,4},{24,8},{28,12},{1,17},{... | collective-permute-start | bytes 2359304 | tf_op jit(solution)/shard_map/ppermute | solution.py:323
  600.4 26.8 %collective-permute-start.27 = (bf16[256,2048]{1,0:T(8,128)(2,1)S(1)}, bf16[256,2048]{1,0:T(8,128)(2,1)S(1)}, u32[]{:S(2)}, u32[]{:S(2)}) collective-permute-start(bf16[256,2048]{1,0:T(8,128)(2,1)S(1)} %add_convert_fusion.2), channel_id=1, source_target_pairs={{0,1},{1,3},{3,2},{2,0},{4,5},{5,7},{7,6},{6,4},{8,9},{9,11},{11,1... | collective-permute-start | bytes 3145736 | tf_op jit(solution)/shard_map/ppermute | solution.py:304
  627.1 24.8 %collective-permute-start.28 = (bf16[256,768]{1,0:T(8,128)(2,1)S(1)}, bf16[256,768]{1,0:T(8,128)(2,1)}, u32[]{:S(2)}, u32[]{:S(2)}) collective-permute-start(bf16[256,768]{1,0:T(8,128)(2,1)S(1)} %dynamic-slice_bitcast_fusion.4), channel_id=1, source_target_pairs={{0,16},{4,20},{8,24},{12,28},{16,0},{20,4},{24,8},{28,12},{1,17},{... | collective-permute-start | bytes 1179656 | tf_op jit(solution)/shard_map/ppermute | solution.py:323
  647.6 25.0 %collective-permute-start.29 = (bf16[256,2048]{1,0:T(8,128)(2,1)}, bf16[256,2048]{1,0:T(8,128)(2,1)}, u32[]{:S(2)}, u32[]{:S(2)}) collective-permute-start(bf16[256,2048]{1,0:T(8,128)(2,1)} %get-tuple-element.96), channel_id=1, source_target_pairs={{0,1},{1,3},{3,2},{2,0},{4,5},{5,7},{7,6},{6,4},{8,9},{9,11},{11,1... | collective-permute-start | bytes 3145736 | tf_op jit(solution)/shard_map/ppermute | solution.py:304
  648.6 16.3 %collective-permute-start.30 = (bf16[256,768]{1,0:T(8,128)(2,1)}, bf16[256,768]{1,0:T(8,128)(2,1)}, u32[]{:S(2)}, u32[]{:S(2)}) collective-permute-start(bf16[256,768]{1,0:T(8,128)(2,1)} %dynamic-slice_bitcast_fusion.3), channel_id=1, source_target_pairs={{0,8},{4,12},{8,0},{12,4},{16,24},{20,28},{24,16},{28,20},{1,9},{5... | collective-permute-start | bytes 1179656 | tf_op jit(solution)/shard_map/ppermute | solution.py:323
  677.3 9.0 %collective-permute-start.33 = (bf16[3,256,256]{2,1,0:T(8,128)(2,1)}, bf16[3,256,256]{2,1,0:T(8,128)(2,1)}, u32[]{:S(2)}, u32[]{:S(2)}) collective-permute-start(bf16[3,256,256]{2,1,0:T(8,128)(2,1)} %get-tuple-element.173), channel_id=1, source_target_pairs={{0,8},{4,12},{8,0},{12,4},{16,24},{20,28},{24,16},{28,20},{1,9},{5... | collective-permute-start | bytes 1179656 | tf_op jit(solution)/shard_map/ppermute | solution.py:323
  678.9 8.7 %collective-permute-start.31 = (bf16[3,256,256]{2,1,0:T(8,128)(2,1)}, bf16[3,256,256]{2,1,0:T(8,128)(2,1)}, u32[]{:S(2)}, u32[]{:S(2)}) collective-permute-start(bf16[3,256,256]{2,1,0:T(8,128)(2,1)} %get-tuple-element.174), channel_id=1, source_target_pairs={{0,16},{4,20},{8,24},{12,28},{16,0},{20,4},{24,8},{28,12},{1,17},{... | collective-permute-start | bytes 1179656 | tf_op jit(solution)/shard_map/ppermute | solution.py:323
  689.0 24.4 %collective-permute-start.32 = (bf16[2,3,256,256]{3,2,1,0:T(8,128)(2,1)S(1)}, bf16[2,3,256,256]{3,2,1,0:T(8,128)(2,1)S(1)}, u32[]{:S(2)}, u32[]{:S(2)}) collective-permute-start(bf16[2,3,256,256]{3,2,1,0:T(8,128)(2,1)S(1)} %pad_maximum_fusion.10), channel_id=1, source_target_pairs={{0,8},{4,12},{8,0},{12,4},{16,24},{20,28},{24,16},{28,20},{1,9},{5... | collective-permute-start | bytes 2359304 | tf_op jit(solution)/shard_map/ppermute | solution.py:323
  689.5 25.4 %collective-permute-start.34 = (bf16[2,3,256,256]{3,2,1,0:T(8,128)(2,1)S(1)}, bf16[2,3,256,256]{3,2,1,0:T(8,128)(2,1)S(1)}, u32[]{:S(2)}, u32[]{:S(2)}) collective-permute-start(bf16[2,3,256,256]{3,2,1,0:T(8,128)(2,1)S(1)} %pad_maximum_fusion.11), channel_id=1, source_target_pairs={{0,16},{4,20},{8,24},{12,28},{16,0},{20,4},{24,8},{28,12},{1,17},{... | collective-permute-start | bytes 2359304 | tf_op jit(solution)/shard_map/ppermute | solution.py:323
  691.5 25.1 %collective-permute-start.35 = (bf16[256,2048]{1,0:T(8,128)(2,1)S(1)}, bf16[256,2048]{1,0:T(8,128)(2,1)S(1)}, u32[]{:S(2)}, u32[]{:S(2)}) collective-permute-start(bf16[256,2048]{1,0:T(8,128)(2,1)S(1)} %add_convert_fusion.1), channel_id=1, source_target_pairs={{0,1},{1,3},{3,2},{2,0},{4,5},{5,7},{7,6},{6,4},{8,9},{9,11},{11,1... | collective-permute-start | bytes 3145736 | tf_op jit(solution)/shard_map/ppermute | solution.py:304
  718.0 28.7 %copy-start.26 = (f32[256,2048]{1,0:T(8,128)S(1)}, f32[256,2048]{1,0:T(8,128)}, u32[]{:S(2)}) copy-start(f32[256,2048]{1,0:T(8,128)} %get-tuple-element.135) | copy-start | bytes 6291460
  718.0 28.7 %copy-start.84 = (f32[256]{0:T(256)S(1)}, f32[256]{0:T(256)}, u32[]{:S(2)}) copy-start(f32[256]{0:T(256)} %copy-done.83) | copy-start | bytes 3076
  718.0 28.7 %copy-start.85 = (f32[256]{0:T(256)S(1)}, f32[256]{0:T(256)}, u32[]{:S(2)}) copy-start(f32[256]{0:T(256)} %get-tuple-element.185) | copy-start | bytes 3076
  718.0 23.6 %collective-permute-start.36 = (bf16[256,2048]{1,0:T(8,128)(2,1)}, bf16[256,2048]{1,0:T(8,128)(2,1)}, u32[]{:S(2)}, u32[]{:S(2)}) collective-permute-start(bf16[256,2048]{1,0:T(8,128)(2,1)} %add_convert_fusion), channel_id=1, source_target_pairs={{0,1},{1,3},{3,2},{2,0},{4,5},{5,7},{7,6},{6,4},{8,9},{9,11},{11,1... | collective-permute-start | bytes 3145736 | tf_op jit(solution)/shard_map/ppermute | solution.py:304
  720.0 1.3 collective-permute-start.37
  721.3 4.3 collective-permute-start.38
  725.7 4.3 collective-permute-start.39
  730.0 23.7 %collective-permute-start.43 = (bf16[2,2,3,256,256]{4,3,2,1,0:T(8,128)(2,1)}, bf16[2,2,3,256,256]{4,3,2,1,0:T(8,128)(2,1)S(1)}, u32[]{:S(2)}, u32[]{:S(2)}) collective-permute-start(bf16[2,2,3,256,256]{4,3,2,1,0:T(8,128)(2,1)} %pad_maximum_fusion.8), channel_id=1, source_target_pairs={{0,4},{4,0},{8,12},{12,8},{16,20},{20,16},{24,28},{28,24},{1,5},{5... | collective-permute-start | bytes 4718600 | tf_op jit(solution)/shard_map/ppermute | solution.py:323
  730.1 23.9 %collective-permute-start.42 = (bf16[2,2,3,256,256]{4,3,2,1,0:T(8,128)(2,1)}, bf16[2,2,3,256,256]{4,3,2,1,0:T(8,128)(2,1)S(1)}, u32[]{:S(2)}, u32[]{:S(2)}) collective-permute-start(bf16[2,2,3,256,256]{4,3,2,1,0:T(8,128)(2,1)} %pad_maximum_fusion.7), channel_id=1, source_target_pairs={{0,4},{4,0},{8,12},{12,8},{16,20},{20,16},{24,28},{28,24},{1,5},{5... | collective-permute-start | bytes 4718600 | tf_op jit(solution)/shard_map/ppermute | solution.py:323
  741.7 5.0 collective-permute-start.40
  746.7 5.2 collective-permute-start.41
  (94 other events, 686.1 us)
Sparse Core Ops, SparseCore 0:
  10.5 48.2 all-gather.7
  61.2 28.1 all-gather.9
  91.9 44.3 all-gather.13
  138.6 67.6 all-gather.11
  383.3 86.8 reduce-scatter.4
  474.0 59.0 reduce-scatter.2
  535.8 89.6 all-gather.15
  627.5 48.4 all-gather.19
  678.0 36.2 all-gather.17
